TPU v7x, 32 devices: a whole 2x2x4 slice. The times are simulated.
32 devices in a mesh: parts: 16 (over z, y, x), mp: 2 (over core).
Axes of the slice: x: 2, y: 2, z: 4, core: 2. Of those that a mesh axis runs over, the one named last changes fastest.
Arguments:
- features: bfloat16 [4, 6144, 2048], P('mp', 'parts'), may hold values from -6 to 6
- weight: bfloat16 [2048, 2048], P('mp'), may hold values from -0.25 to 0.25
- bias: bfloat16 [2048], P('mp'), may hold values from -3 to 3
- local_adj: int32 [4, 6144, 384], P('mp', 'parts'), may hold values from 0 to 1, as said below
- send_index: int32 [4, 16, 16, 4], P('mp', 'parts'), may hold values from -1 to 383, as said below
- recv_target: int32 [4, 16, 16, 4], P('mp', 'parts'), may hold values from -1 to 383, as said below
- cotangent: bfloat16 [4, 6144, 2048], P('mp', 'parts'), may hold values from -6 to 6
Outputs:
- activations: bfloat16 [4, 6144, 2048], P('mp', 'parts')
- input_grad: bfloat16 [4, 6144, 2048], P('mp', 'parts')
- weight_grad: float32 [2048, 2048], P(('parts', 'mp'))
- bias_grad: float32 [2048], P(('parts', 'mp'))
Inputs may be any that keep to these rules, and one draw needn't show every extreme that they name: `local_adj`: 0 or 1, zero on the diagonal of every part's block. `send_index`: -1 marks an unused slot; slot (p, q, h) is used exactly when slot (q, p, h) of recv_target is; used slots of a pair come first; no part sends to itself; some pairs use all 4 slots. `recv_target`: -1 marks an unused slot, used exactly as in send_index with the two part dimensions swapped.
All inputs are finite; a program needn't handle non-finite values.
Results may differ from a plain program's by a relative error of at most 0.006.
Values may be sent and summed in bfloat16 or wider, within the bound.
No kernel may reach another device: no remote copies, remote signals or barrier semaphores. Data moves between devices by JAX's collectives and lax.ppermute only.
A program may use at most 128 MiB of HBM per device.

v0:
```python
import jax
import jax.numpy as jnp
from jax import lax
from jax.sharding import PartitionSpec as P


def fetch_weights(weight, bias):
    return (
        lax.all_gather(weight, "mp", axis=0, tiled=True),
        lax.all_gather(bias, "mp", axis=0, tiled=True),
    )


def gelu_tanh(value):
    return jax.nn.gelu(value, approximate=True)


def local(features, weight, bias, local_adj, send_index, recv_target, cotangent):
    batches = features.shape[0]
    rows = features.shape[1]
    width = features.shape[2]
    positions = jnp.arange(rows, dtype=jnp.int32)
    weight_sum = jnp.zeros((width, width), jnp.float32)
    bias_sum = jnp.zeros((width,), jnp.float32)
    outputs = []
    input_grads = []
    for batch in range(batches):
        weight_full, bias_full = fetch_weights(weight, bias)
        node_feats = features[batch]
        neighbours = local_adj[batch]
        adjacency = neighbours.astype(jnp.bfloat16)
        sender = send_index[batch, 0].reshape(-1)
        targets = recv_target[batch, 0].reshape(-1)
        recv_match = targets[None, :] == positions[:, None]
        recv_hot = recv_match.astype(jnp.bfloat16)
        send_hot = (sender[None, :] == positions[:, None]).astype(jnp.bfloat16)
        degree = jnp.sum(neighbours, axis=1).astype(jnp.float32) + jnp.sum(
            recv_match.astype(jnp.float32), axis=1
        )
        ratio = 1.0 / (1.0 + degree)
        slot_shape = send_index.shape[2:]
        outgoing = jnp.take(node_feats, jnp.maximum(sender, 0), axis=0).reshape(
            slot_shape + (width,)
        )
        arrived = lax.all_to_all(outgoing, "parts", split_axis=0, concat_axis=0, tiled=True)
        total = jnp.dot(adjacency, node_feats, preferred_element_type=jnp.float32)
        total = total + jnp.dot(
            recv_hot, arrived.reshape(-1, width), preferred_element_type=jnp.float32
        )
        total = total + 2.0 * node_feats.astype(jnp.float32)
        mixed = (total * ratio[:, None]).astype(jnp.bfloat16)
        pre = jnp.dot(mixed, weight_full, preferred_element_type=jnp.float32) + bias_full.astype(
            jnp.float32
        )
        result, pull = jax.vjp(gelu_tanh, pre)
        outputs.append(result.astype(jnp.bfloat16))
        dpre = pull(cotangent[batch].astype(jnp.float32))[0].astype(jnp.bfloat16)
        weight_term = lax.dot_general(
            mixed, dpre, (((0,), (0,)), ((), ())), preferred_element_type=jnp.float32
        )
        bias_term = jnp.sum(dpre.astype(jnp.float32), axis=0)
        weight_part, bias_part = (
            lax.psum_scatter(weight_term, ("parts", "mp"), scatter_dimension=0, tiled=True),
            lax.psum_scatter(bias_term, ("parts", "mp"), scatter_dimension=0, tiled=True),
        )
        if batch == 0:
            weight_sum = weight_part
            bias_sum = bias_part
        else:
            weight_sum = weight_sum + weight_part
            bias_sum = bias_sum + bias_part
        dmixed = lax.dot_general(
            dpre, weight_full, (((1,), (1,)), ((), ())), preferred_element_type=jnp.float32
        )
        dtotal = (dmixed * ratio[:, None]).astype(jnp.bfloat16)
        dfeats = lax.dot_general(
            adjacency, dtotal, (((0,), (0,)), ((), ())), preferred_element_type=jnp.float32
        )
        dfeats = dfeats + 2.0 * dtotal.astype(jnp.float32)
        dsent = lax.dot_general(
            recv_hot, dtotal, (((0,), (0,)), ((), ())), preferred_element_type=jnp.float32
        )
        dsent = dsent.astype(jnp.bfloat16).reshape(slot_shape + (width,))
        returned = lax.all_to_all(dsent, "parts", split_axis=0, concat_axis=0, tiled=True)
        dfeats = dfeats + jnp.dot(
            send_hot, returned.reshape(-1, width), preferred_element_type=jnp.float32
        )
        input_grads.append(dfeats.astype(jnp.bfloat16))
    return (jnp.stack(outputs), jnp.stack(input_grads), weight_sum, bias_sum)


def solution(mesh):
    return jax.shard_map(
        local,
        mesh=mesh,
        in_specs=(
            P("mp", "parts", None),
            P("mp", None),
            P("mp"),
            P("mp", "parts", None),
            P("mp", "parts", None, None),
            P("mp", "parts", None, None),
            P("mp", "parts", None),
        ),
        out_specs=(
            P("mp", "parts", None),
            P("mp", "parts", None),
            P(("parts", "mp"), None),
            P(("parts", "mp")),
        ),
        check_vma=False,
    )
```

profile of v0, /device:TPU:1, one launch (start us, length us, event | category | flops | bytes accessed | tf_op | source)
XLA Modules:
  0.0 274.8 jit_solution(2068344041060453766)
XLA Ops:
  7.2 0.7 all-gather.2.cloned.1.call-update
  8.1 2.1 slice_bitcast_fusion.1
  10.2 0.7 gather_fusion
  11.0 0.1 broadcast_select_fusion.1
  11.1 0.8 reshape.66
  11.9 7.4 %all-to-all-start = ((bf16[16,4,2048]{2,1,0:T(4,128)(2,1)}), bf16[16,4,2048]{2,1,0:T(4,128)(2,1)S(1)}, u32[]{:S(2)}, u32[]{:S(2)}) async-start(bf16[16,4,2048]{2,1,0:T(4,128)(2,1)} %reshape.66), calls=%async_computation | async-start | bytes 524288 | tf_op jit(solution)/shard_map/all_to_all | solution.py:45
  19.6 0.1 eq.60
  19.9 0.7 gather_fusion.1
  20.7 0.1 broadcast_select_fusion
  20.8 0.8 reshape.68
  21.7 0.2 slice_reduce_fusion.1
  21.9 5.4 %all-to-all-done = bf16[16,4,2048]{2,1,0:T(4,128)(2,1)S(1)} async-done(((bf16[16,4,2048]{2,1,0:T(4,128)(2,1)}), bf16[16,4,2048]{2,1,0:T(4,128)(2,1)S(1)}, u32[]{:S(2)}, u32[]{:S(2)}) %all-to-all-start) | async-done | bytes 262176 | tf_op jit(solution)/shard_map/all_to_all | solution.py:45
  27.3 4.8 %all-to-all-start.1 = ((bf16[16,4,2048]{2,1,0:T(4,128)(2,1)}), bf16[16,4,2048]{2,1,0:T(4,128)(2,1)S(1)}, u32[]{:S(2)}, u32[]{:S(2)}) async-start(bf16[16,4,2048]{2,1,0:T(4,128)(2,1)} %reshape.68), calls=%async_computation.1 | async-start | bytes 524288 | tf_op jit(solution)/shard_map/all_to_all | solution.py:45
  32.2 0.1 convert_reduce_fusion.2
  32.3 3.1 %all_gather.9 = bf16[2048]{0:T(1024)(128)(2,1)S(1)} all-gather(bf16[1024]{0:T(1024)(128)(2,1)S(1)} %copy-done.14), channel_id=1, replica_groups=mesh['parts'=16,'mp'=2] {'mp'}, dimensions={0}, use_global_device_ids=true | all-gather | bytes 6144 | tf_op jit(solution)/shard_map/all_gather | solution.py:10
  35.5 4.2 %all-to-all-done.1 = bf16[16,4,2048]{2,1,0:T(4,128)(2,1)S(1)} async-done(((bf16[16,4,2048]{2,1,0:T(4,128)(2,1)}), bf16[16,4,2048]{2,1,0:T(4,128)(2,1)S(1)}, u32[]{:S(2)}, u32[]{:S(2)}) %all-to-all-start.1) | async-done | bytes 262176 | tf_op jit(solution)/shard_map/all_to_all | solution.py:45
  39.7 0.7 fusion.38
  40.4 0.7 fusion.39
  41.1 0.5 copy-done.4
  41.6 1.1 multiply_convert_fusion.3
  42.7 2.2 multiply_convert_fusion.5
  45.0 6.1 %convolution_add_fusion.1 = f32[384,2048]{1,0:T(8,128)S(1)} fusion(bf16[384,2048]{1,0:T(8,128)(2,1)S(1)} %multiply_convert_fusion.3, bf16[2048,2048]{1,0:T(8,128)(2,1)} %all-gather.2.cloned.1.call-done, f32[2048]{0:T(1024)S(1)} %convert_element_type.114), kind=kOutput, calls=%fused_computation.47 | convolution fusion | flops 3222011904 | bytes 13115392 | tf_op jit(solution)/shard_map/dot_general | solution.py:52
  51.1 0.1 copy-done.15
  51.3 0.9 copy-done.16
  52.2 10.0 %convert_reduce_fusion.1 = (f32[2048]{0:T(1024)S(1)}, bf16[384,2048]{1,0:T(8,128)(2,1)S(1)}, f32[2048]{0:T(1024)S(1)}, bf16[384,2048]{1,0:T(8,128)(2,1)}, bf16[1...) fusion(bf16[2,384,2048]{2,1,0:T(8,128)(2,1)S(1)} %copy-done.16, f32[384,2048]{1,0:T(8,128)S(1)} %convolution_add_fusion.1, ...), kind=kOutput, calls=%fused_computation.40 | convolution fusion | flops 3261329408 | bytes 22568960 | tf_op jit(solution)/shard_map/dot_general | solution.py:52
  62.2 4.6 %fusion.48 = f32[2048,2048]{1,0:T(8,128)S(1)} fusion(bf16[384,2048]{1,0:T(8,128)(2,1)S(1)} %copy-done.6, bf16[384,2048]{1,0:T(8,128)(2,1)S(1)} %get-tuple-element.10), kind=kOutput, calls=%fused_computation.91 | convolution fusion | flops 3221225472 | bytes 19922944 | tf_op jit(solution)/shard_map/dot_general | solution.py:58
  66.8 9.9 %convolution_add_fusion = f32[2048,2048]{1,0:T(8,128)} fusion(f32[2048,2048]{1,0:T(8,128)S(1)} %fusion.48, bf16[384,2048]{1,0:T(8,128)(2,1)S(1)} %copy-done.3, bf16[384,2048]{1,0:T(8,128)(2,1)} %get-tuple-element.12), kind=kOutput, calls=%fused_computation.2 | convolution fusion | flops 3225419776 | bytes 36700160 | tf_op jit(solution)/shard_map/dot_general | solution.py:58
  76.7 1.4 copy-done.7
  78.1 6.8 %multiply_convert_fusion = bf16[384,2048]{1,0:T(8,128)(2,1)S(1)} fusion(bf16[384,2048]{1,0:T(8,128)(2,1)S(1)} %copy-done.7, bf16[2048,2048]{1,0:T(8,128)(2,1)} %all-gather.2.cloned.1.call-done, f32[384]{0:T(512)S(1)} %add_divide_fusion), kind=kOutput, calls=%fused_computation.41 | convolution fusion | flops 3222798336 | bytes 11535872 | tf_op jit(solution)/shard_map/dot_general | solution.py:72
  84.9 0.4 convolution_convert_fusion
  85.3 0.8 reshape.72
  86.2 5.2 %all-to-all-start.3 = ((bf16[16,4,2048]{2,1,0:T(4,128)(2,1)}), bf16[16,4,2048]{2,1,0:T(4,128)(2,1)S(1)}, u32[]{:S(2)}, u32[]{:S(2)}) async-start(bf16[16,4,2048]{2,1,0:T(4,128)(2,1)} %reshape.72), calls=%async_computation.3 | async-start | bytes 524288 | tf_op jit(solution)/shard_map/all_to_all | solution.py:84
  91.3 7.4 %multiply_convert_fusion.1 = bf16[384,2048]{1,0:T(8,128)(2,1)S(1)} fusion(bf16[384,2048]{1,0:T(8,128)(2,1)} %copy-done.10, bf16[2048,2048]{1,0:T(8,128)(2,1)} %all-gather.2.cloned.1.call-done, f32[384]{0:T(512)S(1)} %add_divide_fusion.1), kind=kOutput, calls=%fused_computation.42 | convolution fusion | flops 3222798336 | bytes 11535872 | tf_op jit(solution)/shard_map/dot_general | solution.py:72
  98.7 1.1 convolution_convert_fusion.1
  99.9 1.8 reshape.70
  101.6 7.5 %all-to-all-start.2 = ((bf16[16,4,2048]{2,1,0:T(4,128)(2,1)}), bf16[16,4,2048]{2,1,0:T(4,128)(2,1)}, u32[]{:S(2)}, u32[]{:S(2)}) async-start(bf16[16,4,2048]{2,1,0:T(4,128)(2,1)} %reshape.70), calls=%async_computation.2 | async-start | bytes 524288 | tf_op jit(solution)/shard_map/all_to_all | solution.py:84
  109.2 45.9 %all-reduce = f32[2048]{0:T(1024)S(1)} all-reduce(f32[2048]{0:T(1024)S(1)} %add.124), channel_id=5, replica_groups=mesh['parts'=16,'mp'=2] {'parts','mp'}, use_global_device_ids=true, to_apply=%region_7.9.clone | all-reduce | flops 2048 | bytes 16384
  155.1 0.6 dynamic-slice
  155.7 1.0 reshape.73
  156.7 1.7 reshape.71
  158.5 1.6 fusion.30
  160.1 0.5 fusion.31
  160.6 1.2 fusion.24
  161.9 1.2 fusion.25
  163.1 0.2 copy-done.8
  163.3 0.5 copy-done.9
  163.8 3.0 %pad_maximum_fusion = (bf16[2,384,2048]{2,1,0:T(8,128)(2,1)}, bf16[2,384,2048]{2,1,0:T(8,128)(2,1)}) fusion(bf16[1,384,2048]{2,1,0:T(8,128)(2,1)S(1)} %copy-done.8, bf16[1,384,2048]{2,1,0:T(8,128)(2,1)S(1)} %copy-done.9, bf16[1,384,2048]{2,1,0:T(8,128)(2,1)S(1)} %fusion.25, bf16[1,384,2048]{2,1,0:T(8,128)(2,1)S(1)} %fusion.24), kind=kLoop, calls=%fused_computation.31 | loop fusion | flops 3145728 | bytes 12582912 | tf_op jit(solution)/shard_map/stack | solution.py:89
  166.8 101.2 %reduce-scatter.2.cloned.1.call-done = f32[64,2048]{1,0:T(8,128)} async-done(((f32[2048,2048]{1,0:T(8,128)}), f32[64,2048]{1,0:T(8,128)}) %reduce-scatter.2.cloned.1.call-update) | async-done | bytes 524304 | tf_op jit(solution)/shard_map/reduce_scatter | solution.py:63
  (56 shorter events, 1.0 us)
Async XLA Ops:
  7.2 0.7 copy-start.12
  7.2 37.8 %all-gather.2.cloned.1.call-start = ((), (), s32[]{:S(2)}) async-start(), calls=%async_computation.5 | async-start | bytes 12582912 | tf_op jit(solution)/shard_map/all_gather | solution.py:9
  10.2 9.1 %copy-start.13 = (s32[2,1,16,4]{2,3,1,0:T(4,128)S(1)}, s32[2,1,16,4]{2,3,1,0:T(4,128)}, u32[]{:S(2)}) copy-start(s32[2,1,16,4]{2,3,1,0:T(4,128)} %param.14) | copy-start | bytes 1540
  11.0 10.7 %copy-start = (s32[2,384,384]{2,1,0:T(8,128)S(1)}, s32[2,384,384]{2,1,0:T(8,128)}, u32[]{:S(2)}) copy-start(s32[2,384,384]{2,1,0:T(8,128)} %param.12) | copy-start | bytes 3538948
  11.1 21.2 %copy-start.14 = (bf16[1024]{0:T(1024)(128)(2,1)S(1)}, bf16[1024]{0:T(1024)(128)(2,1)}, u32[]{:S(2)}) copy-start(bf16[1024]{0:T(1024)(128)(2,1)} %param.11) | copy-start | bytes 6148
  11.9 15.4 %all-to-all-start = ((bf16[16,4,2048]{2,1,0:T(4,128)(2,1)}), bf16[16,4,2048]{2,1,0:T(4,128)(2,1)S(1)}, u32[]{:S(2)}, u32[]{:S(2)}) async-start(bf16[16,4,2048]{2,1,0:T(4,128)(2,1)} %reshape.66), calls=%async_computation | async-start | bytes 524288 | tf_op jit(solution)/shard_map/all_to_all | solution.py:45
  27.3 12.3 %all-to-all-start.1 = ((bf16[16,4,2048]{2,1,0:T(4,128)(2,1)}), bf16[16,4,2048]{2,1,0:T(4,128)(2,1)S(1)}, u32[]{:S(2)}, u32[]{:S(2)}) async-start(bf16[16,4,2048]{2,1,0:T(4,128)(2,1)} %reshape.68), calls=%async_computation.1 | async-start | bytes 524288 | tf_op jit(solution)/shard_map/all_to_all | solution.py:45
  32.1 235.8 %reduce-scatter.2.cloned.1.call-start = ((), (), s32[]{:S(2)}) async-start(), calls=%async_computation.6 | async-start | bytes 17301504 | tf_op jit(solution)/shard_map/reduce_scatter | solution.py:63
  39.7 1.9 copy-start.4
  42.7 2.3 copy-start.2
  44.9 6.2 %copy-start.5 = (bf16[384,2048]{1,0:T(8,128)(2,1)S(1)}, bf16[384,2048]{1,0:T(8,128)(2,1)}, u32[]{:S(2)}) copy-start(bf16[384,2048]{1,0:T(8,128)(2,1)} %multiply_convert_fusion.5) | copy-start | bytes 4718596
  44.9 6.3 %copy-start.15 = (bf16[2048,2048]{1,0:T(8,128)(2,1)S(1)}, bf16[2048,2048]{1,0:T(8,128)(2,1)}, u32[]{:S(2)}) copy-start(bf16[2048,2048]{1,0:T(8,128)(2,1)} %all-gather.2.cloned.1.call-done) | copy-start | bytes 25165828
  44.9 7.2 %copy-start.16 = (bf16[2,384,2048]{2,1,0:T(8,128)(2,1)S(1)}, bf16[2,384,2048]{2,1,0:T(8,128)(2,1)}, u32[]{:S(2)}) copy-start(bf16[2,384,2048]{2,1,0:T(8,128)(2,1)} %param.15) | copy-start | bytes 9437188
  52.2 10.0 %copy-start.6 = (bf16[384,2048]{1,0:T(8,128)(2,1)S(1)}, bf16[384,2048]{1,0:T(8,128)(2,1)}, u32[]{:S(2)}) copy-start(bf16[384,2048]{1,0:T(8,128)(2,1)} %multiply_convert_fusion.5) | copy-start | bytes 4718596
  62.2 4.6 %copy-start.10 = (bf16[384,2048]{1,0:T(8,128)(2,1)}, bf16[384,2048]{1,0:T(8,128)(2,1)S(1)}, u32[]{:S(2)}) copy-start(bf16[384,2048]{1,0:T(8,128)(2,1)S(1)} %get-tuple-element.10) | copy-start | bytes 4718596
  62.2 4.6 %copy-start.3 = (bf16[384,2048]{1,0:T(8,128)(2,1)S(1)}, bf16[384,2048]{1,0:T(8,128)(2,1)}, u32[]{:S(2)}) copy-start(bf16[384,2048]{1,0:T(8,128)(2,1)} %copy-done.2) | copy-start | bytes 4718596
  76.7 1.4 copy-start.7
  86.2 15.5 %all-to-all-start.3 = ((bf16[16,4,2048]{2,1,0:T(4,128)(2,1)}), bf16[16,4,2048]{2,1,0:T(4,128)(2,1)S(1)}, u32[]{:S(2)}, u32[]{:S(2)}) async-start(bf16[16,4,2048]{2,1,0:T(4,128)(2,1)} %reshape.72), calls=%async_computation.3 | async-start | bytes 524288 | tf_op jit(solution)/shard_map/all_to_all | solution.py:84
  101.6 53.5 %copy-start.11 = (bf16[16,4,2048]{2,1,0:T(4,128)(2,1)}, bf16[16,4,2048]{2,1,0:T(4,128)(2,1)S(1)}, u32[]{:S(2)}) copy-start(bf16[16,4,2048]{2,1,0:T(4,128)(2,1)S(1)} %all-to-all-done.3) | copy-start | bytes 786436
  101.6 55.1 %all-to-all-start.2 = ((bf16[16,4,2048]{2,1,0:T(4,128)(2,1)}), bf16[16,4,2048]{2,1,0:T(4,128)(2,1)}, u32[]{:S(2)}, u32[]{:S(2)}) async-start(bf16[16,4,2048]{2,1,0:T(4,128)(2,1)} %reshape.70), calls=%async_computation.2 | async-start | bytes 524288 | tf_op jit(solution)/shard_map/all_to_all | solution.py:84
  158.5 2.2 copy-start.1
  161.9 1.4 copy-start.8
  161.9 1.9 copy-start.9
Sparse Core Ops, SparseCore 0:
  9.5 22.3 all-gather.1
  76.8 191.0 reduce-scatter.1
where the time goes:
time: 277 us; the launch traced here: 275 us
  waiting for transfers between devices  111 us (40%)
  matrix products  55.7 us (20%)
  blocking collectives  49 us (18%)
  starting transfers between devices  25 us (9%)
  local copies, waits for them, and re-layouts  15.6 us (6%)
  between operations  14.4 us (5%)
  other arithmetic  3.57 us (1%)
    reduce_scatter x1, waiting for transfers between devices, local(): lax.psum_scatter(weight_term, ('parts', 'mp'), scatter_dimension=0, tiled...  101 us
    unnamed x1, blocking collectives  45.9 us
    dot_general x2, matrix products, local(): jnp.dot(mixed, weight_full, preferred_element_type=jnp.float32)  16.1 us
    dot_general x2, matrix products, local(): lax.dot_general(mixed, dpre, (((0,), (0,)), ((), ())), preferred_element_...  14.5 us
    dot_general x2, matrix products, local(): lax.dot_general(dpre, weight_full, (((1,), (1,)), ((), ())), preferred_el...  14.2 us
    all_to_all x2, starting transfers between devices, local(): lax.all_to_all(dsent, 'parts', split_axis=0, concat_axis=0, tiled=True)  12.7 us
    all_to_all x2, starting transfers between devices, local(): lax.all_to_all(outgoing, 'parts', split_axis=0, concat_axis=0, tiled=True)  12.2 us
    all_to_all x2, waiting for transfers between devices, local(): lax.all_to_all(outgoing, 'parts', split_axis=0, concat_axis=0, tiled=True)  9.61 us
  transfers between devices with their start and end apart: 6, of which 3 were waited for; matrix products, arithmetic and copies ran while one was open for 15% of the time, Pallas kernels for 0%

commit v1 on v0

v1 whole, which is shorter than its diff:
```python
import functools
import math

import jax
import jax.numpy as jnp
from jax import lax
from jax.experimental import pallas as pl
from jax.experimental.pallas import tpu as pltpu
from jax.sharding import PartitionSpec as P

F32 = jnp.float32
BF16 = jnp.bfloat16
AXES = ("parts", "mp")
SWAP = ((0, 1), (1, 0))
GELU_C = math.sqrt(2.0 / math.pi)
GELU_A = 0.044715
CHUNKS = (512, 768, 768)
COSTS = {}
VMEM = pl.BlockSpec(memory_space=pltpu.VMEM)
SMEM = pl.BlockSpec(memory_space=pltpu.SMEM)
ANY = pl.BlockSpec(memory_space=pl.ANY)
HBM = pl.BlockSpec(memory_space=pltpu.HBM)
NT = (((1,), (1,)), ((), ()))


def sds(shape, dtype):
    return jax.ShapeDtypeStruct(shape, dtype)


class Order:
    def __init__(self, limit):
        self.token = None
        self.limit = limit

    def run(self, kernel, name, out_shape, args, scalars=(), far=(), scratch=(), keep=False, limit=None):
        specs = [SMEM] * len(scalars) + [HBM] * len(far) + [VMEM] * len(args)
        args = [*scalars, *far, *args]
        used = len(args)
        aliases = {}
        if keep is not None and keep is not False:
            aliases = {len(args): 0}
            args.append(keep)
            specs.append(ANY)
        if self.token is not None:
            args.append(self.token)
            specs.append(VMEM)
        count, results = len(args), len(out_shape)

        def body(*refs):
            refs[count + results][...] = jnp.zeros((8, 128), F32)
            kernel(*refs[:used], *refs[count : count + results], *refs[count + results + 1 :])

        *out, self.token = pl.pallas_call(
            body,
            name=name,
            in_specs=specs,
            out_specs=((VMEM if keep is False else ANY,) + (VMEM,) * results),
            out_shape=(*out_shape, sds((8, 128), F32)),
            scratch_shapes=scratch,
            input_output_aliases=aliases,
            compiler_params=pltpu.CompilerParams(vmem_limit_bytes=(limit or self.limit) * 2**20),
            cost_estimate=pl.CostEstimate(flops=COSTS.get(name, 1), bytes_accessed=1, transcendentals=0),
        )(*args)
        return out


def hot_rows(index_row, rows):
    match = lax.broadcasted_iota(jnp.int32, (rows, index_row.shape[1]), 0) == index_row
    return jnp.where(match, 1.0, 0.0)


def tiles(width, size=512):
    return [slice(i, min(i + size, width)) for i in range(0, width, size)]


def index_column(index, part, nodes, order=None, turned=0):
    batches, _, depth, parts = index.shape
    slots = batches * parts * depth
    slot = lax.broadcasted_iota(jnp.int32, (slots, parts), 0)
    spot, rest = lax.div(slot, batches * depth), lax.rem(slot, batches * depth)
    if order is not None:
        apart = jnp.zeros((slots, parts), jnp.int32)
        for i, distance in enumerate(order):
            apart = jnp.where(spot == i, distance, apart)
        spot = turn_digits(apart, turned) ^ part
    here = lax.broadcasted_iota(jnp.int32, (slots, parts), 1) == spot
    total = jnp.zeros((slots, parts), jnp.int32)
    for batch in range(batches):
        node = index[batch, 0]
        node = jnp.where(node < 0, -1, node + batch * nodes)
        for h in range(depth):
            total = jnp.where(rest == batch * depth + h, node[h : h + 1], total)
    return jnp.sum(jnp.where(here, total, 0), axis=1, keepdims=True)


def turn_digits(value, turned):
    differ = (value ^ lax.shift_right_logical(value, 1)) & turned
    return value ^ differ ^ (differ << 1)


def as_row(column):
    return jnp.broadcast_to(column, (column.shape[0], 128)).T[:1]


def hot_cols(index_col, cols):
    match = lax.broadcasted_iota(jnp.int32, (index_col.shape[0], cols), 1) == index_col
    return jnp.where(match, 1.0, 0.0)


def outgoing_kernel(nodes, orders, place, feats, adj, send, recv, here, edges, send_row, recv_row, back_row, *rest):
    outs, sems = rest[:-1], rest[-1]
    width = feats.shape[1]
    ranges = tiles(width, width // (sems.shape[0] - 1))
    copies = [pltpu.make_async_copy(feats.at[:, at], here.at[:, at], sems.at[i]) for i, at in enumerate(ranges)]
    copies.append(pltpu.make_async_copy(adj, edges, sems.at[len(ranges)]))
    for copy in copies:
        copy.start()
    me, part = place[0], place[1]
    column = index_column(send, part, nodes, orders[0])
    recv_row[...] = as_row(index_column(recv, part, nodes, orders[1]))
    back_row[...] = as_row(index_column(recv, part, nodes, orders[2], me))
    send_row[...] = as_row(index_column(send, part, nodes, orders[3], me))
    hot = hot_cols(column, feats.shape[0]).astype(BF16)
    size = outs[0].shape[0]
    for at, copy in zip(ranges, copies):
        copy.wait()
        value = jnp.dot(hot, here[:, at], preferred_element_type=F32)
        for i, out in enumerate(outs):
            out[:, at] = value[i * size : (i + 1) * size].astype(BF16)
    copies[-1].wait()


def regroup_kernel(size, orders, *refs):
    pieces, outs = refs[: -len(orders)], refs[-len(orders) :]
    values = [piece[...].astype(F32) for piece in pieces]
    for order, out in zip(orders, outs):
        blocks = [values[i][block * size : (block + 1) * size] for i, block in order]
        out[...] = jnp.concatenate(blocks, axis=0).astype(BF16)


def stack(pieces):
    return jnp.concatenate([piece[...] for piece in pieces], axis=0)


def mix_kernel(weight, adj, recv_row, feats, mixed, mixed_t, ratio, ratio_row, adj_t, own, sem):
    copy = pltpu.make_async_copy(weight, own, sem)
    copy.start()
    batches, nodes, _ = adj.shape
    half = mixed.shape[2]
    eye = lax.broadcasted_iota(jnp.int32, (nodes, nodes), 0) == lax.broadcasted_iota(
        jnp.int32, (nodes, nodes), 1
    )
    for batch in range(batches):
        here = slice(batch * nodes, (batch + 1) * nodes)
        count = adj[batch].astype(F32)
        hot = hot_rows(recv_row[...] - batch * nodes, nodes)
        degree = jnp.sum(count, axis=1, keepdims=True) + jnp.sum(hot, axis=1, keepdims=True)
        scale = 1.0 / (1.0 + degree)
        ratio[here] = scale
        ratio_row[:, here] = jnp.broadcast_to(scale, (nodes, 128)).T[:8]
        count = count + jnp.where(eye, 2.0, 0.0)
        adj_t[batch] = count.T.astype(BF16)
        count = count.astype(BF16)
        for at in tiles(feats.shape[1]):
            value = scale * jnp.dot(count, feats[here, at], preferred_element_type=F32)
            low = at.start % half
            mixed[at.start // half, here, low : low + at.stop - at.start] = value.astype(BF16)
            mixed_t[at, here] = value.T.astype(BF16)
    copy.wait()


def pre_own_kernel(place, away, mixed, weight, pre, other, sem):
    copy = pltpu.make_async_copy(away, other, sem)
    copy.start()
    me = place[0]
    for at in tiles(pre.shape[1]):
        pre[:, at] = jnp.dot(mixed[me], weight[:, at], preferred_element_type=F32)
    copy.wait()


def pre_other_kernel(place, before, mixed, weight, bias_own, bias_other, pre):
    me = place[0]
    half = weight.shape[0]
    first = me == 0
    mine, theirs = bias_own[...].astype(F32), bias_other[...].astype(F32)
    bias = (jnp.where(first, mine, theirs), jnp.where(first, theirs, mine))
    for at in tiles(pre.shape[1]):
        total = before[:, at] + jnp.dot(mixed[1 - me], weight[:, at], preferred_element_type=F32)
        low = at.start % half
        pre[:, at] = total + bias[at.start // half][:, low : low + at.stop - at.start]


def finish_kernel(axes, block, place, recv_row, ratio_row, mixed_t, *refs):
    pieces, (mine, theirs) = refs[:-2], refs[-2:]
    me, part = place[0], place[1]
    first = me == 0
    rows = mixed_t.shape[1]
    hot = hot_rows(recv_row[...], rows).T.astype(BF16)
    scale = ratio_row[0:1]
    for at in tiles(mixed_t.shape[0], 256):
        remote = jnp.dot(stack([piece.at[:, at] for piece in pieces]).T, hot, preferred_element_type=F32)
        value = (mixed_t[at].astype(F32) + scale * remote).reshape(128 // block, 2, block, rows)
        for out, swap in ((mine, False), (theirs, True)):
            low, high = (1, 0) if swap else (0, 1)
            chosen = jnp.where(first, value[:, low], value[:, high])
            if axes is None:
                out[at.start // 2 : at.stop // 2] = chosen.reshape(128, rows).astype(BF16)
                continue
            owner = 1 - me if swap else me
            for i in range(128 // block):
                spot = spot_of(axes, part, owner, at.start // (2 * block) + i)
                out[pl.ds(pl.multiple_of(spot * block, block), block)] = chosen[i].astype(BF16)


def remote_kernel(place, own, other, *refs):
    pieces, out = refs[:-1], refs[-1]
    half = own.shape[0]
    me = place[0]
    spots = out.shape[0] // 2
    here = stack([piece.at[:, pl.ds(pl.multiple_of(me * half, half), half)] for piece in pieces])
    there = stack([piece.at[:, pl.ds(pl.multiple_of((1 - me) * half, half), half)] for piece in pieces])
    for at in tiles(own.shape[1]):
        product = jnp.dot(here, own[:, at], preferred_element_type=F32)
        product += jnp.dot(there, other[:, at], preferred_element_type=F32)
        high = product.astype(BF16)
        out[:spots, at] = high
        out[spots:, at] = (product - high.astype(F32)).astype(BF16)


def gelu_kernel(start, recv_row, ratio, remote, pre, cot, act, dpre, bias_term, value, result, sems):
    rows, size = dpre.shape
    at = slice(start, start + size)
    hot = hot_rows(recv_row[...], rows).astype(BF16)
    value[...] = pre[:, at] + ratio[...] * jnp.dot(
        jnp.concatenate([hot, hot], axis=1), remote[:, at], preferred_element_type=F32
    )
    step = 64

    def body(i, total):
        here = pl.ds(pl.multiple_of(i * step, step), step)
        v = value[here]
        square = v * v
        left = 0.5 + 0.5 * jnp.tanh(v * (GELU_C + GELU_C * GELU_A * square))
        out = v * left
        result[here] = out.astype(BF16)
        slope = left + (out - out * left) * (2.0 * GELU_C + 6.0 * GELU_C * GELU_A * square)
        grad = (cot[here, at].astype(F32) * slope).astype(BF16)
        dpre[here] = grad
        return total + grad.astype(F32).reshape(step // 8, 8, size).sum(axis=0)

    total = jnp.zeros((8, size), F32)
    pieces = sems.shape[0]
    steps = rows // step
    copies = []
    for piece in range(pieces):
        low, high = piece * steps // pieces, (piece + 1) * steps // pieces
        total = lax.fori_loop(low, high, body, total)
        here = slice(low * step, high * step)
        copies.append(pltpu.make_async_copy(result.at[here], act.at[here, at], sems.at[piece]))
        copies[-1].start()
    bias_term[...] = jnp.sum(total, axis=0, keepdims=True)
    for copy in copies:
        copy.wait()


def spot_of(axes, part, owner, index):
    apart = turn_digits(part ^ index, owner)
    spot = 0
    for axis in axes:
        spot = spot * 2 + (lax.shift_right_logical(apart, axis) & 1)
    return spot


def grad_kernel(order, block, mine, theirs, dpre_mine, dpre_theirs, keep, leave):
    half = keep.shape[0]
    count = min(256 // block, len(order) // 2)
    for i in range(0, len(order), count):
        spots = [slice(spot * block, (spot + 1) * block) for spot in order[i : i + count]]
        total = jnp.dot(stack([mine.at[at] for at in spots]), dpre_mine[...], preferred_element_type=F32)
        total += jnp.dot(stack([theirs.at[at] for at in spots]), dpre_theirs[...], preferred_element_type=F32)
        low = i * block % half
        out = keep if i * block < half else leave
        out[low : low + count * block] = total.astype(BF16)


def sent_kernel(chunks, parts, per_part, sources, place, recv_row, ratio_row, own, other, *refs):
    dpres, bias_terms, outs = refs[:chunks], refs[chunks : 2 * chunks], refs[2 * chunks : -1]
    lines = refs[-1]
    half, width = own.shape
    rows = ratio_row.shape[1]
    hot = (hot_rows(recv_row[...], rows).T * ratio_row[0:1]).astype(BF16)
    grad = jnp.concatenate(
        [jnp.dot(hot, dpre[...], preferred_element_type=F32).astype(BF16) for dpre in dpres], axis=1
    )
    me, part = place[0], place[1]
    size = outs[0].shape[0]
    for weight, spot in ((own, me), (other, 1 - me)):
        for at in tiles(half, 256):
            value = lax.dot_general(grad, weight[at], NT, preferred_element_type=F32)
            for i, out in enumerate(outs):
                here = pl.ds(pl.multiple_of(spot * half + at.start, 256), 256)
                out[:, here] = value[i * size : (i + 1) * size].astype(BF16)
    bias = jnp.concatenate([term[...] for term in bias_terms], axis=1)
    high = bias.astype(BF16).astype(F32)
    middle = (bias - high).astype(BF16).astype(F32)
    line = lax.broadcasted_iota(jnp.int32, (8, width), 0)
    lines[...] = jnp.where(line == 0, high, jnp.where(line == 1, middle, bias - high - middle))
    count = width // parts
    line = lax.broadcasted_iota(jnp.int32, (8, count), 0)
    for i, out in enumerate(outs):
        pieces = []
        for source in sources[i]:
            if len(outs) > 1:
                to = part ^ turn_digits(source, me)
                piece = lines[:, pl.ds(pl.multiple_of(to * count, count), count)]
            else:
                piece = lines[:, source * count : (source + 1) * count]
            piece = jnp.where(line < 3, piece, 0.0)
            if count < 128:
                piece = jnp.concatenate([piece, jnp.zeros((8, 128 - count), F32)], axis=1)
            if per_part > 8:
                piece = jnp.concatenate([piece, jnp.zeros((per_part - 8, piece.shape[1]), F32)], axis=0)
            pieces.append(piece)
        out[:, width:] = jnp.concatenate(pieces, axis=0).astype(BF16)


def back_kernel(chunks, ratio, weight, *refs):
    dpres, out = refs[:chunks], refs[chunks]
    for at in tiles(weight.shape[0], 256):
        total = None
        start = 0
        for dpre in dpres:
            size = dpre.shape[1]
            term = lax.dot_general(dpre[...], weight[at, start : start + size], NT, preferred_element_type=F32)
            total = term if total is None else total + term
            start += size
        out[:, at] = (ratio[...] * total).astype(BF16)


def local_kernel(adj_t, dtotal, out):
    batches, nodes, _ = adj_t.shape
    for batch in range(batches):
        here = slice(batch * nodes, (batch + 1) * nodes)
        for at in tiles(dtotal.shape[1]):
            out[here, at] = jnp.dot(adj_t[batch], dtotal[here, at], preferred_element_type=F32)


def input_kernel(place, send_row, own, other, *refs):
    pieces, (out, bias_out) = refs[:-2], refs[-2:]
    rows, half = own.shape
    hot = hot_rows(send_row[...], rows).astype(BF16)
    me = place[0]
    for partial, spot in ((own, me), (other, 1 - me)):
        for at in tiles(half):
            here = pl.ds(pl.multiple_of(spot * half + at.start, 512), at.stop - at.start)
            total = partial[:, at] + jnp.dot(hot, stack([piece.at[:, here] for piece in pieces]), preferred_element_type=F32)
            out[:, here] = total.astype(BF16)
    bias_out[...] = sum(jnp.sum(piece[:, 2 * half :].astype(F32), axis=0, keepdims=True) for piece in pieces)


def halve_kernel(keep, arrived, stay, leave):
    half = stay.shape[0]
    for out, low in ((leave, half), (stay, 0)):
        at = slice(low, low + half)
        out[...] = (keep[at].astype(F32) + arrived[at].astype(F32)).astype(BF16)


def last_kernel(*refs):
    out = refs[-1]
    start = 0
    for keep, arrived in zip(refs[:-1:2], refs[1:-1:2]):
        size = keep.shape[1]
        out[:, start : start + size] = keep[...].astype(F32) + arrived[...].astype(F32)
        start += size


def partners(parts, axis):
    turned = {0: 1, 1: 0}.get(axis, axis) if parts > 2 else axis
    return [(p * 2 + c, (p ^ (1 << (axis, turned)[c])) * 2 + c) for p in range(parts) for c in range(2)]


class Reduction:
    def __init__(self, order, parts, axes, keep, leave):
        self.order = order
        self.parts = parts
        self.axes = list(axes)
        self.keep = keep
        self.send(leave)

    def send(self, leave):
        self.arrived = lax.ppermute(leave, AXES, partners(self.parts, self.axes.pop(0)))

    def step(self):
        rows, size = self.keep.shape
        half = sds((rows // 2, size), BF16)
        self.keep, leave = self.order.run(halve_kernel, "halve", (half, half), (self.keep, self.arrived))
        self.send(leave)


class Exchange:
    def __init__(self, order, parts, axes, size, pieces):
        self.order, self.parts, self.axes, self.size = order, parts, list(axes), size
        self.lists = halves(range(parts), self.axes[0])
        self.stay, leave = pieces
        self.arrived = lax.ppermute(leave, AXES, partners(parts, self.axes.pop(0)))

    def step(self):
        if not self.axes:
            return
        found = {r: (i, spot) for i in range(2) for spot, r in enumerate(self.lists[i])}
        axis = self.axes.pop(0)
        self.lists = halves(self.lists[0] + self.lists[1], axis)
        orders = [[found[r] for r in part] for part in self.lists]
        shape = sds(self.stay.shape, BF16)
        self.stay, leave = self.order.run(
            functools.partial(regroup_kernel, self.size, orders), "regroup", (shape, shape), (self.stay, self.arrived)
        )
        self.arrived = lax.ppermute(leave, AXES, partners(self.parts, axis))


def halves(distances, axis):
    return [[r for r in distances if (r >> axis) & 1 == side] for side in range(2)]


def local(parts, features, weight, bias, local_adj, send_index, recv_target, cotangent):
    batches, nodes, width = features.shape
    rows = batches * nodes
    half = width // 2
    core = lax.axis_index("mp").astype(jnp.int32)
    part = lax.axis_index("parts").astype(jnp.int32)
    place = jnp.stack([core, part])
    paired = parts & (parts - 1) == 0 and width % (2 * parts) == 0 and (width // (2 * parts)) % 16 == 0
    block = width // (2 * parts)

    feats = features.reshape(rows, width)
    cot = cotangent.reshape(rows, width)
    digits = parts.bit_length() - 1
    near = min(4, parts)
    far = parts // near
    orders = [None] * 4
    early = late = None
    if paired:
        late = list(range(digits))
        early = late[2:] + late[:2]
        back = late[:1:-1] + late[:2]
        first, last = halves(range(parts), back[0]), list(range(parts))
        for axis in back:
            last = sum(halves(last, axis), [])
        orders = [list(range(parts)), [k * near + j for j in range(near) for k in range(far)], sum(first, []), last]
    slots = send_index.size
    per_part = slots // parts

    def move(pieces, stride):
        moved = [pieces[0]]
        for i in range(1, len(pieces)):
            perm = [(p, p ^ (i * stride)) for p in range(parts)]
            moved.append(lax.ppermute(pieces[i], "parts", perm))
        return moved

    def exchange(values):
        moved = lax.all_to_all(
            values.reshape(parts, per_part, values.shape[1]), "parts", split_axis=0, concat_axis=0, tiled=True
        )
        return moved.reshape(values.shape)

    other = lax.ppermute(weight, "mp", SWAP)
    bias_own = bias.reshape(1, half)
    bias_other = lax.ppermute(bias_own, "mp", SWAP)
    order = Order(12 if paired else 48)
    run = order.run
    turn = (0, 1, 3, 2)
    pieces = far if paired else 1
    row = sds((1, slots), jnp.int32)
    feats, local_adj, send_row, recv_row, back_row, *outgoing = run(
        functools.partial(outgoing_kernel, nodes, orders),
        "outgoing",
        (sds((rows, width), BF16), sds(local_adj.shape, jnp.int32), row, row, row)
        + (sds((slots // pieces, width), BF16),) * pieces,
        (jnp.transpose(send_index, turn), jnp.transpose(recv_target, turn)),
        scalars=(place,),
        far=(feats, local_adj),
        scratch=[pltpu.SemaphoreType.DMA((5,))],
        limit=47,
    )
    if paired:
        outgoing = move(outgoing, near)

    mixed, mixed_t, ratio, ratio_row, adj_t, weight = run(
        mix_kernel,
        "mix",
        (
            sds((2, rows, half), BF16),
            sds((width, rows), BF16),
            sds((rows, 1), F32),
            sds((8, rows), F32),
            sds((batches, nodes, nodes), BF16),
            sds(weight.shape, BF16),
        ),
        (local_adj, recv_row, feats),
        far=(weight,),
        scratch=[pltpu.SemaphoreType.DMA(())],
        limit=36,
    )
    if paired:
        arrived = run(
            functools.partial(
                regroup_kernel, per_part, [[(k, j) for k in range(far)] for j in range(near)]
            ),
            "regroup",
            (sds((far * per_part, width), BF16),) * near,
            outgoing,
        )
        arrived = move(arrived, 1)
    else:
        arrived = [exchange(outgoing[0])]
    pre, other = run(
        pre_own_kernel,
        "pre_own",
        (sds((rows, width), F32), sds(other.shape, BF16)),
        (mixed, weight),
        scalars=(place,),
        far=(other,),
        scratch=[pltpu.SemaphoreType.DMA(())],
    )
    (pre,) = run(
        pre_other_kernel,
        "pre_other",
        (sds((rows, width), F32),),
        (pre, mixed, other, bias_own, bias_other),
        scalars=(place,),
    )
    (remote,) = run(
        remote_kernel,
        "remote_product",
        (sds((2 * slots, width), BF16),),
        (weight, other, *arrived),
        scalars=(place,),
    )

    starts = [sum(CHUNKS[:i]) for i in range(len(CHUNKS))]
    act = None
    dpres, dpres_other, bias_terms, sums = [], [], [], []

    def gelu(i):
        nonlocal act
        size = CHUNKS[i]
        act, dpre, bias_term = run(
            functools.partial(gelu_kernel, starts[i]),
            "gelu",
            (sds((rows, width), BF16), sds((rows, size), BF16), sds((1, size), F32)),
            (recv_row, ratio, remote, pre, cot),
            scratch=[pltpu.VMEM((rows, size), F32), pltpu.VMEM((rows, size), BF16), pltpu.SemaphoreType.DMA((3,))],
            keep=act,
        )
        dpres.append(dpre)
        dpres_other.append(lax.ppermute(dpre, "mp", SWAP))
        bias_terms.append(bias_term)

    def grad(i):
        size = CHUNKS[i]
        shape = sds((half // 2, size), BF16)
        if paired:
            axes = early if i == 0 else late
            spots = [sum(((r >> axes[::-1].index(axis)) & 1) << d for d, axis in enumerate(late[::-1])) for r in range(parts)]
            size_of = block
        else:
            spots, size_of = list(range(half // 128)), 128
        keep, leave = run(
            functools.partial(grad_kernel, spots, size_of),
            "grad",
            (shape, shape),
            (mine, theirs, dpres[i], dpres_other[i]),
        )
        if paired:
            sums.append(Reduction(order, parts, axes, keep, leave))
            return
        both = jnp.concatenate([keep, leave]).astype(F32)
        sums.append(lax.psum_scatter(both, "parts", scatter_dimension=0, tiled=True))

    def step(i):
        if paired:
            sums[i].step()

    def back_half(matrix):
        (dtotal,) = run(back_kernel_of, "back", (sds((rows, half), BF16),), (ratio, matrix, *dpres))
        return dtotal

    def around(dtotal):
        (partial,) = run(local_kernel, "input_local", (sds((rows, half), F32),), (adj_t, dtotal))
        return partial

    back_kernel_of = functools.partial(back_kernel, len(CHUNKS))

    mine, theirs = run(
        functools.partial(finish_kernel, late, block),
        "finish_mixed",
        (sds((half, rows), BF16), sds((half, rows), BF16)),
        (recv_row, ratio_row, mixed_t, *arrived),
        scalars=(place,),
    )
    theirs = lax.ppermute(theirs, "mp", SWAP)
    for i in range(len(CHUNKS)):
        gelu(i)
    grad(0)
    grad(1)

    extra = max(128, width // parts)
    pieces = 2 if paired else 1
    sent = run(
        functools.partial(
            sent_kernel, len(CHUNKS), parts, per_part, first if paired else [list(range(parts))]
        ),
        "sent_grads",
        (sds((slots // pieces, width + extra), BF16),) * pieces,
        (back_row, ratio_row, weight, other, *dpres, *bias_terms),
        scalars=(place,),
        scratch=[pltpu.VMEM((8, width), F32)],
    )
    if paired:
        swap = Exchange(order, parts, back, per_part, sent)
    else:
        returned = [exchange(sent[0])]

    def pass_on():
        if paired:
            swap.step()

    grad(2)
    step(0)
    step(1)
    pass_on()
    dtotal_own = back_half(weight)
    step(2)
    dtotal_other = back_half(other)
    step(0)
    step(1)
    pass_on()
    partial_own = around(dtotal_own)
    step(2)
    partial_other = around(dtotal_other)
    step(0)
    step(1)
    pass_on()
    step(2)
    if paired:
        returned = [swap.stay, swap.arrived]
    input_grad, bias_all = run(
        input_kernel,
        "input_gradient",
        (sds((rows, width), BF16), sds((1, extra), F32)),
        (send_row, partial_own, partial_other, *returned),
        scalars=(place,),
    )
    if paired:
        (weight_grad,) = run(
            last_kernel, "last_sum", (sds((block, width), F32),), [x for s in sums for x in (s.keep, s.arrived)]
        )
    else:
        weight_grad = jnp.concatenate(sums, axis=1)
    bias_all = bias_all + lax.ppermute(bias_all, "mp", SWAP)
    count = width // (2 * parts)
    bias_grad = jnp.where(core == 0, bias_all[0, :count], bias_all[0, count : 2 * count])
    return (
        act.reshape(batches, nodes, width),
        input_grad.reshape(batches, nodes, width),
        weight_grad,
        bias_grad,
    )


def solution(mesh):
    return jax.shard_map(
        functools.partial(local, mesh.shape["parts"]),
        mesh=mesh,
        in_specs=(
            P("mp", "parts", None),
            P("mp", None),
            P("mp"),
            P("mp", "parts", None),
            P("mp", "parts", None, None),
            P("mp", "parts", None, None),
            P("mp", "parts", None),
        ),
        out_specs=(
            P("mp", "parts", None),
            P("mp", "parts", None),
            P(("parts", "mp"), None),
            P(("parts", "mp")),
        ),
        check_vma=False,
    )
```

time: 277 us -> 116 us (0.42)
  waiting for transfers between devices: 111 us -> 28.2 us
  matrix products: 55.7 us -> 0 us
  Pallas kernels: 0 us -> 50.2 us
  blocking collectives: 49 us -> 0 us
  between operations: 14.4 us -> 0.97 us
  local copies, waits for them, and re-layouts: 15.6 us -> 2.66 us
  starting transfers between devices: 25 us -> 33.2 us
  other arithmetic: 3.57 us -> 0.66 us
    reduce_scatter x1 -> x0, waiting for transfers between devices: 101 us -> none  [local(): lax.psum_scatter(weight_term, ('parts', 'mp'), scatter_dimension=0, tiled...]
    dot_general x16 -> x0, matrix products: 55.7 us -> none  [the longest x2 16.1 us: local(): jnp.dot(mixed, weight_full, preferred_element_type=jnp.float32)]
    pallas_call x0 -> x32, Pallas kernels: none -> 50.2 us  [run(): pl.pallas_call(body, name=name, in_specs=specs, out_specs=(VMEM if keep i...]
    unnamed x1 -> x0, blocking collectives: 45.9 us -> none
    ppermute x0 -> x29, starting transfers between devices: none -> 33.2 us  [the longest x12 12.8 us: send(): lax.ppermute(leave, AXES, partners(self.parts, self.axes.pop(0)))]
    ppermute x0 -> x29, waiting for transfers between devices: none -> 28.2 us  [the longest x12 12.5 us: send(): lax.ppermute(leave, AXES, partners(self.parts, self.axes.pop(0)))]
    all_to_all x4 -> x0, starting transfers between devices: 24.9 us -> none  [the longest x2 12.7 us: local(): lax.all_to_all(dsent, 'parts', split_axis=0, concat_axis=0, tiled=True)]
    all_to_all x4 -> x0, waiting for transfers between devices: 9.61 us -> none  [the longest x2 9.61 us: local(): lax.all_to_all(outgoing, 'parts', split_axis=0, concat_axis=0, tiled=True)]
  transfers between devices with their start and end apart: 6 -> 29, of which waited for: 3 -> 9; matrix products, arithmetic and copies ran while one was open for 15% -> 0% of each run, Pallas kernels for 0% -> 40%
where the time goes in v1:
time: 116 us
  Pallas kernels  50.2 us (43%)
  starting transfers between devices  33.2 us (29%)
  waiting for transfers between devices  28.2 us (24%)
  local copies, waits for them, and re-layouts  2.66 us (2%)
    pallas_call x32, Pallas kernels, run(): pl.pallas_call(body, name=name, in_specs=specs, out_specs=(VMEM if keep i...  50.2 us
    ppermute x12, starting transfers between devices, send(): lax.ppermute(leave, AXES, partners(self.parts, self.axes.pop(0)))  12.8 us
    ppermute x12, waiting for transfers between devices, send(): lax.ppermute(leave, AXES, partners(self.parts, self.axes.pop(0)))  12.5 us
    ppermute x6, starting transfers between devices, move(): moved.append(lax.ppermute(pieces[i], 'parts', perm))  7.84 us
    ppermute x6, waiting for transfers between devices, move(): moved.append(lax.ppermute(pieces[i], 'parts', perm))  6.78 us
    ppermute x1, starting transfers between devices, local(): bias_all = bias_all + lax.ppermute(bias_all, 'mp', SWAP)  5.27 us
    ppermute x3, waiting for transfers between devices, gelu(): dpres_other.append(lax.ppermute(dpre, 'mp', SWAP))  3.47 us
    ppermute x1, waiting for transfers between devices, __init__(): self.arrived = lax.ppermute(leave, AXES, partners(parts, self.axes.pop(0)))  3.19 us
  transfers between devices with their start and end apart: 29, of which 9 were waited for; matrix products, arithmetic and copies ran while one was open for 0% of the time, Pallas kernels for 40%

profile of v1, /device:TPU:1, one launch (start us, length us, event | category | flops | bytes accessed | tf_op | source)
XLA Modules:
  0.0 115.8 jit_solution(4670457584085543869)
XLA Ops:
  0.8 1.3 %copy-done.1 = s32[2,384,384]{2,1,0:T(8,128)S(1)} copy-done((s32[2,384,384]{2,1,0:T(8,128)S(1)}, s32[2,384,384]{2,1,0:T(8,128)}, u32[]{:S(2)}) %copy-start.1) | copy-done | bytes 1179672
  2.1 0.7 copy-done.2
  2.8 0.7 copy-done.3
  3.5 2.8 %outgoing.1 = (bf16[768,2048]{1,0:T(8,128)(2,1)S(1)}, s32[2,384,384]{2,1,0:T(8,128)S(1)}, s32[1,128]{1,0:T(1,128)S(1)}, s32[1,128]{1,0:T(1,128)S(1)}, s32[1,128]...) custom-call(s32[2]{0:T(128)S(1)} %pad_add_fusion.refs_0_, ...), custom_call_target="tpu_custom_call" | custom-call | flops 1 | bytes 1 | tf_op jit(solution)/shard_map/outgoing/pallas_call | solution.py:53
  6.3 2.8 %collective-permute-start.1 = (bf16[32,2048]{1,0:T(8,128)(2,1)S(1)}, bf16[32,2048]{1,0:T(8,128)(2,1)S(1)}, u32[]{:S(2)}, u32[]{:S(2)}) collective-permute-start(bf16[32,2048]{1,0:T(8,128)(2,1)S(1)} %get-tuple-element.116), channel_id=1, source_target_pairs={{0,8},{2,10},{4,12},{6,14},{8,0},{10,2},{12,4},{14,6},{16,24},{18,... | collective-permute-start | bytes 393224 | tf_op jit(solution)/shard_map/ppermute | solution.py:457
  9.1 2.3 %collective-permute-start.2 = (bf16[32,2048]{1,0:T(8,128)(2,1)S(1)}, bf16[32,2048]{1,0:T(8,128)(2,1)S(1)}, u32[]{:S(2)}, u32[]{:S(2)}) collective-permute-start(bf16[32,2048]{1,0:T(8,128)(2,1)S(1)} %get-tuple-element.117), channel_id=1, source_target_pairs={{0,16},{2,18},{4,20},{6,22},{8,24},{10,26},{12,28},{14,30},{16,0},... | collective-permute-start | bytes 393224 | tf_op jit(solution)/shard_map/ppermute | solution.py:457
  11.4 2.4 %mix.1 = (bf16[2,768,1024]{2,1,0:T(8,128)(2,1)S(1)}, bf16[2048,768]{1,0:T(8,128)(2,1)S(1)}, f32[768,1]{1,0:T(8,128)S(1)}, f32[8,768]{1,0:T(8,128)S(1)}, bf16[2,3...) custom-call(bf16[1024,2048]{1,0:T(8,128)(2,1)} %refs_0_.1, ...), custom_call_target="tpu_custom_call" | custom-call | flops 1 | bytes 1 | tf_op jit(solution)/shard_map/mix/pallas_call | solution.py:53
  13.9 1.3 %collective-permute-done.1.refs_1_ = bf16[32,2048]{1,0:T(8,128)(2,1)S(1)} collective-permute-done((bf16[32,2048]{1,0:T(8,128)(2,1)S(1)}, bf16[32,2048]{1,0:T(8,128)(2,1)S(1)}, u32[]{:S(2)}, u32[]{:S(2)}) %collective-permute-start.1) | collective-permute-done | bytes 131104 | tf_op jit(solution)/shard_map/ppermute | solution.py:457
  15.2 5.5 %collective-permute-done.3.refs_3_ = bf16[32,2048]{1,0:T(8,128)(2,1)S(1)} collective-permute-done((bf16[32,2048]{1,0:T(8,128)(2,1)S(1)}, bf16[32,2048]{1,0:T(8,128)(2,1)S(1)}, u32[]{:S(2)}, u32[]{:S(2)}) %collective-permute-start.3) | collective-permute-done | bytes 131104 | tf_op jit(solution)/shard_map/ppermute | solution.py:457
  20.7 1.3 %collective-permute-start.4 = (bf16[32,2048]{1,0:T(8,128)(2,1)S(1)}, bf16[32,2048]{1,0:T(8,128)(2,1)S(1)}, u32[]{:S(2)}, u32[]{:S(2)}) collective-permute-start(bf16[32,2048]{1,0:T(8,128)(2,1)S(1)} %get-tuple-element.123), channel_id=1, source_target_pairs={{0,2},{2,0},{4,6},{6,4},{8,10},{10,8},{12,14},{14,12},{16,18},{18,... | collective-permute-start | bytes 393224 | tf_op jit(solution)/shard_map/ppermute | solution.py:457
  21.9 1.2 %collective-permute-start.5 = (bf16[32,2048]{1,0:T(8,128)(2,1)S(1)}, bf16[32,2048]{1,0:T(8,128)(2,1)S(1)}, u32[]{:S(2)}, u32[]{:S(2)}) collective-permute-start(bf16[32,2048]{1,0:T(8,128)(2,1)S(1)} %get-tuple-element.124), channel_id=1, source_target_pairs={{0,4},{2,6},{4,0},{6,2},{8,12},{10,14},{12,8},{14,10},{16,20},{18,... | collective-permute-start | bytes 393224 | tf_op jit(solution)/shard_map/ppermute | solution.py:457
  23.4 2.6 %collective-permute-start.7 = (bf16[1,1024]{1,0:T(2,128)(2,1)S(1)}, bf16[1,1024]{1,0:T(2,128)(2,1)S(1)}, u32[]{:S(2)}, u32[]{:S(2)}) collective-permute-start(bf16[1,1024]{1,0:T(2,128)(2,1)S(1)} %reshape.26.refs_4_), channel_id=1, source_target_pairs={{0,1},{1,0},{2,3},{3,2},{4,5},{5,4},{6,7},{7,6},{8,9},{9,8},{10,11... | collective-permute-start | bytes 6152 | tf_op jit(solution)/shard_map/ppermute | solution.py:468
  26.0 4.0 %pre_own.1 = (f32[768,2048]{1,0:T(8,128)S(1)}, bf16[1024,2048]{1,0:T(8,128)(2,1)S(1)}, f32[8,128]{1,0:T(8,128)S(1)}) custom-call(s32[2]{0:T(128)S(1)} %pad_add_fusion.refs_0_, bf16[1024,2048]{1,0:T(8,128)(2,1)} %collective-permute-done.refs_1_, bf16[2,768,1024]{2,1,0:T(8,128)(2,1)S(1)} %get-tuple-element.114.refs_2_, ...), custom_call_target="tpu_custom_call" | custom-call | flops 1 | bytes 1 | tf_op jit(solution)/shard_map/pre_own/pallas_call | solution.py:53
  30.0 4.1 %pre_other.1 = (f32[768,2048]{1,0:T(8,128)S(1)}, f32[8,128]{1,0:T(8,128)S(1)}) custom-call(s32[2]{0:T(128)S(1)} %pad_add_fusion.refs_0_, f32[768,2048]{1,0:T(8,128)S(1)} %get-tuple-element.126.refs_1_, bf16[2,768,1024]{2,1,0:T(8,128)(2,1)S(1)} %get-tuple-element.114.refs_2_, bf16[1024,2048]{1,0:T(8,128)(2,1)S(1)} %get-tuple-element.121.refs_3_.refs_2_.refs_4_.refs_1_, ...), custom_call_target="tpu_custom_call" | custom-call | flops 1 | bytes 1 | tf_op jit(solution)/shard_map/pre_other/pallas_call | solution.py:53
  34.1 1.9 %remote_product.1 = (bf16[256,2048]{1,0:T(8,128)(2,1)S(1)}, f32[8,128]{1,0:T(8,128)S(1)}) custom-call(s32[2]{0:T(128)S(1)} %pad_add_fusion.refs_0_, bf16[1024,2048]{1,0:T(8,128)(2,1)S(1)} %get-tuple-element.113.refs_3_.refs_1_, bf16[1024,2048]{1,0:T(8,128)(2,1)S(1)} %get-tuple-element.121.refs_3_.refs_2_.refs_4_.refs_1_, ...), custom_call_target="tpu_custom_call" | custom-call | flops 1 | bytes 1 | tf_op jit(solution)/shard_map/remote_product/pallas_call | solution.py:53
  36.0 1.9 %finish_mixed.1 = (bf16[1024,768]{1,0:T(8,128)(2,1)S(1)}, bf16[1024,768]{1,0:T(8,128)(2,1)S(1)}, f32[8,128]{1,0:T(8,128)S(1)}) custom-call(s32[2]{0:T(128)S(1)} %pad_add_fusion.refs_0_, s32[1,128]{1,0:T(1,128)S(1)} %get-tuple-element.108.refs_2_.refs_1_.refs_0_, f32[8,768]{1,0:T(8,128)S(1)} %get-tuple-element.131.refs_2_, ...), custom_call_target="tpu_custom_call" | custom-call | flops 1 | bytes 1 | tf_op jit(solution)/shard_map/finish_mixed/pallas_call | solution.py:53
  38.0 2.2 %gelu.3 = (bf16[768,2048]{1,0:T(8,128)(2,1)}, bf16[768,512]{1,0:T(8,128)(2,1)S(1)}, f32[1,512]{1,0:T(1,128)S(1)}, f32[8,128]{1,0:T(8,128)S(1)}) custom-call(s32[1,128]{1,0:T(1,128)S(1)} %get-tuple-element.108.refs_2_.refs_1_.refs_0_, f32[768,1]{1,0:T(8,128)S(1)} %get-tuple-element.112.refs_1_.refs_0_, bf16[256,2048]{1,0:T(8,128)(2,1)S(1)} %get-tuple-element.129.refs_2_, ...), custom_call_target="tpu_custom_call" | custom-call | flops 1 | bytes 1 | tf_op jit(solution)/shard_map/gelu/pallas_call | solution.py:53
  40.2 2.8 %gelu.4 = (bf16[768,2048]{1,0:T(8,128)(2,1)}, bf16[768,768]{1,0:T(8,128)(2,1)S(1)}, f32[1,768]{1,0:T(1,128)S(1)}, f32[8,128]{1,0:T(8,128)S(1)}) custom-call(s32[1,128]{1,0:T(1,128)S(1)} %get-tuple-element.108.refs_2_.refs_1_.refs_0_, f32[768,1]{1,0:T(8,128)S(1)} %get-tuple-element.112.refs_1_.refs_0_, ...), custom_call_target="tpu_custom_call", output_to_operand_aliasing={{0}: (5, {})} | custom-call | flops 1 | bytes 1 | tf_op jit(solution)/shard_map/gelu/pallas_call | solution.py:53
  43.1 0.5 collective-permute-start.9
  43.6 2.8 %gelu.5 = (bf16[768,2048]{1,0:T(8,128)(2,1)}, bf16[768,768]{1,0:T(8,128)(2,1)S(1)}, f32[1,768]{1,0:T(1,128)S(1)}, f32[8,128]{1,0:T(8,128)S(1)}) custom-call(s32[1,128]{1,0:T(1,128)S(1)} %get-tuple-element.108.refs_2_.refs_1_.refs_0_, f32[768,1]{1,0:T(8,128)S(1)} %get-tuple-element.112.refs_1_.refs_0_, ...), custom_call_target="tpu_custom_call", output_to_operand_aliasing={{0}: (5, {})} | custom-call | flops 1 | bytes 1 | tf_op jit(solution)/shard_map/gelu/pallas_call | solution.py:53
  47.0 3.5 %collective-permute-done.10.refs_3_ = bf16[768,512]{1,0:T(8,128)(2,1)S(1)} collective-permute-done((bf16[768,512]{1,0:T(8,128)(2,1)S(1)}, bf16[768,512]{1,0:T(8,128)(2,1)S(1)}, u32[]{:S(2)}, u32[]{:S(2)}) %collective-permute-start.10) | collective-permute-done | bytes 786464 | tf_op jit(solution)/shard_map/ppermute | solution.py:556
  50.5 1.8 %grad.3 = (bf16[512,512]{1,0:T(8,128)(2,1)S(1)}, bf16[512,512]{1,0:T(8,128)(2,1)S(1)}, f32[8,128]{1,0:T(8,128)S(1)}) custom-call(bf16[1024,768]{1,0:T(8,128)(2,1)S(1)} %get-tuple-element.149.refs_0_, bf16[1024,768]{1,0:T(8,128)(2,1)S(1)} %collective-permute-done.8.refs_1_, bf16[768,512]{1,0:T(8,128)(2,1)S(1)} %get-tuple-element.142.refs_2_.refs_5_, ...), custom_call_target="tpu_custom_call" | custom-call | flops 1 | bytes 1 | tf_op jit(solution)/shard_map/grad/pallas_call | solution.py:53
  52.3 2.7 %grad.4 = (bf16[512,768]{1,0:T(8,128)(2,1)S(1)}, bf16[512,768]{1,0:T(8,128)(2,1)S(1)}, f32[8,128]{1,0:T(8,128)S(1)}) custom-call(bf16[1024,768]{1,0:T(8,128)(2,1)S(1)} %get-tuple-element.149.refs_0_, bf16[1024,768]{1,0:T(8,128)(2,1)S(1)} %collective-permute-done.8.refs_1_, bf16[768,768]{1,0:T(8,128)(2,1)S(1)} %get-tuple-element.143.refs_2_.refs_6_.refs_3_, ...), custom_call_target="tpu_custom_call" | custom-call | flops 1 | bytes 1 | tf_op jit(solution)/shard_map/grad/pallas_call | solution.py:53
  55.0 1.3 %collective-permute-start.12 = (bf16[512,768]{1,0:T(8,128)(2,1)S(1)}, bf16[512,768]{1,0:T(8,128)(2,1)S(1)}, u32[]{:S(2)}, u32[]{:S(2)}) collective-permute-start(bf16[512,768]{1,0:T(8,128)(2,1)S(1)} %get-tuple-element.157), channel_id=1, source_target_pairs={{0,2},{1,5},{2,0},{3,7},{4,6},{5,1},{6,4},{7,3},{8,10},{9,13},{10,... | collective-permute-start | bytes 2359304 | tf_op jit(solution)/shard_map/ppermute | solution.py:391
  56.3 2.4 %collective-permute-start.13 = (bf16[512,512]{1,0:T(8,128)(2,1)S(1)}, bf16[512,512]{1,0:T(8,128)(2,1)S(1)}, u32[]{:S(2)}, u32[]{:S(2)}) collective-permute-start(bf16[512,512]{1,0:T(8,128)(2,1)S(1)} %get-tuple-element.159), channel_id=1, source_target_pairs={{0,8},{1,9},{2,10},{3,11},{4,12},{5,13},{6,14},{7,15},{8,0},{9,1},... | collective-permute-start | bytes 1572872 | tf_op jit(solution)/shard_map/ppermute | solution.py:391
  58.6 3.9 %sent_grads.1 = (bf16[64,2176]{1,0:T(8,128)(2,1)S(1)}, bf16[64,2176]{1,0:T(8,128)(2,1)S(1)}, f32[8,128]{1,0:T(8,128)S(1)}) custom-call(s32[2]{0:T(128)S(1)} %pad_add_fusion.refs_0_, s32[1,128]{1,0:T(1,128)S(1)} %get-tuple-element.145.refs_1_, f32[8,768]{1,0:T(8,128)S(1)} %get-tuple-element.131.refs_2_, ...), custom_call_target="tpu_custom_call" | custom-call | flops 1 | bytes 1 | tf_op jit(solution)/shard_map/sent_grads/pallas_call | solution.py:53
  62.5 2.7 %grad.5 = (bf16[512,768]{1,0:T(8,128)(2,1)S(1)}, bf16[512,768]{1,0:T(8,128)(2,1)S(1)}, f32[8,128]{1,0:T(8,128)S(1)}) custom-call(bf16[1024,768]{1,0:T(8,128)(2,1)S(1)} %get-tuple-element.149.refs_0_, bf16[1024,768]{1,0:T(8,128)(2,1)S(1)} %collective-permute-done.8.refs_1_, bf16[768,768]{1,0:T(8,128)(2,1)S(1)} %get-tuple-element.144.refs_7_.refs_2_.refs_4_, ...), custom_call_target="tpu_custom_call" | custom-call | flops 1 | bytes 1 | tf_op jit(solution)/shard_map/grad/pallas_call | solution.py:53
  65.5 1.0 collective-permute-start.11
  66.5 8.3 %collective-permute-done.13.refs_1_ = bf16[512,512]{1,0:T(8,128)(2,1)S(1)} collective-permute-done((bf16[512,512]{1,0:T(8,128)(2,1)S(1)}, bf16[512,512]{1,0:T(8,128)(2,1)S(1)}, u32[]{:S(2)}, u32[]{:S(2)}) %collective-permute-start.13) | collective-permute-done | bytes 524320 | tf_op jit(solution)/shard_map/ppermute | solution.py:391
  75.2 1.3 %collective-permute-start.16 = (bf16[256,768]{1,0:T(8,128)(2,1)S(1)}, bf16[256,768]{1,0:T(8,128)(2,1)S(1)}, u32[]{:S(2)}, u32[]{:S(2)}) collective-permute-start(bf16[256,768]{1,0:T(8,128)(2,1)S(1)} %get-tuple-element.169), channel_id=1, source_target_pairs={{0,4},{1,3},{2,6},{3,1},{4,0},{5,7},{6,2},{7,5},{8,12},{9,11},{10,... | collective-permute-start | bytes 1179656 | tf_op jit(solution)/shard_map/ppermute | solution.py:391
  76.5 3.2 %collective-permute-done.11.refs_1_ = bf16[64,2176]{1,0:T(8,128)(2,1)S(1)} collective-permute-done((bf16[64,2176]{1,0:T(8,128)(2,1)S(1)}, bf16[64,2176]{1,0:T(8,128)(2,1)S(1)}, u32[]{:S(2)}, u32[]{:S(2)}) %collective-permute-start.11) | collective-permute-done | bytes 278560 | tf_op jit(solution)/shard_map/ppermute | solution.py:405
  79.8 2.5 %collective-permute-start.17 = (bf16[256,512]{1,0:T(8,128)(2,1)S(1)}, bf16[256,512]{1,0:T(8,128)(2,1)S(1)}, u32[]{:S(2)}, u32[]{:S(2)}) collective-permute-start(bf16[256,512]{1,0:T(8,128)(2,1)S(1)} %get-tuple-element.171), channel_id=1, source_target_pairs={{0,16},{1,17},{2,18},{3,19},{4,20},{5,21},{6,22},{7,23},{8,24},{9,... | collective-permute-start | bytes 786440 | tf_op jit(solution)/shard_map/ppermute | solution.py:391
  82.3 3.5 %back.2 = (bf16[768,1024]{1,0:T(8,128)(2,1)S(1)}, f32[8,128]{1,0:T(8,128)S(1)}) custom-call(f32[768,1]{1,0:T(8,128)S(1)} %get-tuple-element.112.refs_1_.refs_0_, bf16[1024,2048]{1,0:T(8,128)(2,1)S(1)} %get-tuple-element.113.refs_3_.refs_1_, bf16[768,512]{1,0:T(8,128)(2,1)S(1)} %get-tuple-element.142.refs_2_.refs_5_, ...), custom_call_target="tpu_custom_call" | custom-call | flops 1 | bytes 1 | tf_op jit(solution)/shard_map/back/pallas_call | solution.py:53
  85.9 1.3 %collective-permute-start.19 = (bf16[256,768]{1,0:T(8,128)(2,1)S(1)}, bf16[256,768]{1,0:T(8,128)(2,1)S(1)}, u32[]{:S(2)}, u32[]{:S(2)}) collective-permute-start(bf16[256,768]{1,0:T(8,128)(2,1)S(1)} %get-tuple-element.183), channel_id=1, source_target_pairs={{0,4},{1,3},{2,6},{3,1},{4,0},{5,7},{6,2},{7,5},{8,12},{9,11},{10,... | collective-permute-start | bytes 1179656 | tf_op jit(solution)/shard_map/ppermute | solution.py:391
  87.2 3.7 %back.3 = (bf16[768,1024]{1,0:T(8,128)(2,1)S(1)}, f32[8,128]{1,0:T(8,128)S(1)}) custom-call(f32[768,1]{1,0:T(8,128)S(1)} %get-tuple-element.112.refs_1_.refs_0_, bf16[1024,2048]{1,0:T(8,128)(2,1)S(1)} %get-tuple-element.121.refs_3_.refs_2_.refs_4_.refs_1_, bf16[768,512]{1,0:T(8,128)(2,1)S(1)} %get-tuple-element.142.refs_2_.refs_5_, ...), custom_call_target="tpu_custom_call" | custom-call | flops 1 | bytes 1 | tf_op jit(solution)/shard_map/back/pallas_call | solution.py:53
  91.1 1.7 %collective-permute-done.15.refs_1_ = bf16[64,2176]{1,0:T(8,128)(2,1)S(1)} collective-permute-done((bf16[64,2176]{1,0:T(8,128)(2,1)S(1)}, bf16[64,2176]{1,0:T(8,128)(2,1)S(1)}, u32[]{:S(2)}, u32[]{:S(2)}) %collective-permute-start.15) | collective-permute-done | bytes 278560 | tf_op jit(solution)/shard_map/ppermute | solution.py:418
  92.9 0.9 collective-permute-start.20
  93.8 1.9 %collective-permute-start.21 = (bf16[128,768]{1,0:T(8,128)(2,1)S(1)}, bf16[128,768]{1,0:T(8,128)(2,1)S(1)}, u32[]{:S(2)}, u32[]{:S(2)}) collective-permute-start(bf16[128,768]{1,0:T(8,128)(2,1)S(1)} %get-tuple-element.190), channel_id=1, source_target_pairs={{0,8},{1,9},{2,10},{3,11},{4,12},{5,13},{6,14},{7,15},{8,0},{9,1},... | collective-permute-start | bytes 589832 | tf_op jit(solution)/shard_map/ppermute | solution.py:391
  95.8 1.0 input_local.2
  97.1 1.0 input_local.3
  98.1 2.1 %collective-permute-done.22.refs_1_ = bf16[128,512]{1,0:T(8,128)(2,1)S(1)} collective-permute-done((bf16[128,512]{1,0:T(8,128)(2,1)S(1)}, bf16[128,512]{1,0:T(8,128)(2,1)S(1)}, u32[]{:S(2)}, u32[]{:S(2)}) %collective-permute-start.22) | collective-permute-done | bytes 131104 | tf_op jit(solution)/shard_map/ppermute | solution.py:391
  100.3 1.3 %collective-permute-start.23 = (bf16[64,2176]{1,0:T(8,128)(2,1)S(1)}, bf16[64,2176]{1,0:T(8,128)(2,1)S(1)}, u32[]{:S(2)}, u32[]{:S(2)}) collective-permute-start(bf16[64,2176]{1,0:T(8,128)(2,1)S(1)} %get-tuple-element.197), channel_id=1, source_target_pairs={{0,4},{1,3},{2,6},{3,1},{4,0},{5,7},{6,2},{7,5},{8,12},{9,11},{10,... | collective-permute-start | bytes 835592 | tf_op jit(solution)/shard_map/ppermute | solution.py:418
  101.8 2.1 %collective-permute-done.24.refs_1_ = bf16[128,768]{1,0:T(8,128)(2,1)S(1)} collective-permute-done((bf16[128,768]{1,0:T(8,128)(2,1)S(1)}, bf16[128,768]{1,0:T(8,128)(2,1)S(1)}, u32[]{:S(2)}, u32[]{:S(2)}) %collective-permute-start.24) | collective-permute-done | bytes 196640 | tf_op jit(solution)/shard_map/ppermute | solution.py:391
  104.1 1.3 %collective-permute-start.25 = (bf16[64,512]{1,0:T(8,128)(2,1)S(1)}, bf16[64,512]{1,0:T(8,128)(2,1)S(1)}, u32[]{:S(2)}, u32[]{:S(2)}) collective-permute-start(bf16[64,512]{1,0:T(8,128)(2,1)S(1)} %get-tuple-element.204), channel_id=1, source_target_pairs={{0,4},{1,3},{2,6},{3,1},{4,0},{5,7},{6,2},{7,5},{8,12},{9,11},{10,... | collective-permute-start | bytes 196616 | tf_op jit(solution)/shard_map/ppermute | solution.py:391
  105.9 3.2 %input_gradient.1 = (bf16[768,2048]{1,0:T(8,128)(2,1)}, f32[1,128]{1,0:T(1,128)S(1)}, f32[8,128]{1,0:T(8,128)S(1)}) custom-call(s32[2]{0:T(128)S(1)} %pad_add_fusion.refs_0_, s32[1,128]{1,0:T(1,128)S(1)} %get-tuple-element.140.refs_1_, f32[768,1024]{1,0:T(8,128)S(1)} %get-tuple-element.180.refs_2_, f32[768,1024]{1,0:T(8,128)S(1)} %get-tuple-element.186.refs_3_, ...), custom_call_target="tpu_custom_call" | custom-call | flops 1 | bytes 1 | tf_op jit(solution)/shard_map/input_gradient/pallas_call | solution.py:53
  109.1 5.3 %collective-permute-start.28 = (f32[1,128]{1,0:T(1,128)S(1)}, f32[1,128]{1,0:T(1,128)S(1)}, u32[]{:S(2)}, u32[]{:S(2)}) collective-permute-start(f32[1,128]{1,0:T(1,128)S(1)} %get-tuple-element.211), channel_id=1, source_target_pairs={{0,1},{1,0},{2,3},{3,2},{4,5},{5,4},{6,7},{7,6},{8,9},{9,8},{10,11... | collective-permute-start | bytes 1544 | tf_op jit(solution)/shard_map/ppermute | solution.py:660
  114.4 0.9 last_sum.1
  115.2 0.6 fusion
  (56 shorter events, 3.6 us)
Async XLA Ops:
  0.6 25.4 %collective-permute-start = (bf16[1024,2048]{1,0:T(8,128)(2,1)}, bf16[1024,2048]{1,0:T(8,128)(2,1)}, u32[]{:S(2)}, u32[]{:S(2)}) collective-permute-start(bf16[1024,2048]{1,0:T(8,128)(2,1)} %refs_0_.1), channel_id=1, source_target_pairs={{0,1},{1,0},{2,3},{3,2},{4,5},{5,4},{6,7},{7,6},{8,9},{9,8},{10,11... | collective-permute-start | bytes 12582920 | tf_op jit(solution)/shard_map/ppermute | solution.py:466
  0.8 1.3 %copy-start.1 = (s32[2,384,384]{2,1,0:T(8,128)S(1)}, s32[2,384,384]{2,1,0:T(8,128)}, u32[]{:S(2)}) copy-start(s32[2,384,384]{2,1,0:T(8,128)} %refs_2_.1) | copy-start | bytes 3538948
  2.1 0.7 copy-start.2
  2.8 0.7 copy-start.3
  6.3 8.8 %collective-permute-start.1 = (bf16[32,2048]{1,0:T(8,128)(2,1)S(1)}, bf16[32,2048]{1,0:T(8,128)(2,1)S(1)}, u32[]{:S(2)}, u32[]{:S(2)}) collective-permute-start(bf16[32,2048]{1,0:T(8,128)(2,1)S(1)} %get-tuple-element.116), channel_id=1, source_target_pairs={{0,8},{2,10},{4,12},{6,14},{8,0},{10,2},{12,4},{14,6},{16,24},{18,... | collective-permute-start | bytes 393224 | tf_op jit(solution)/shard_map/ppermute | solution.py:457
  9.1 6.0 %collective-permute-start.2 = (bf16[32,2048]{1,0:T(8,128)(2,1)S(1)}, bf16[32,2048]{1,0:T(8,128)(2,1)S(1)}, u32[]{:S(2)}, u32[]{:S(2)}) collective-permute-start(bf16[32,2048]{1,0:T(8,128)(2,1)S(1)} %get-tuple-element.117), channel_id=1, source_target_pairs={{0,16},{2,18},{4,20},{6,22},{8,24},{10,26},{12,28},{14,30},{16,0},... | collective-permute-start | bytes 393224 | tf_op jit(solution)/shard_map/ppermute | solution.py:457
  11.4 9.2 %collective-permute-start.3 = (bf16[32,2048]{1,0:T(8,128)(2,1)S(1)}, bf16[32,2048]{1,0:T(8,128)(2,1)S(1)}, u32[]{:S(2)}, u32[]{:S(2)}) collective-permute-start(bf16[32,2048]{1,0:T(8,128)(2,1)S(1)} %get-tuple-element.118), channel_id=1, source_target_pairs={{0,24},{2,26},{4,28},{6,30},{8,16},{10,18},{12,20},{14,22},{16,8},... | collective-permute-start | bytes 393224 | tf_op jit(solution)/shard_map/ppermute | solution.py:457
  11.4 11.9 %copy-start.4 = (bf16[1024]{0:T(1024)(128)(2,1)S(1)}, bf16[1024]{0:T(1024)(128)(2,1)}, u32[]{:S(2)}) copy-start(bf16[1024]{0:T(1024)(128)(2,1)} %param.9) | copy-start | bytes 6148
  20.7 13.4 %collective-permute-start.4 = (bf16[32,2048]{1,0:T(8,128)(2,1)S(1)}, bf16[32,2048]{1,0:T(8,128)(2,1)S(1)}, u32[]{:S(2)}, u32[]{:S(2)}) collective-permute-start(bf16[32,2048]{1,0:T(8,128)(2,1)S(1)} %get-tuple-element.123), channel_id=1, source_target_pairs={{0,2},{2,0},{4,6},{6,4},{8,10},{10,8},{12,14},{14,12},{16,18},{18,... | collective-permute-start | bytes 393224 | tf_op jit(solution)/shard_map/ppermute | solution.py:457
  21.9 12.1 %collective-permute-start.5 = (bf16[32,2048]{1,0:T(8,128)(2,1)S(1)}, bf16[32,2048]{1,0:T(8,128)(2,1)S(1)}, u32[]{:S(2)}, u32[]{:S(2)}) collective-permute-start(bf16[32,2048]{1,0:T(8,128)(2,1)S(1)} %get-tuple-element.124), channel_id=1, source_target_pairs={{0,4},{2,6},{4,0},{6,2},{8,12},{10,14},{12,8},{14,10},{16,20},{18,... | collective-permute-start | bytes 393224 | tf_op jit(solution)/shard_map/ppermute | solution.py:457
  23.2 10.9 %collective-permute-start.6 = (bf16[32,2048]{1,0:T(8,128)(2,1)S(1)}, bf16[32,2048]{1,0:T(8,128)(2,1)S(1)}, u32[]{:S(2)}, u32[]{:S(2)}) collective-permute-start(bf16[32,2048]{1,0:T(8,128)(2,1)S(1)} %get-tuple-element.125), channel_id=1, source_target_pairs={{0,6},{2,4},{4,2},{6,0},{8,14},{10,12},{12,10},{14,8},{16,22},{18,... | collective-permute-start | bytes 393224 | tf_op jit(solution)/shard_map/ppermute | solution.py:457
  23.4 6.6 %collective-permute-start.7 = (bf16[1,1024]{1,0:T(2,128)(2,1)S(1)}, bf16[1,1024]{1,0:T(2,128)(2,1)S(1)}, u32[]{:S(2)}, u32[]{:S(2)}) collective-permute-start(bf16[1,1024]{1,0:T(2,128)(2,1)S(1)} %reshape.26.refs_4_), channel_id=1, source_target_pairs={{0,1},{1,0},{2,3},{3,2},{4,5},{5,4},{6,7},{7,6},{8,9},{9,8},{10,11... | collective-permute-start | bytes 6152 | tf_op jit(solution)/shard_map/ppermute | solution.py:468
  36.0 2.1 %copy-start = (bf16[2,384,2048]{2,1,0:T(8,128)(2,1)S(1)}, bf16[2,384,2048]{2,1,0:T(8,128)(2,1)}, u32[]{:S(2)}) copy-start(bf16[2,384,2048]{2,1,0:T(8,128)(2,1)} %param.13) | copy-start | bytes 9437188
  38.0 12.5 %collective-permute-start.8 = (bf16[1024,768]{1,0:T(8,128)(2,1)S(1)}, bf16[1024,768]{1,0:T(8,128)(2,1)S(1)}, u32[]{:S(2)}, u32[]{:S(2)}) collective-permute-start(bf16[1024,768]{1,0:T(8,128)(2,1)S(1)} %get-tuple-element.150), channel_id=1, source_target_pairs={{0,1},{1,0},{2,3},{3,2},{4,5},{5,4},{6,7},{7,6},{8,9},{9,8},{10,11... | collective-permute-start | bytes 4718600 | tf_op jit(solution)/shard_map/ppermute | solution.py:601
  43.1 9.2 %collective-permute-start.9 = (bf16[768,768]{1,0:T(8,128)(2,1)S(1)}, bf16[768,768]{1,0:T(8,128)(2,1)S(1)}, u32[]{:S(2)}, u32[]{:S(2)}) collective-permute-start(bf16[768,768]{1,0:T(8,128)(2,1)S(1)} %get-tuple-element.143.refs_2_.refs_6_.refs_3_), channel_id=1, source_target_pairs={{0,1},{1,0},{2,3},{3,2},{4,5},{5,4},{6,7},{7,6},{8,9},{9,8},{10,11... | collective-permute-start | bytes 3538952 | tf_op jit(solution)/shard_map/ppermute | solution.py:556
  46.4 16.1 %collective-permute-start.14 = (bf16[768,768]{1,0:T(8,128)(2,1)S(1)}, bf16[768,768]{1,0:T(8,128)(2,1)S(1)}, u32[]{:S(2)}, u32[]{:S(2)}) collective-permute-start(bf16[768,768]{1,0:T(8,128)(2,1)S(1)} %get-tuple-element.144.refs_7_.refs_2_.refs_4_), channel_id=1, source_target_pairs={{0,1},{1,0},{2,3},{3,2},{4,5},{5,4},{6,7},{7,6},{8,9},{9,8},{10,11... | collective-permute-start | bytes 3538952 | tf_op jit(solution)/shard_map/ppermute | solution.py:556
  46.5 3.9 %collective-permute-start.10 = (bf16[768,512]{1,0:T(8,128)(2,1)S(1)}, bf16[768,512]{1,0:T(8,128)(2,1)S(1)}, u32[]{:S(2)}, u32[]{:S(2)}) collective-permute-start(bf16[768,512]{1,0:T(8,128)(2,1)S(1)} %get-tuple-element.142.refs_2_.refs_5_), channel_id=1, source_target_pairs={{0,1},{1,0},{2,3},{3,2},{4,5},{5,4},{6,7},{7,6},{8,9},{9,8},{10,11... | collective-permute-start | bytes 2359304 | tf_op jit(solution)/shard_map/ppermute | solution.py:556
  55.0 20.0 %collective-permute-start.12 = (bf16[512,768]{1,0:T(8,128)(2,1)S(1)}, bf16[512,768]{1,0:T(8,128)(2,1)S(1)}, u32[]{:S(2)}, u32[]{:S(2)}) collective-permute-start(bf16[512,768]{1,0:T(8,128)(2,1)S(1)} %get-tuple-element.157), channel_id=1, source_target_pairs={{0,2},{1,5},{2,0},{3,7},{4,6},{5,1},{6,4},{7,3},{8,10},{9,13},{10,... | collective-permute-start | bytes 2359304 | tf_op jit(solution)/shard_map/ppermute | solution.py:391
  56.3 18.6 %collective-permute-start.13 = (bf16[512,512]{1,0:T(8,128)(2,1)S(1)}, bf16[512,512]{1,0:T(8,128)(2,1)S(1)}, u32[]{:S(2)}, u32[]{:S(2)}) collective-permute-start(bf16[512,512]{1,0:T(8,128)(2,1)S(1)} %get-tuple-element.159), channel_id=1, source_target_pairs={{0,8},{1,9},{2,10},{3,11},{4,12},{5,13},{6,14},{7,15},{8,0},{9,1},... | collective-permute-start | bytes 1572872 | tf_op jit(solution)/shard_map/ppermute | solution.py:391
  65.2 20.5 %collective-permute-start.18 = (bf16[512,768]{1,0:T(8,128)(2,1)S(1)}, bf16[512,768]{1,0:T(8,128)(2,1)S(1)}, u32[]{:S(2)}, u32[]{:S(2)}) collective-permute-start(bf16[512,768]{1,0:T(8,128)(2,1)S(1)} %get-tuple-element.173), channel_id=1, source_target_pairs={{0,2},{1,5},{2,0},{3,7},{4,6},{5,1},{6,4},{7,3},{8,10},{9,13},{10,... | collective-permute-start | bytes 2359304 | tf_op jit(solution)/shard_map/ppermute | solution.py:391
  65.5 14.2 %collective-permute-start.11 = (bf16[64,2176]{1,0:T(8,128)(2,1)S(1)}, bf16[64,2176]{1,0:T(8,128)(2,1)S(1)}, u32[]{:S(2)}, u32[]{:S(2)}) collective-permute-start(bf16[64,2176]{1,0:T(8,128)(2,1)S(1)} %get-tuple-element.155), channel_id=1, source_target_pairs={{0,16},{1,17},{2,18},{3,19},{4,20},{5,21},{6,22},{7,23},{8,24},{9,... | collective-permute-start | bytes 835592 | tf_op jit(solution)/shard_map/ppermute | solution.py:405
  75.2 15.9 %collective-permute-start.16 = (bf16[256,768]{1,0:T(8,128)(2,1)S(1)}, bf16[256,768]{1,0:T(8,128)(2,1)S(1)}, u32[]{:S(2)}, u32[]{:S(2)}) collective-permute-start(bf16[256,768]{1,0:T(8,128)(2,1)S(1)} %get-tuple-element.169), channel_id=1, source_target_pairs={{0,4},{1,3},{2,6},{3,1},{4,0},{5,7},{6,2},{7,5},{8,12},{9,11},{10,... | collective-permute-start | bytes 1179656 | tf_op jit(solution)/shard_map/ppermute | solution.py:391
  79.7 13.2 %collective-permute-start.15 = (bf16[64,2176]{1,0:T(8,128)(2,1)S(1)}, bf16[64,2176]{1,0:T(8,128)(2,1)S(1)}, u32[]{:S(2)}, u32[]{:S(2)}) collective-permute-start(bf16[64,2176]{1,0:T(8,128)(2,1)S(1)} %get-tuple-element.167), channel_id=1, source_target_pairs={{0,8},{1,9},{2,10},{3,11},{4,12},{5,13},{6,14},{7,15},{8,0},{9,1},... | collective-permute-start | bytes 835592 | tf_op jit(solution)/shard_map/ppermute | solution.py:418
  79.8 11.2 %collective-permute-start.17 = (bf16[256,512]{1,0:T(8,128)(2,1)S(1)}, bf16[256,512]{1,0:T(8,128)(2,1)S(1)}, u32[]{:S(2)}, u32[]{:S(2)}) collective-permute-start(bf16[256,512]{1,0:T(8,128)(2,1)S(1)} %get-tuple-element.171), channel_id=1, source_target_pairs={{0,16},{1,17},{2,18},{3,19},{4,20},{5,21},{6,22},{7,23},{8,24},{9,... | collective-permute-start | bytes 786440 | tf_op jit(solution)/shard_map/ppermute | solution.py:391
  85.9 10.9 %collective-permute-start.19 = (bf16[256,768]{1,0:T(8,128)(2,1)S(1)}, bf16[256,768]{1,0:T(8,128)(2,1)S(1)}, u32[]{:S(2)}, u32[]{:S(2)}) collective-permute-start(bf16[256,768]{1,0:T(8,128)(2,1)S(1)} %get-tuple-element.183), channel_id=1, source_target_pairs={{0,4},{1,3},{2,6},{3,1},{4,0},{5,7},{6,2},{7,5},{8,12},{9,11},{10,... | collective-permute-start | bytes 1179656 | tf_op jit(solution)/shard_map/ppermute | solution.py:391
  92.9 7.4 %collective-permute-start.20 = (bf16[64,2176]{1,0:T(8,128)(2,1)S(1)}, bf16[64,2176]{1,0:T(8,128)(2,1)S(1)}, u32[]{:S(2)}, u32[]{:S(2)}) collective-permute-start(bf16[64,2176]{1,0:T(8,128)(2,1)S(1)} %get-tuple-element.188), channel_id=1, source_target_pairs={{0,2},{1,5},{2,0},{3,7},{4,6},{5,1},{6,4},{7,3},{8,10},{9,13},{10,... | collective-permute-start | bytes 835592 | tf_op jit(solution)/shard_map/ppermute | solution.py:418
  93.8 6.4 %collective-permute-start.21 = (bf16[128,768]{1,0:T(8,128)(2,1)S(1)}, bf16[128,768]{1,0:T(8,128)(2,1)S(1)}, u32[]{:S(2)}, u32[]{:S(2)}) collective-permute-start(bf16[128,768]{1,0:T(8,128)(2,1)S(1)} %get-tuple-element.190), channel_id=1, source_target_pairs={{0,8},{1,9},{2,10},{3,11},{4,12},{5,13},{6,14},{7,15},{8,0},{9,1},... | collective-permute-start | bytes 589832 | tf_op jit(solution)/shard_map/ppermute | solution.py:391
  95.7 4.4 %collective-permute-start.22 = (bf16[128,512]{1,0:T(8,128)(2,1)S(1)}, bf16[128,512]{1,0:T(8,128)(2,1)S(1)}, u32[]{:S(2)}, u32[]{:S(2)}) collective-permute-start(bf16[128,512]{1,0:T(8,128)(2,1)S(1)} %get-tuple-element.192), channel_id=1, source_target_pairs={{0,2},{1,5},{2,0},{3,7},{4,6},{5,1},{6,4},{7,3},{8,10},{9,13},{10,... | collective-permute-start | bytes 393224 | tf_op jit(solution)/shard_map/ppermute | solution.py:391
  96.9 6.9 %collective-permute-start.24 = (bf16[128,768]{1,0:T(8,128)(2,1)S(1)}, bf16[128,768]{1,0:T(8,128)(2,1)S(1)}, u32[]{:S(2)}, u32[]{:S(2)}) collective-permute-start(bf16[128,768]{1,0:T(8,128)(2,1)S(1)} %get-tuple-element.199), channel_id=1, source_target_pairs={{0,8},{1,9},{2,10},{3,11},{4,12},{5,13},{6,14},{7,15},{8,0},{9,1},... | collective-permute-start | bytes 589832 | tf_op jit(solution)/shard_map/ppermute | solution.py:391
  100.3 5.6 %collective-permute-start.23 = (bf16[64,2176]{1,0:T(8,128)(2,1)S(1)}, bf16[64,2176]{1,0:T(8,128)(2,1)S(1)}, u32[]{:S(2)}, u32[]{:S(2)}) collective-permute-start(bf16[64,2176]{1,0:T(8,128)(2,1)S(1)} %get-tuple-element.197), channel_id=1, source_target_pairs={{0,4},{1,3},{2,6},{3,1},{4,0},{5,7},{6,2},{7,5},{8,12},{9,11},{10,... | collective-permute-start | bytes 835592 | tf_op jit(solution)/shard_map/ppermute | solution.py:418
  101.6 12.8 %collective-permute-start.26 = (bf16[64,768]{1,0:T(8,128)(2,1)S(1)}, bf16[64,768]{1,0:T(8,128)(2,1)S(1)}, u32[]{:S(2)}, u32[]{:S(2)}) collective-permute-start(bf16[64,768]{1,0:T(8,128)(2,1)S(1)} %get-tuple-element.206), channel_id=1, source_target_pairs={{0,16},{1,17},{2,18},{3,19},{4,20},{5,21},{6,22},{7,23},{8,24},{9,... | collective-permute-start | bytes 294920 | tf_op jit(solution)/shard_map/ppermute | solution.py:391
  103.9 10.5 %collective-permute-start.27 = (bf16[64,768]{1,0:T(8,128)(2,1)S(1)}, bf16[64,768]{1,0:T(8,128)(2,1)S(1)}, u32[]{:S(2)}, u32[]{:S(2)}) collective-permute-start(bf16[64,768]{1,0:T(8,128)(2,1)S(1)} %get-tuple-element.208), channel_id=1, source_target_pairs={{0,16},{1,17},{2,18},{3,19},{4,20},{5,21},{6,22},{7,23},{8,24},{9,... | collective-permute-start | bytes 294920 | tf_op jit(solution)/shard_map/ppermute | solution.py:391
  104.1 10.3 %collective-permute-start.25 = (bf16[64,512]{1,0:T(8,128)(2,1)S(1)}, bf16[64,512]{1,0:T(8,128)(2,1)S(1)}, u32[]{:S(2)}, u32[]{:S(2)}) collective-permute-start(bf16[64,512]{1,0:T(8,128)(2,1)S(1)} %get-tuple-element.204), channel_id=1, source_target_pairs={{0,4},{1,3},{2,6},{3,1},{4,0},{5,7},{6,2},{7,5},{8,12},{9,11},{10,... | collective-permute-start | bytes 196616 | tf_op jit(solution)/shard_map/ppermute | solution.py:391
  109.1 6.1 %collective-permute-start.28 = (f32[1,128]{1,0:T(1,128)S(1)}, f32[1,128]{1,0:T(1,128)S(1)}, u32[]{:S(2)}, u32[]{:S(2)}) collective-permute-start(f32[1,128]{1,0:T(1,128)S(1)} %get-tuple-element.211), channel_id=1, source_target_pairs={{0,1},{1,0},{2,3},{3,2},{4,5},{5,4},{6,7},{7,6},{8,9},{9,8},{10,11... | collective-permute-start | bytes 1544 | tf_op jit(solution)/shard_map/ppermute | solution.py:660

commit v2 on v1

--- a/solution.py
+++ b/solution.py
@@ -14,8 +14,13 @@
 SWAP = ((0, 1), (1, 0))
 GELU_C = math.sqrt(2.0 / math.pi)
 GELU_A = 0.044715
-CHUNKS = (512, 768, 768)
-COSTS = {}
+CHUNKS = (1024, 768, 256)
+FAR_FIRST = 2
+BACK = (3, 2, 0, 1)
+DIRECT = True
+JOIN = False
+PLAN = ('f', 'g0', 'g1', 'g2', 's', 'd0', 'd1', 'd2', 'e', 'r0', 'b0', 'r2', 'r1', 'r0', 'b1', 'l0', 'r1', 'r2', 'r0', 'r2', 'r1', 'l1', 'i')
+COSTS = (1, 1000000000, 4000000000, 1, 8000000000, 16000000000, 1, 1, 4000000000, 1, 1, 4000000000, 2000000000, 4000000000, 1000000000, 1, 1, 1000000000, 1, 1, 1, 1, 1)
 VMEM = pl.BlockSpec(memory_space=pltpu.VMEM)
 SMEM = pl.BlockSpec(memory_space=pltpu.SMEM)
 ANY = pl.BlockSpec(memory_space=pl.ANY)
@@ -31,10 +36,11 @@
     def __init__(self, limit):
         self.token = None
         self.limit = limit
-
-    def run(self, kernel, name, out_shape, args, scalars=(), far=(), scratch=(), keep=False, limit=None):
+        self.cost = 1
+
+    def run(self, kernel, name, out_shape, args, scalars=(), far=(), scratch=(), keep=False):
         specs = [SMEM] * len(scalars) + [HBM] * len(far) + [VMEM] * len(args)
-        args = [*scalars, *far, *args]
+        args = [*scalars, *(pltpu.with_memory_space_constraint(x, pltpu.HBM) for x in far), *args]
         used = len(args)
         aliases = {}
         if keep is not None and keep is not False:
@@ -58,8 +64,8 @@
             out_shape=(*out_shape, sds((8, 128), F32)),
             scratch_shapes=scratch,
             input_output_aliases=aliases,
-            compiler_params=pltpu.CompilerParams(vmem_limit_bytes=(limit or self.limit) * 2**20),
-            cost_estimate=pl.CostEstimate(flops=COSTS.get(name, 1), bytes_accessed=1, transcendentals=0),
+            compiler_params=pltpu.CompilerParams(vmem_limit_bytes=self.limit * 2**20),
+            cost_estimate=pl.CostEstimate(flops=self.cost, bytes_accessed=1, transcendentals=0),
         )(*args)
         return out
 
@@ -107,27 +113,22 @@
     return jnp.where(match, 1.0, 0.0)
 
 
-def outgoing_kernel(nodes, orders, place, feats, adj, send, recv, here, edges, send_row, recv_row, back_row, *rest):
-    outs, sems = rest[:-1], rest[-1]
+def outgoing_kernel(nodes, order, place, feats, send_far, here, *rest):
+    outs, (send, sems) = rest[:-2], rest[-2:]
     width = feats.shape[1]
     ranges = tiles(width, width // (sems.shape[0] - 1))
     copies = [pltpu.make_async_copy(feats.at[:, at], here.at[:, at], sems.at[i]) for i, at in enumerate(ranges)]
-    copies.append(pltpu.make_async_copy(adj, edges, sems.at[len(ranges)]))
-    for copy in copies:
+    fetch = pltpu.make_async_copy(send_far, send, sems.at[len(ranges)])
+    for copy in (fetch, *copies):
         copy.start()
-    me, part = place[0], place[1]
-    column = index_column(send, part, nodes, orders[0])
-    recv_row[...] = as_row(index_column(recv, part, nodes, orders[1]))
-    back_row[...] = as_row(index_column(recv, part, nodes, orders[2], me))
-    send_row[...] = as_row(index_column(send, part, nodes, orders[3], me))
-    hot = hot_cols(column, feats.shape[0]).astype(BF16)
+    fetch.wait()
+    hot = hot_cols(index_column(send, place[1], nodes, order), feats.shape[0]).astype(BF16)
     size = outs[0].shape[0]
     for at, copy in zip(ranges, copies):
         copy.wait()
         value = jnp.dot(hot, here[:, at], preferred_element_type=F32)
         for i, out in enumerate(outs):
             out[:, at] = value[i * size : (i + 1) * size].astype(BF16)
-    copies[-1].wait()
 
 
 def regroup_kernel(size, orders, *refs):
@@ -142,9 +143,21 @@
     return jnp.concatenate([piece[...] for piece in pieces], axis=0)
 
 
-def mix_kernel(weight, adj, recv_row, feats, mixed, mixed_t, ratio, ratio_row, adj_t, own, sem):
-    copy = pltpu.make_async_copy(weight, own, sem)
-    copy.start()
+def mix_kernel(orders, place, weight, edges, send_far, recv_far, feats, *refs):
+    mixed, mixed_t, ratio, ratio_row, adj_t, own, send_row, recv_row, back_row, adj, send, recv, sems = refs
+    copies = [
+        pltpu.make_async_copy(source, target, sems.at[i])
+        for i, (source, target) in enumerate(((recv_far, recv), (send_far, send), (edges, adj), (weight, own)))
+    ]
+    for copy in copies:
+        copy.start()
+    for copy in copies[:3]:
+        copy.wait()
+    me, part = place[0], place[1]
+    nodes = adj.shape[1]
+    recv_row[...] = as_row(index_column(recv, part, nodes, orders[1]))
+    back_row[...] = as_row(index_column(recv, part, nodes, orders[2], 0 if DIRECT else me))
+    send_row[...] = as_row(index_column(send, part, nodes, orders[3], 0 if DIRECT else me))
     batches, nodes, _ = adj.shape
     half = mixed.shape[2]
     eye = lax.broadcasted_iota(jnp.int32, (nodes, nodes), 0) == lax.broadcasted_iota(
@@ -166,7 +179,7 @@
             low = at.start % half
             mixed[at.start // half, here, low : low + at.stop - at.start] = value.astype(BF16)
             mixed_t[at, here] = value.T.astype(BF16)
-    copy.wait()
+    copies[3].wait()
 
 
 def pre_own_kernel(place, away, mixed, weight, pre, other, sem):
@@ -178,16 +191,10 @@
     copy.wait()
 
 
-def pre_other_kernel(place, before, mixed, weight, bias_own, bias_other, pre):
+def pre_other_kernel(place, before, mixed, weight, pre):
     me = place[0]
-    half = weight.shape[0]
-    first = me == 0
-    mine, theirs = bias_own[...].astype(F32), bias_other[...].astype(F32)
-    bias = (jnp.where(first, mine, theirs), jnp.where(first, theirs, mine))
     for at in tiles(pre.shape[1]):
-        total = before[:, at] + jnp.dot(mixed[1 - me], weight[:, at], preferred_element_type=F32)
-        low = at.start % half
-        pre[:, at] = total + bias[at.start // half][:, low : low + at.stop - at.start]
+        pre[:, at] = before[:, at] + jnp.dot(mixed[1 - me], weight[:, at], preferred_element_type=F32)
 
 
 def finish_kernel(axes, block, place, recv_row, ratio_row, mixed_t, *refs):
@@ -212,8 +219,8 @@
                 out[pl.ds(pl.multiple_of(spot * block, block), block)] = chosen[i].astype(BF16)
 
 
-def remote_kernel(place, own, other, *refs):
-    pieces, out = refs[:-1], refs[-1]
+def remote_kernel(place, own, other, bias_own, bias_other, *refs):
+    pieces, (out, bias) = refs[:-2], refs[-2:]
     half = own.shape[0]
     me = place[0]
     spots = out.shape[0] // 2
@@ -225,13 +232,16 @@
         high = product.astype(BF16)
         out[:spots, at] = high
         out[spots:, at] = (product - high.astype(F32)).astype(BF16)
-
-
-def gelu_kernel(start, recv_row, ratio, remote, pre, cot, act, dpre, bias_term, value, result, sems):
+    mine, theirs = bias_own[...].astype(F32), bias_other[...].astype(F32)
+    bias[:, :half] = jnp.where(me == 0, mine, theirs)
+    bias[:, half:] = jnp.where(me == 0, theirs, mine)
+
+
+def gelu_kernel(start, recv_row, ratio, remote, pre, bias, cot, act, dpre, bias_term, value, result, sems):
     rows, size = dpre.shape
     at = slice(start, start + size)
     hot = hot_rows(recv_row[...], rows).astype(BF16)
-    value[...] = pre[:, at] + ratio[...] * jnp.dot(
+    value[...] = pre[:, at] + bias[:, at] + ratio[...] * jnp.dot(
         jnp.concatenate([hot, hot], axis=1), remote[:, at], preferred_element_type=F32
     )
     step = 64
@@ -283,23 +293,21 @@
         out[low : low + count * block] = total.astype(BF16)
 
 
-def sent_kernel(chunks, parts, per_part, sources, place, recv_row, ratio_row, own, other, *refs):
+def sent_kernel(chunks, parts, per_part, sources, place, recv_row, ratio_row, *refs):
     dpres, bias_terms, outs = refs[:chunks], refs[chunks : 2 * chunks], refs[2 * chunks : -1]
     lines = refs[-1]
-    half, width = own.shape
+    width = lines.shape[1]
     rows = ratio_row.shape[1]
     hot = (hot_rows(recv_row[...], rows).T * ratio_row[0:1]).astype(BF16)
-    grad = jnp.concatenate(
-        [jnp.dot(hot, dpre[...], preferred_element_type=F32).astype(BF16) for dpre in dpres], axis=1
-    )
     me, part = place[0], place[1]
     size = outs[0].shape[0]
-    for weight, spot in ((own, me), (other, 1 - me)):
-        for at in tiles(half, 256):
-            value = lax.dot_general(grad, weight[at], NT, preferred_element_type=F32)
-            for i, out in enumerate(outs):
-                here = pl.ds(pl.multiple_of(spot * half + at.start, 256), 256)
-                out[:, here] = value[i * size : (i + 1) * size].astype(BF16)
+    start = 0
+    for dpre in dpres:
+        at = slice(start, start + dpre.shape[1])
+        value = jnp.dot(hot, dpre[...], preferred_element_type=F32)
+        for i, out in enumerate(outs):
+            out[:, at] = value[i * size : (i + 1) * size].astype(BF16)
+        start = at.stop
     bias = jnp.concatenate([term[...] for term in bias_terms], axis=1)
     high = bias.astype(BF16).astype(F32)
     middle = (bias - high).astype(BF16).astype(F32)
@@ -311,7 +319,7 @@
         pieces = []
         for source in sources[i]:
             if len(outs) > 1:
-                to = part ^ turn_digits(source, me)
+                to = part ^ turn_digits(source, 0 if DIRECT else me)
                 piece = lines[:, pl.ds(pl.multiple_of(to * count, count), count)]
             else:
                 piece = lines[:, source * count : (source + 1) * count]
@@ -345,33 +353,54 @@
             out[here, at] = jnp.dot(adj_t[batch], dtotal[here, at], preferred_element_type=F32)
 
 
-def input_kernel(place, send_row, own, other, *refs):
-    pieces, (out, bias_out) = refs[:-2], refs[-2:]
+def input_kernel(place, send_row, own, other, weight_own, weight_other, *refs):
+    pieces, (out, result, sems) = refs[:-3], refs[-3:]
     rows, half = own.shape
     hot = hot_rows(send_row[...], rows).astype(BF16)
+    grad = stack([piece.at[:, : 2 * half] for piece in pieces])
     me = place[0]
-    for partial, spot in ((own, me), (other, 1 - me)):
+    copies = []
+    for partial, weight, spot in ((own, weight_own, me), (other, weight_other, 1 - me)):
         for at in tiles(half):
             here = pl.ds(pl.multiple_of(spot * half + at.start, 512), at.stop - at.start)
-            total = partial[:, at] + jnp.dot(hot, stack([piece.at[:, here] for piece in pieces]), preferred_element_type=F32)
-            out[:, here] = total.astype(BF16)
-    bias_out[...] = sum(jnp.sum(piece[:, 2 * half :].astype(F32), axis=0, keepdims=True) for piece in pieces)
-
-
-def halve_kernel(keep, arrived, stay, leave):
+            returned = lax.dot_general(grad, weight[at], NT, preferred_element_type=F32).astype(BF16)
+            total = partial[:, at] + jnp.dot(hot, returned, preferred_element_type=F32)
+            i = len(copies)
+            result[i] = total.astype(BF16)
+            copies.append(pltpu.make_async_copy(result.at[i], out.at[:, here], sems.at[i]))
+            copies[-1].start()
+    for copy in copies:
+        copy.wait()
+
+
+def bias_kernel(*refs):
+    out = refs[-1]
+    width = refs[0].shape[1] - out.shape[1]
+    out[...] = sum(jnp.sum(piece[:, width:].astype(F32), axis=0, keepdims=True) for piece in refs[:-1])
+
+
+def halve_kernel(*refs):
+    pairs, (stay, leave) = refs[:-2], refs[-2:]
     half = stay.shape[0]
     for out, low in ((leave, half), (stay, 0)):
-        at = slice(low, low + half)
-        out[...] = (keep[at].astype(F32) + arrived[at].astype(F32)).astype(BF16)
-
-
-def last_kernel(*refs):
-    out = refs[-1]
+        here = slice(low, low + half)
+        start = 0
+        for keep, arrived in zip(pairs[::2], pairs[1::2]):
+            at = slice(start, start + keep.shape[1])
+            out[:, at] = (keep[here].astype(F32) + arrived[here].astype(F32)).astype(BF16)
+            start = at.stop
+
+
+def last_kernel(place, bias_mine, bias_theirs, *refs):
+    out, bias_out = refs[-2:]
     start = 0
-    for keep, arrived in zip(refs[:-1:2], refs[1:-1:2]):
+    for keep, arrived in zip(refs[:-2:2], refs[1:-2:2]):
         size = keep.shape[1]
         out[:, start : start + size] = keep[...].astype(F32) + arrived[...].astype(F32)
         start += size
+    bias = bias_mine[...] + bias_theirs[...]
+    count = bias_out.shape[1]
+    bias_out[...] = jnp.where(place[0] == 0, bias[:, :count], bias[:, count : 2 * count])
 
 
 def partners(parts, axis):
@@ -384,17 +413,22 @@
         self.order = order
         self.parts = parts
         self.axes = list(axes)
-        self.keep = keep
-        self.send(leave)
-
-    def send(self, leave):
-        self.arrived = lax.ppermute(leave, AXES, partners(self.parts, self.axes.pop(0)))
+        self.send(keep, leave)
+
+    def send(self, keep, leave):
+        self.pairs = [(keep, lax.ppermute(leave, AXES, partners(self.parts, self.axes.pop(0))))]
+
+    def join(self, other):
+        self.pairs = other.pairs + self.pairs
+        other.pairs = []
+
+    def flat(self):
+        return [x for pair in self.pairs for x in pair]
 
     def step(self):
-        rows, size = self.keep.shape
-        half = sds((rows // 2, size), BF16)
-        self.keep, leave = self.order.run(halve_kernel, "halve", (half, half), (self.keep, self.arrived))
-        self.send(leave)
+        rows = self.pairs[0][0].shape[0]
+        half = sds((rows // 2, sum(keep.shape[1] for keep, _ in self.pairs)), BF16)
+        self.send(*self.order.run(halve_kernel, "halve", (half, half), self.flat()))
 
 
 class Exchange:
@@ -442,19 +476,23 @@
     if paired:
         late = list(range(digits))
         early = late[2:] + late[:2]
-        back = late[:1:-1] + late[:2]
+        back = [axis for axis in BACK if axis < digits] + list(range(len(BACK), digits))
         first, last = halves(range(parts), back[0]), list(range(parts))
         for axis in back:
             last = sum(halves(last, axis), [])
-        orders = [list(range(parts)), [k * near + j for j in range(near) for k in range(far)], sum(first, []), last]
+        across = [k * near + j for j in range(near) for k in range(far)]
+        orders = [list(range(parts)), across, sum(first, []), last]
+        if DIRECT:
+            orders[2:] = [list(range(parts)), across]
+            first = [[k * near + j for j in range(near)] for k in range(far)]
     slots = send_index.size
     per_part = slots // parts
 
     def move(pieces, stride):
-        moved = [pieces[0]]
-        for i in range(1, len(pieces)):
+        moved = list(pieces)
+        for i in reversed(range(1, len(pieces))):
             perm = [(p, p ^ (i * stride)) for p in range(parts)]
-            moved.append(lax.ppermute(pieces[i], "parts", perm))
+            moved[i] = lax.ppermute(pieces[i], "parts", perm)
         return moved
 
     def exchange(values):
@@ -470,23 +508,23 @@
     run = order.run
     turn = (0, 1, 3, 2)
     pieces = far if paired else 1
-    row = sds((1, slots), jnp.int32)
-    feats, local_adj, send_row, recv_row, back_row, *outgoing = run(
-        functools.partial(outgoing_kernel, nodes, orders),
+    turned = jnp.transpose(send_index, turn), jnp.transpose(recv_target, turn)
+    indices = [pltpu.VMEM(x.shape, jnp.int32) for x in turned]
+    feats, *outgoing = run(
+        functools.partial(outgoing_kernel, nodes, orders[0]),
         "outgoing",
-        (sds((rows, width), BF16), sds(local_adj.shape, jnp.int32), row, row, row)
-        + (sds((slots // pieces, width), BF16),) * pieces,
-        (jnp.transpose(send_index, turn), jnp.transpose(recv_target, turn)),
+        (sds((rows, width), BF16),) + (sds((slots // pieces, width), BF16),) * pieces,
+        (),
         scalars=(place,),
-        far=(feats, local_adj),
-        scratch=[pltpu.SemaphoreType.DMA((5,))],
-        limit=47,
+        far=(feats, turned[0]),
+        scratch=[indices[0], pltpu.SemaphoreType.DMA((5,))],
     )
     if paired:
         outgoing = move(outgoing, near)
 
-    mixed, mixed_t, ratio, ratio_row, adj_t, weight = run(
-        mix_kernel,
+    row = sds((1, slots), jnp.int32)
+    mixed, mixed_t, ratio, ratio_row, adj_t, weight, send_row, recv_row, back_row = run(
+        functools.partial(mix_kernel, orders),
         "mix",
         (
             sds((2, rows, half), BF16),
@@ -495,11 +533,23 @@
             sds((8, rows), F32),
             sds((batches, nodes, nodes), BF16),
             sds(weight.shape, BF16),
+            row,
+            row,
+            row,
         ),
-        (local_adj, recv_row, feats),
-        far=(weight,),
+        (feats,),
+        scalars=(place,),
+        far=(weight, local_adj, *turned),
+        scratch=[pltpu.VMEM(local_adj.shape, jnp.int32), *indices, pltpu.SemaphoreType.DMA((4,))],
+    )
+    pre, other = run(
+        pre_own_kernel,
+        "pre_own",
+        (sds((rows, width), F32), sds(other.shape, BF16)),
+        (mixed, weight),
+        scalars=(place,),
+        far=(other,),
         scratch=[pltpu.SemaphoreType.DMA(())],
-        limit=36,
     )
     if paired:
         arrived = run(
@@ -513,33 +563,24 @@
         arrived = move(arrived, 1)
     else:
         arrived = [exchange(outgoing[0])]
-    pre, other = run(
-        pre_own_kernel,
-        "pre_own",
-        (sds((rows, width), F32), sds(other.shape, BF16)),
-        (mixed, weight),
-        scalars=(place,),
-        far=(other,),
-        scratch=[pltpu.SemaphoreType.DMA(())],
-    )
     (pre,) = run(
         pre_other_kernel,
         "pre_other",
         (sds((rows, width), F32),),
-        (pre, mixed, other, bias_own, bias_other),
+        (pre, mixed, other),
         scalars=(place,),
     )
-    (remote,) = run(
+    remote, bias_full = run(
         remote_kernel,
         "remote_product",
-        (sds((2 * slots, width), BF16),),
-        (weight, other, *arrived),
+        (sds((2 * slots, width), BF16), sds((1, width), F32)),
+        (weight, other, bias_own, bias_other, *arrived),
         scalars=(place,),
     )
 
     starts = [sum(CHUNKS[:i]) for i in range(len(CHUNKS))]
     act = None
-    dpres, dpres_other, bias_terms, sums = [], [], [], []
+    dpres, dpres_other, bias_terms, sums, dtotals, partials = [], [], [], [], [], []
 
     def gelu(i):
         nonlocal act
@@ -548,7 +589,7 @@
             functools.partial(gelu_kernel, starts[i]),
             "gelu",
             (sds((rows, width), BF16), sds((rows, size), BF16), sds((1, size), F32)),
-            (recv_row, ratio, remote, pre, cot),
+            (recv_row, ratio, remote, pre, bias_full, cot),
             scratch=[pltpu.VMEM((rows, size), F32), pltpu.VMEM((rows, size), BF16), pltpu.SemaphoreType.DMA((3,))],
             keep=act,
         )
@@ -556,11 +597,11 @@
         dpres_other.append(lax.ppermute(dpre, "mp", SWAP))
         bias_terms.append(bias_term)
 
-    def grad(i):
+    def grad(i, mine, theirs):
         size = CHUNKS[i]
         shape = sds((half // 2, size), BF16)
         if paired:
-            axes = early if i == 0 else late
+            axes = early if i == FAR_FIRST else late
             spots = [sum(((r >> axes[::-1].index(axis)) & 1) << d for d, axis in enumerate(late[::-1])) for r in range(parts)]
             size_of = block
         else:
@@ -577,89 +618,96 @@
         both = jnp.concatenate([keep, leave]).astype(F32)
         sums.append(lax.psum_scatter(both, "parts", scatter_dimension=0, tiled=True))
 
-    def step(i):
-        if paired:
-            sums[i].step()
-
-    def back_half(matrix):
-        (dtotal,) = run(back_kernel_of, "back", (sds((rows, half), BF16),), (ratio, matrix, *dpres))
-        return dtotal
-
-    def around(dtotal):
-        (partial,) = run(local_kernel, "input_local", (sds((rows, half), F32),), (adj_t, dtotal))
-        return partial
-
-    back_kernel_of = functools.partial(back_kernel, len(CHUNKS))
-
-    mine, theirs = run(
-        functools.partial(finish_kernel, late, block),
-        "finish_mixed",
-        (sds((half, rows), BF16), sds((half, rows), BF16)),
-        (recv_row, ratio_row, mixed_t, *arrived),
-        scalars=(place,),
-    )
-    theirs = lax.ppermute(theirs, "mp", SWAP)
-    for i in range(len(CHUNKS)):
-        gelu(i)
-    grad(0)
-    grad(1)
-
     extra = max(128, width // parts)
-    pieces = 2 if paired else 1
-    sent = run(
-        functools.partial(
-            sent_kernel, len(CHUNKS), parts, per_part, first if paired else [list(range(parts))]
-        ),
-        "sent_grads",
-        (sds((slots // pieces, width + extra), BF16),) * pieces,
-        (back_row, ratio_row, weight, other, *dpres, *bias_terms),
-        scalars=(place,),
-        scratch=[pltpu.VMEM((8, width), F32)],
-    )
+    pieces = (far if DIRECT else 2) if paired else 1
+    for step, cost in zip(PLAN, COSTS):
+        kind, number = step[0], int(step[1:] or 0)
+        order.cost = cost
+        if kind == "g":
+            gelu(number)
+        elif kind == "f":
+            mine, theirs = run(
+                functools.partial(finish_kernel, late, block),
+                "finish_mixed",
+                (sds((half, rows), BF16), sds((half, rows), BF16)),
+                (recv_row, ratio_row, mixed_t, *arrived),
+                scalars=(place,),
+            )
+            theirs = lax.ppermute(theirs, "mp", SWAP)
+        elif kind == "d":
+            grad(number, mine, theirs)
+        elif kind == "s":
+            sent = run(
+                functools.partial(
+                    sent_kernel, len(CHUNKS), parts, per_part, first if paired else [list(range(parts))]
+                ),
+                "sent_grads",
+                (sds((slots // pieces, width + extra), BF16),) * pieces,
+                (back_row, ratio_row, *dpres, *bias_terms),
+                scalars=(place,),
+                scratch=[pltpu.VMEM((8, width), F32)],
+            )
+            if paired:
+                swap = move(sent, near) if DIRECT else Exchange(order, parts, back, per_part, sent)
+            else:
+                returned = [exchange(sent[0])]
+        elif kind == "b":
+            (dtotal,) = run(
+                functools.partial(back_kernel, len(CHUNKS)),
+                "back",
+                (sds((rows, half), BF16),),
+                (ratio, (weight, other)[number], *dpres),
+            )
+            dtotals.append(dtotal)
+        elif kind == "l":
+            (partial,) = run(local_kernel, "input_local", (sds((rows, half), F32),), (adj_t, dtotals[number]))
+            partials.append(partial)
+        elif kind == "i":
+            if paired:
+                returned = swap if DIRECT else [swap.stay, swap.arrived]
+            (bias_mine,) = run(bias_kernel, "bias_sum", (sds((1, extra), F32),), returned)
+            bias_theirs = lax.ppermute(bias_mine, "mp", SWAP)
+            size = min(512, half)
+            (input_grad,) = run(
+                input_kernel,
+                "input_gradient",
+                (sds((rows, width), BF16),),
+                (send_row, *partials, weight, other, *returned),
+                scalars=(place,),
+                scratch=[pltpu.VMEM((width // size, rows, size), BF16), pltpu.SemaphoreType.DMA((width // size,))],
+                keep=None,
+            )
+        elif paired and kind == "r":
+            if JOIN and number == 1 and len(sums[1].axes) == digits - 2:
+                sums[1].join(sums[0])
+            sums[number].step()
+        elif paired and kind == "e":
+            if DIRECT:
+                swap = move(
+                    run(
+                        functools.partial(regroup_kernel, per_part, [[(k, j) for k in range(far)] for j in range(near)]),
+                        "regroup",
+                        (sds((far * per_part, width + extra), BF16),) * near,
+                        swap,
+                    ),
+                    1,
+                )
+            else:
+                swap.step()
+    count = width // (2 * parts)
     if paired:
-        swap = Exchange(order, parts, back, per_part, sent)
-    else:
-        returned = [exchange(sent[0])]
-
-    def pass_on():
-        if paired:
-            swap.step()
-
-    grad(2)
-    step(0)
-    step(1)
-    pass_on()
-    dtotal_own = back_half(weight)
-    step(2)
-    dtotal_other = back_half(other)
-    step(0)
-    step(1)
-    pass_on()
-    partial_own = around(dtotal_own)
-    step(2)
-    partial_other = around(dtotal_other)
-    step(0)
-    step(1)
-    pass_on()
-    step(2)
-    if paired:
-        returned = [swap.stay, swap.arrived]
-    input_grad, bias_all = run(
-        input_kernel,
-        "input_gradient",
-        (sds((rows, width), BF16), sds((1, extra), F32)),
-        (send_row, partial_own, partial_other, *returned),
-        scalars=(place,),
-    )
-    if paired:
-        (weight_grad,) = run(
-            last_kernel, "last_sum", (sds((block, width), F32),), [x for s in sums for x in (s.keep, s.arrived)]
+        weight_grad, bias_grad = run(
+            last_kernel,
+            "last_sum",
+            (sds((block, width), F32), sds((1, count), F32)),
+            [bias_mine, bias_theirs] + sum((s.flat() for s in sums), []),
+            scalars=(place,),
         )
+        bias_grad = bias_grad.reshape(count)
     else:
         weight_grad = jnp.concatenate(sums, axis=1)
-    bias_all = bias_all + lax.ppermute(bias_all, "mp", SWAP)
-    count = width // (2 * parts)
-    bias_grad = jnp.where(core == 0, bias_all[0, :count], bias_all[0, count : 2 * count])
+        bias_all = (bias_mine + bias_theirs)[0]
+        bias_grad = jnp.where(core == 0, bias_all[:count], bias_all[count : 2 * count])
     return (
         act.reshape(batches, nodes, width),
         input_grad.reshape(batches, nodes, width),

time: 116 us -> 102 us (0.88)
  waiting for transfers between devices: 28.2 us -> 9.84 us
  starting transfers between devices: 33.2 us -> 39.2 us
  local copies, waits for them, and re-layouts: 2.66 us -> 0.02 us
  Pallas kernels: 50.2 us -> 51.8 us
    ppermute x12, waiting for transfers between devices: 12.5 us -> 4.29 us  [send(): lax.ppermute(leave, AXES, partners(self.parts, self.axes.pop(0)))]
    ppermute x11 -> x13, waiting for transfers between devices: 12.2 us -> 5.54 us  [the longest x12 5.53 us: move(): moved[i] = lax.ppermute(pieces[i], 'parts', perm)]
    ppermute x3, waiting for transfers between devices: 3.47 us -> 0.01 us  [gelu(): dpres_other.append(lax.ppermute(dpre, 'mp', SWAP))]
    ppermute x11 -> x13, starting transfers between devices: 16.4 us -> 19.2 us  [the longest x12 15.3 us: move(): moved[i] = lax.ppermute(pieces[i], 'parts', perm)]
    unnamed x10 -> x4, local copies, waits for them, and re-layouts: 2.65 us -> 0.01 us
    ppermute x12, starting transfers between devices: 12.8 us -> 15 us  [send(): lax.ppermute(leave, AXES, partners(self.parts, self.axes.pop(0)))]
    pallas_call x32 -> x31, Pallas kernels: 50.2 us -> 51.8 us  [run(): pl.pallas_call(body, name=name, in_specs=specs, out_specs=(VMEM if keep i...]
    ppermute x1, starting transfers between devices: 0.09 us -> 1.62 us  [local(): theirs = lax.ppermute(theirs, 'mp', SWAP)]
  transfers between devices with their start and end apart: 29 -> 31, of which waited for: 9 -> 4; matrix products, arithmetic and copies ran while one was open for 0% -> 0% of each run, Pallas kernels for 40% -> 46%
where the time goes in v2:
time: 102 us
  Pallas kernels  51.8 us (51%)
  starting transfers between devices  39.2 us (38%)
  waiting for transfers between devices  9.84 us (10%)
  between operations  1.02 us (1%)
    pallas_call x31, Pallas kernels, run(): pl.pallas_call(body, name=name, in_specs=specs, out_specs=(VMEM if keep i...  51.8 us
    ppermute x12, starting transfers between devices, move(): moved[i] = lax.ppermute(pieces[i], 'parts', perm)  15.3 us
    ppermute x12, starting transfers between devices, send(): lax.ppermute(leave, AXES, partners(self.parts, self.axes.pop(0)))  15 us
    ppermute x12, waiting for transfers between devices, move(): moved[i] = lax.ppermute(pieces[i], 'parts', perm)  5.53 us
    ppermute x12, waiting for transfers between devices, send(): lax.ppermute(leave, AXES, partners(self.parts, self.axes.pop(0)))  4.29 us
    ppermute x1, starting transfers between devices, local(): bias_theirs = lax.ppermute(bias_mine, 'mp', SWAP)  3.88 us
    ppermute x1, starting transfers between devices, local(): bias_other = lax.ppermute(bias_own, 'mp', SWAP)  2.6 us
  transfers between devices with their start and end apart: 31, of which 4 were waited for; matrix products, arithmetic and copies ran while one was open for 0% of the time, Pallas kernels for 46%

profile of v2, /device:TPU:1, one launch (start us, length us, event | category | flops | bytes accessed | tf_op | source)
XLA Modules:
  0.0 101.9 jit_solution(1541038620304411387)
XLA Ops:
  0.8 2.8 %outgoing.1 = (bf16[768,2048]{1,0:T(8,128)(2,1)S(1)}, bf16[32,2048]{1,0:T(8,128)(2,1)S(1)}, bf16[32,2048]{1,0:T(8,128)(2,1)S(1)}, bf16[32,2048]{1,0:T(8,128)(2,1...) custom-call(s32[2]{0:T(128)S(1)} %pad_add_fusion.refs_0_, bf16[768,2048]{1,0:T(8,128)(2,1)} %bitcast.12, ...), custom_call_target="tpu_custom_call" | custom-call | flops 1 | bytes 1 | tf_op jit(solution)/shard_map/outgoing/pallas_call | solution.py:59
  3.7 2.8 %collective-permute-start.2 = (bf16[32,2048]{1,0:T(8,128)(2,1)S(1)}, bf16[32,2048]{1,0:T(8,128)(2,1)S(1)}, u32[]{:S(2)}, u32[]{:S(2)}) collective-permute-start(bf16[32,2048]{1,0:T(8,128)(2,1)S(1)} %get-tuple-element.117), channel_id=1, source_target_pairs={{0,8},{2,10},{4,12},{6,14},{8,0},{10,2},{12,4},{14,6},{16,24},{18,... | collective-permute-start | bytes 393224 | tf_op jit(solution)/shard_map/ppermute | solution.py:495
  6.5 2.3 %collective-permute-start.3 = (bf16[32,2048]{1,0:T(8,128)(2,1)S(1)}, bf16[32,2048]{1,0:T(8,128)(2,1)S(1)}, u32[]{:S(2)}, u32[]{:S(2)}) collective-permute-start(bf16[32,2048]{1,0:T(8,128)(2,1)S(1)} %get-tuple-element.118), channel_id=1, source_target_pairs={{0,16},{2,18},{4,20},{6,22},{8,24},{10,26},{12,28},{14,30},{16,0},... | collective-permute-start | bytes 393224 | tf_op jit(solution)/shard_map/ppermute | solution.py:495
  8.8 4.0 %mix.1 = (bf16[2,768,1024]{2,1,0:T(8,128)(2,1)S(1)}, bf16[2048,768]{1,0:T(8,128)(2,1)S(1)}, f32[768,1]{1,0:T(8,128)S(1)}, f32[8,768]{1,0:T(8,128)S(1)}, bf16[2,3...) custom-call(s32[2]{0:T(128)S(1)} %pad_add_fusion.refs_0_, ...), custom_call_target="tpu_custom_call" | custom-call | flops 1 | bytes 1 | tf_op jit(solution)/shard_map/mix/pallas_call | solution.py:59
  12.8 4.0 %pre_own.1 = (f32[768,2048]{1,0:T(8,128)S(1)}, bf16[1024,2048]{1,0:T(8,128)(2,1)S(1)}, f32[8,128]{1,0:T(8,128)S(1)}) custom-call(s32[2]{0:T(128)S(1)} %pad_add_fusion.refs_0_, bf16[1024,2048]{1,0:T(8,128)(2,1)} %collective-permute-done.refs_1_, bf16[2,768,1024]{2,1,0:T(8,128)(2,1)S(1)} %get-tuple-element.113.refs_2_, ...), custom_call_target="tpu_custom_call" | custom-call | flops 1 | bytes 1 | tf_op jit(solution)/shard_map/pre_own/pallas_call | solution.py:59
  16.8 1.2 %collective-permute-done.4.refs_3_ = bf16[32,2048]{1,0:T(8,128)(2,1)S(1)} collective-permute-done((bf16[32,2048]{1,0:T(8,128)(2,1)S(1)}, bf16[32,2048]{1,0:T(8,128)(2,1)S(1)}, u32[]{:S(2)}, u32[]{:S(2)}) %collective-permute-start.4) | collective-permute-done | bytes 131104 | tf_op jit(solution)/shard_map/ppermute | solution.py:495
  18.0 1.3 %collective-permute-start.5 = (bf16[32,2048]{1,0:T(8,128)(2,1)S(1)}, bf16[32,2048]{1,0:T(8,128)(2,1)S(1)}, u32[]{:S(2)}, u32[]{:S(2)}) collective-permute-start(bf16[32,2048]{1,0:T(8,128)(2,1)S(1)} %get-tuple-element.122), channel_id=1, source_target_pairs={{0,2},{2,0},{4,6},{6,4},{8,10},{10,8},{12,14},{14,12},{16,18},{18,... | collective-permute-start | bytes 393224 | tf_op jit(solution)/shard_map/ppermute | solution.py:495
  19.3 1.2 %collective-permute-start.6 = (bf16[32,2048]{1,0:T(8,128)(2,1)S(1)}, bf16[32,2048]{1,0:T(8,128)(2,1)S(1)}, u32[]{:S(2)}, u32[]{:S(2)}) collective-permute-start(bf16[32,2048]{1,0:T(8,128)(2,1)S(1)} %get-tuple-element.123), channel_id=1, source_target_pairs={{0,4},{2,6},{4,0},{6,2},{8,12},{10,14},{12,8},{14,10},{16,20},{18,... | collective-permute-start | bytes 393224 | tf_op jit(solution)/shard_map/ppermute | solution.py:495
  20.8 2.6 %collective-permute-start.1 = (bf16[1,1024]{1,0:T(2,128)(2,1)S(1)}, bf16[1,1024]{1,0:T(2,128)(2,1)S(1)}, u32[]{:S(2)}, u32[]{:S(2)}) collective-permute-start(bf16[1,1024]{1,0:T(2,128)(2,1)S(1)} %reshape.27.refs_3_), channel_id=1, source_target_pairs={{0,1},{1,0},{2,3},{3,2},{4,5},{5,4},{6,7},{7,6},{8,9},{9,8},{10,11... | collective-permute-start | bytes 6152 | tf_op jit(solution)/shard_map/ppermute | solution.py:506
  23.4 3.9 %pre_other.1 = (f32[768,2048]{1,0:T(8,128)S(1)}, f32[8,128]{1,0:T(8,128)S(1)}) custom-call(s32[2]{0:T(128)S(1)} %pad_add_fusion.refs_0_, f32[768,2048]{1,0:T(8,128)S(1)} %get-tuple-element.125.refs_1_, bf16[2,768,1024]{2,1,0:T(8,128)(2,1)S(1)} %get-tuple-element.113.refs_2_, bf16[1024,2048]{1,0:T(8,128)(2,1)S(1)} %get-tuple-element.115.refs_3_.refs_2_.refs_1_.refs_5_, ...), custom_call_target="tpu_custom_call" | custom-call | flops 1 | bytes 1 | tf_op jit(solution)/shard_map/pre_other/pallas_call | solution.py:59
  27.4 1.9 %remote_product.1 = (bf16[256,2048]{1,0:T(8,128)(2,1)S(1)}, f32[1,2048]{1,0:T(1,128)S(1)}, f32[8,128]{1,0:T(8,128)S(1)}) custom-call(s32[2]{0:T(128)S(1)} %pad_add_fusion.refs_0_, bf16[1024,2048]{1,0:T(8,128)(2,1)S(1)} %get-tuple-element.112.refs_3_.refs_1_.refs_4_, bf16[1024,2048]{1,0:T(8,128)(2,1)S(1)} %get-tuple-element.115.refs_3_.refs_2_.refs_1_.refs_5_, ...), custom_call_target="tpu_custom_call" | custom-call | flops 1 | bytes 1 | tf_op jit(solution)/shard_map/remote_product/pallas_call | solution.py:59
  29.3 1.9 %finish_mixed.1 = (bf16[1024,768]{1,0:T(8,128)(2,1)S(1)}, bf16[1024,768]{1,0:T(8,128)(2,1)S(1)}, f32[8,128]{1,0:T(8,128)S(1)}) custom-call(s32[2]{0:T(128)S(1)} %pad_add_fusion.refs_0_, s32[1,128]{1,0:T(1,128)S(1)} %get-tuple-element.110.refs_1_.refs_0_, f32[8,768]{1,0:T(8,128)S(1)} %get-tuple-element.131.refs_2_, ...), custom_call_target="tpu_custom_call" | custom-call | flops 1 | bytes 1 | tf_op jit(solution)/shard_map/finish_mixed/pallas_call | solution.py:59
  31.1 1.6 %collective-permute-start.8 = (bf16[1024,768]{1,0:T(8,128)(2,1)S(1)}, bf16[1024,768]{1,0:T(8,128)(2,1)S(1)}, u32[]{:S(2)}, u32[]{:S(2)}) collective-permute-start(bf16[1024,768]{1,0:T(8,128)(2,1)S(1)} %get-tuple-element.146), channel_id=1, source_target_pairs={{0,1},{1,0},{2,3},{3,2},{4,5},{5,4},{6,7},{7,6},{8,9},{9,8},{10,11... | collective-permute-start | bytes 4718600 | tf_op jit(solution)/shard_map/ppermute | solution.py:636
  32.8 3.5 %gelu.3 = (bf16[768,2048]{1,0:T(8,128)(2,1)}, bf16[768,1024]{1,0:T(8,128)(2,1)S(1)}, f32[1,1024]{1,0:T(1,128)S(1)}, f32[8,128]{1,0:T(8,128)S(1)}) custom-call(s32[1,128]{1,0:T(1,128)S(1)} %get-tuple-element.110.refs_1_.refs_0_, f32[768,1]{1,0:T(8,128)S(1)} %get-tuple-element.111.refs_1_.refs_0_, bf16[256,2048]{1,0:T(8,128)(2,1)S(1)} %get-tuple-element.128.refs_2_, ...), custom_call_target="tpu_custom_call" | custom-call | flops 1000000000 | bytes 1 | tf_op jit(solution)/shard_map/gelu/pallas_call | solution.py:59
  36.4 2.9 %gelu.4 = (bf16[768,2048]{1,0:T(8,128)(2,1)}, bf16[768,768]{1,0:T(8,128)(2,1)S(1)}, f32[1,768]{1,0:T(1,128)S(1)}, f32[8,128]{1,0:T(8,128)S(1)}) custom-call(s32[1,128]{1,0:T(1,128)S(1)} %get-tuple-element.110.refs_1_.refs_0_, f32[768,1]{1,0:T(8,128)S(1)} %get-tuple-element.111.refs_1_.refs_0_, ...), custom_call_target="tpu_custom_call", output_to_operand_aliasing={{0}: (6, {})} | custom-call | flops 4000000000 | bytes 1 | tf_op jit(solution)/shard_map/gelu/pallas_call | solution.py:59
  39.3 0.6 collective-permute-start.15
  39.8 1.5 %gelu.5 = (bf16[768,2048]{1,0:T(8,128)(2,1)}, bf16[768,256]{1,0:T(8,128)(2,1)S(1)}, f32[1,256]{1,0:T(1,128)S(1)}, f32[8,128]{1,0:T(8,128)S(1)}) custom-call(s32[1,128]{1,0:T(1,128)S(1)} %get-tuple-element.110.refs_1_.refs_0_, f32[768,1]{1,0:T(8,128)S(1)} %get-tuple-element.111.refs_1_.refs_0_, ...), custom_call_target="tpu_custom_call", output_to_operand_aliasing={{0}: (6, {})} | custom-call | flops 1 | bytes 1 | tf_op jit(solution)/shard_map/gelu/pallas_call | solution.py:59
  41.3 1.2 %sent_grads.1 = (bf16[32,2176]{1,0:T(8,128)(2,1)S(1)}, bf16[32,2176]{1,0:T(8,128)(2,1)S(1)}, bf16[32,2176]{1,0:T(8,128)(2,1)S(1)}, bf16[32,2176]{1,0:T(8,128)(2,1)S(1)}, f32[8,128]{1,0:T(8,128)S(1)}) custom-call(s32[2]{0:T(128)S(1)} %pad_add_fusion.refs_0_, s32[1,128]{1,0:T(1,128)S(1)} %get-tuple-element.147.refs_1_, ...), custom_call_target="tpu_custom_call" | custom-call | flops 8000000000 | bytes 1 | tf_op jit(solution)/shard_map/sent_grads/pallas_call | solution.py:59
  42.5 3.5 %grad.3 = (bf16[512,1024]{1,0:T(8,128)(2,1)S(1)}, bf16[512,1024]{1,0:T(8,128)(2,1)S(1)}, f32[8,128]{1,0:T(8,128)S(1)}) custom-call(bf16[1024,768]{1,0:T(8,128)(2,1)S(1)} %get-tuple-element.145.refs_0_, bf16[1024,768]{1,0:T(8,128)(2,1)S(1)} %collective-permute-done.8.refs_1_, bf16[768,1024]{1,0:T(8,128)(2,1)S(1)} %get-tuple-element.142.refs_3_.refs_2_, ...), custom_call_target="tpu_custom_call" | custom-call | flops 16000000000 | bytes 1 | tf_op jit(solution)/shard_map/grad/pallas_call | solution.py:59
  46.1 0.8 collective-permute-start.10
  46.8 2.6 %collective-permute-start.11 = (bf16[32,2176]{1,0:T(8,128)(2,1)S(1)}, bf16[32,2176]{1,0:T(8,128)(2,1)S(1)}, u32[]{:S(2)}, u32[]{:S(2)}) collective-permute-start(bf16[32,2176]{1,0:T(8,128)(2,1)S(1)} %get-tuple-element.156), channel_id=1, source_target_pairs={{0,8},{2,10},{4,12},{6,14},{8,0},{10,2},{12,4},{14,6},{16,24},{18,... | collective-permute-start | bytes 417800 | tf_op jit(solution)/shard_map/ppermute | solution.py:495
  49.5 1.0 collective-permute-start.12
  50.5 1.2 %collective-permute-start.13 = (bf16[32,2176]{1,0:T(8,128)(2,1)S(1)}, bf16[32,2176]{1,0:T(8,128)(2,1)S(1)}, u32[]{:S(2)}, u32[]{:S(2)}) collective-permute-start(bf16[32,2176]{1,0:T(8,128)(2,1)S(1)} %get-tuple-element.158), channel_id=1, source_target_pairs={{0,24},{2,26},{4,28},{6,30},{8,16},{10,18},{12,20},{14,22},{16,8},... | collective-permute-start | bytes 417800 | tf_op jit(solution)/shard_map/ppermute | solution.py:495
  51.7 2.7 %grad.4 = (bf16[512,768]{1,0:T(8,128)(2,1)S(1)}, bf16[512,768]{1,0:T(8,128)(2,1)S(1)}, f32[8,128]{1,0:T(8,128)S(1)}) custom-call(bf16[1024,768]{1,0:T(8,128)(2,1)S(1)} %get-tuple-element.145.refs_0_, bf16[1024,768]{1,0:T(8,128)(2,1)S(1)} %collective-permute-done.8.refs_1_, bf16[768,768]{1,0:T(8,128)(2,1)S(1)} %get-tuple-element.143.refs_4_.refs_2_.refs_3_, ...), custom_call_target="tpu_custom_call" | custom-call | flops 1 | bytes 1 | tf_op jit(solution)/shard_map/grad/pallas_call | solution.py:59
  54.4 0.8 collective-permute-start.17
  55.1 1.0 grad.5
  56.1 0.5 collective-permute-start.18
  56.6 4.3 %collective-permute-done.13.refs_3_ = bf16[32,2176]{1,0:T(8,128)(2,1)S(1)} collective-permute-done((bf16[32,2176]{1,0:T(8,128)(2,1)S(1)}, bf16[32,2176]{1,0:T(8,128)(2,1)S(1)}, u32[]{:S(2)}, u32[]{:S(2)}) %collective-permute-start.13) | collective-permute-done | bytes 139296 | tf_op jit(solution)/shard_map/ppermute | solution.py:495
  61.0 0.2 halve.9
  61.3 1.6 %collective-permute-start.16 = (bf16[256,1024]{1,0:T(8,128)(2,1)S(1)}, bf16[256,1024]{1,0:T(8,128)(2,1)S(1)}, u32[]{:S(2)}, u32[]{:S(2)}) collective-permute-start(bf16[256,1024]{1,0:T(8,128)(2,1)S(1)} %get-tuple-element.166), channel_id=1, source_target_pairs={{0,4},{1,3},{2,6},{3,1},{4,0},{5,7},{6,2},{7,5},{8,12},{9,11},{10,... | collective-permute-start | bytes 1572872 | tf_op jit(solution)/shard_map/ppermute | solution.py:419
  62.9 3.5 %back.2 = (bf16[768,1024]{1,0:T(8,128)(2,1)S(1)}, f32[8,128]{1,0:T(8,128)S(1)}) custom-call(f32[768,1]{1,0:T(8,128)S(1)} %get-tuple-element.111.refs_1_.refs_0_, bf16[1024,2048]{1,0:T(8,128)(2,1)S(1)} %get-tuple-element.112.refs_3_.refs_1_.refs_4_, bf16[768,1024]{1,0:T(8,128)(2,1)S(1)} %get-tuple-element.142.refs_3_.refs_2_, ...), custom_call_target="tpu_custom_call" | custom-call | flops 1 | bytes 1 | tf_op jit(solution)/shard_map/back/pallas_call | solution.py:59
  66.3 0.7 collective-permute-done.18.refs_1_
  67.1 3.5 %collective-permute-start.21 = (bf16[256,256]{1,0:T(8,128)(2,1)S(1)}, bf16[256,256]{1,0:T(8,128)(2,1)S(1)}, u32[]{:S(2)}, u32[]{:S(2)}) collective-permute-start(bf16[256,256]{1,0:T(8,128)(2,1)S(1)} %get-tuple-element.184), channel_id=1, source_target_pairs={{0,16},{1,17},{2,18},{3,19},{4,20},{5,21},{6,22},{7,23},{8,24},{9,... | collective-permute-start | bytes 393224 | tf_op jit(solution)/shard_map/ppermute | solution.py:419
  71.0 3.6 %collective-permute-done.16.refs_1_ = bf16[256,1024]{1,0:T(8,128)(2,1)S(1)} collective-permute-done((bf16[256,1024]{1,0:T(8,128)(2,1)S(1)}, bf16[256,1024]{1,0:T(8,128)(2,1)S(1)}, u32[]{:S(2)}, u32[]{:S(2)}) %collective-permute-start.16) | collective-permute-done | bytes 524320 | tf_op jit(solution)/shard_map/ppermute | solution.py:419
  74.7 2.3 %collective-permute-start.23 = (bf16[128,1024]{1,0:T(8,128)(2,1)S(1)}, bf16[128,1024]{1,0:T(8,128)(2,1)S(1)}, u32[]{:S(2)}, u32[]{:S(2)}) collective-permute-start(bf16[128,1024]{1,0:T(8,128)(2,1)S(1)} %get-tuple-element.189), channel_id=1, source_target_pairs={{0,8},{1,9},{2,10},{3,11},{4,12},{5,13},{6,14},{7,15},{8,0},{9,1},... | collective-permute-start | bytes 786440 | tf_op jit(solution)/shard_map/ppermute | solution.py:419
  77.0 3.7 %back.3 = (bf16[768,1024]{1,0:T(8,128)(2,1)S(1)}, f32[8,128]{1,0:T(8,128)S(1)}) custom-call(f32[768,1]{1,0:T(8,128)S(1)} %get-tuple-element.111.refs_1_.refs_0_, bf16[1024,2048]{1,0:T(8,128)(2,1)S(1)} %get-tuple-element.115.refs_3_.refs_2_.refs_1_.refs_5_, bf16[768,1024]{1,0:T(8,128)(2,1)S(1)} %get-tuple-element.142.refs_3_.refs_2_, ...), custom_call_target="tpu_custom_call" | custom-call | flops 1000000000 | bytes 1 | tf_op jit(solution)/shard_map/back/pallas_call | solution.py:59
  80.7 1.0 input_local.2
  81.9 0.9 collective-permute-start.22
  82.8 0.4 collective-permute-start.24
  83.2 0.8 collective-permute-start.25
  84.0 1.5 %collective-permute-start.26 = (bf16[32,2176]{1,0:T(8,128)(2,1)S(1)}, bf16[32,2176]{1,0:T(8,128)(2,1)S(1)}, u32[]{:S(2)}, u32[]{:S(2)}) collective-permute-start(bf16[32,2176]{1,0:T(8,128)(2,1)S(1)} %get-tuple-element.198), channel_id=1, source_target_pairs={{0,6},{2,4},{4,2},{6,0},{8,14},{10,12},{12,10},{14,8},{16,22},{18,... | collective-permute-start | bytes 417800 | tf_op jit(solution)/shard_map/ppermute | solution.py:495
  85.6 2.5 %collective-permute-start.28 = (bf16[64,1024]{1,0:T(8,128)(2,1)S(1)}, bf16[64,1024]{1,0:T(8,128)(2,1)S(1)}, u32[]{:S(2)}, u32[]{:S(2)}) collective-permute-start(bf16[64,1024]{1,0:T(8,128)(2,1)S(1)} %get-tuple-element.204), channel_id=1, source_target_pairs={{0,16},{1,17},{2,18},{3,19},{4,20},{5,21},{6,22},{7,23},{8,24},{9,... | collective-permute-start | bytes 393224 | tf_op jit(solution)/shard_map/ppermute | solution.py:419
  88.2 0.5 collective-permute-start.29
  88.7 1.3 %collective-permute-start.30 = (bf16[64,256]{1,0:T(8,128)(2,1)S(1)}, bf16[64,256]{1,0:T(8,128)(2,1)S(1)}, u32[]{:S(2)}, u32[]{:S(2)}) collective-permute-start(bf16[64,256]{1,0:T(8,128)(2,1)S(1)} %get-tuple-element.208), channel_id=1, source_target_pairs={{0,4},{1,3},{2,6},{3,1},{4,0},{5,7},{6,2},{7,5},{8,12},{9,11},{10,... | collective-permute-start | bytes 98312 | tf_op jit(solution)/shard_map/ppermute | solution.py:419
  90.0 1.0 input_local.3
  91.0 3.9 %collective-permute-start.27 = (f32[1,128]{1,0:T(1,128)S(1)}, f32[1,128]{1,0:T(1,128)S(1)}, u32[]{:S(2)}, u32[]{:S(2)}) collective-permute-start(f32[1,128]{1,0:T(1,128)S(1)} %get-tuple-element.202.refs_1_), channel_id=1, source_target_pairs={{0,1},{1,0},{2,3},{3,2},{4,5},{5,4},{6,7},{7,6},{8,9},{9,8},{10,11... | collective-permute-start | bytes 1544 | tf_op jit(solution)/shard_map/ppermute | solution.py:669
  94.9 5.6 %input_gradient.1 = (bf16[768,2048]{1,0:T(8,128)(2,1)}, f32[8,128]{1,0:T(8,128)S(1)}) custom-call(s32[2]{0:T(128)S(1)} %pad_add_fusion.refs_0_, s32[1,128]{1,0:T(1,128)S(1)} %get-tuple-element.140.refs_1_, f32[768,1024]{1,0:T(8,128)S(1)} %get-tuple-element.176.refs_2_, f32[768,1024]{1,0:T(8,128)S(1)} %get-tuple-element.194.refs_3_, ...), custom_call_target="tpu_custom_call" | custom-call | flops 1 | bytes 1 | tf_op jit(solution)/shard_map/input_gradient/pallas_call | solution.py:59
  100.5 1.4 %last_sum.1 = (f32[64,2048]{1,0:T(8,128)}, f32[1,64]{1,0:T(1,128)}, f32[8,128]{1,0:T(8,128)}) custom-call(s32[2]{0:T(128)S(1)} %pad_add_fusion.refs_0_, f32[1,128]{1,0:T(1,128)S(1)} %get-tuple-element.202.refs_1_, f32[1,128]{1,0:T(1,128)S(1)} %collective-permute-done.27.refs_2_, bf16[64,1024]{1,0:T(8,128)(2,1)S(1)} %get-tuple-element.203.refs_3_, ...), custom_call_target="tpu_custom_call" | custom-call | flops 1 | bytes 1 | tf_op jit(solution)/shard_map/last_sum/pallas_call | solution.py:59
  (51 shorter events, 1.6 us)
Async XLA Ops:
  0.6 12.2 %collective-permute-start = (bf16[1024,2048]{1,0:T(8,128)(2,1)}, bf16[1024,2048]{1,0:T(8,128)(2,1)}, u32[]{:S(2)}, u32[]{:S(2)}) collective-permute-start(bf16[1024,2048]{1,0:T(8,128)(2,1)} %refs_1_.1), channel_id=1, source_target_pairs={{0,1},{1,0},{2,3},{3,2},{4,5},{5,4},{6,7},{7,6},{8,9},{9,8},{10,11... | collective-permute-start | bytes 12582920 | tf_op jit(solution)/shard_map/ppermute | solution.py:504
  3.7 13.1 %collective-permute-start.2 = (bf16[32,2048]{1,0:T(8,128)(2,1)S(1)}, bf16[32,2048]{1,0:T(8,128)(2,1)S(1)}, u32[]{:S(2)}, u32[]{:S(2)}) collective-permute-start(bf16[32,2048]{1,0:T(8,128)(2,1)S(1)} %get-tuple-element.117), channel_id=1, source_target_pairs={{0,8},{2,10},{4,12},{6,14},{8,0},{10,2},{12,4},{14,6},{16,24},{18,... | collective-permute-start | bytes 393224 | tf_op jit(solution)/shard_map/ppermute | solution.py:495
  6.5 10.3 %collective-permute-start.3 = (bf16[32,2048]{1,0:T(8,128)(2,1)S(1)}, bf16[32,2048]{1,0:T(8,128)(2,1)S(1)}, u32[]{:S(2)}, u32[]{:S(2)}) collective-permute-start(bf16[32,2048]{1,0:T(8,128)(2,1)S(1)} %get-tuple-element.118), channel_id=1, source_target_pairs={{0,16},{2,18},{4,20},{6,22},{8,24},{10,26},{12,28},{14,30},{16,0},... | collective-permute-start | bytes 393224 | tf_op jit(solution)/shard_map/ppermute | solution.py:495
  8.8 9.2 %collective-permute-start.4 = (bf16[32,2048]{1,0:T(8,128)(2,1)S(1)}, bf16[32,2048]{1,0:T(8,128)(2,1)S(1)}, u32[]{:S(2)}, u32[]{:S(2)}) collective-permute-start(bf16[32,2048]{1,0:T(8,128)(2,1)S(1)} %get-tuple-element.119), channel_id=1, source_target_pairs={{0,24},{2,26},{4,28},{6,30},{8,16},{10,18},{12,20},{14,22},{16,8},... | collective-permute-start | bytes 393224 | tf_op jit(solution)/shard_map/ppermute | solution.py:495
  12.8 7.9 %copy-start.1 = (bf16[1024]{0:T(1024)(128)(2,1)S(1)}, bf16[1024]{0:T(1024)(128)(2,1)}, u32[]{:S(2)}) copy-start(bf16[1024]{0:T(1024)(128)(2,1)} %param.9) | copy-start | bytes 6148
  18.0 9.3 %collective-permute-start.5 = (bf16[32,2048]{1,0:T(8,128)(2,1)S(1)}, bf16[32,2048]{1,0:T(8,128)(2,1)S(1)}, u32[]{:S(2)}, u32[]{:S(2)}) collective-permute-start(bf16[32,2048]{1,0:T(8,128)(2,1)S(1)} %get-tuple-element.122), channel_id=1, source_target_pairs={{0,2},{2,0},{4,6},{6,4},{8,10},{10,8},{12,14},{14,12},{16,18},{18,... | collective-permute-start | bytes 393224 | tf_op jit(solution)/shard_map/ppermute | solution.py:495
  19.3 8.0 %collective-permute-start.6 = (bf16[32,2048]{1,0:T(8,128)(2,1)S(1)}, bf16[32,2048]{1,0:T(8,128)(2,1)S(1)}, u32[]{:S(2)}, u32[]{:S(2)}) collective-permute-start(bf16[32,2048]{1,0:T(8,128)(2,1)S(1)} %get-tuple-element.123), channel_id=1, source_target_pairs={{0,4},{2,6},{4,0},{6,2},{8,12},{10,14},{12,8},{14,10},{16,20},{18,... | collective-permute-start | bytes 393224 | tf_op jit(solution)/shard_map/ppermute | solution.py:495
  20.5 6.8 %collective-permute-start.7 = (bf16[32,2048]{1,0:T(8,128)(2,1)S(1)}, bf16[32,2048]{1,0:T(8,128)(2,1)S(1)}, u32[]{:S(2)}, u32[]{:S(2)}) collective-permute-start(bf16[32,2048]{1,0:T(8,128)(2,1)S(1)} %get-tuple-element.124), channel_id=1, source_target_pairs={{0,6},{2,4},{4,2},{6,0},{8,14},{10,12},{12,10},{14,8},{16,22},{18,... | collective-permute-start | bytes 393224 | tf_op jit(solution)/shard_map/ppermute | solution.py:495
  20.8 6.6 %collective-permute-start.1 = (bf16[1,1024]{1,0:T(2,128)(2,1)S(1)}, bf16[1,1024]{1,0:T(2,128)(2,1)S(1)}, u32[]{:S(2)}, u32[]{:S(2)}) collective-permute-start(bf16[1,1024]{1,0:T(2,128)(2,1)S(1)} %reshape.27.refs_3_), channel_id=1, source_target_pairs={{0,1},{1,0},{2,3},{3,2},{4,5},{5,4},{6,7},{7,6},{8,9},{9,8},{10,11... | collective-permute-start | bytes 6152 | tf_op jit(solution)/shard_map/ppermute | solution.py:506
  29.2 3.5 %copy-start = (bf16[2,384,2048]{2,1,0:T(8,128)(2,1)S(1)}, bf16[2,384,2048]{2,1,0:T(8,128)(2,1)}, u32[]{:S(2)}) copy-start(bf16[2,384,2048]{2,1,0:T(8,128)(2,1)} %param.13) | copy-start | bytes 9437188
  31.1 11.4 %collective-permute-start.8 = (bf16[1024,768]{1,0:T(8,128)(2,1)S(1)}, bf16[1024,768]{1,0:T(8,128)(2,1)S(1)}, u32[]{:S(2)}, u32[]{:S(2)}) collective-permute-start(bf16[1024,768]{1,0:T(8,128)(2,1)S(1)} %get-tuple-element.146), channel_id=1, source_target_pairs={{0,1},{1,0},{2,3},{3,2},{4,5},{5,4},{6,7},{7,6},{8,9},{9,8},{10,11... | collective-permute-start | bytes 4718600 | tf_op jit(solution)/shard_map/ppermute | solution.py:636
  36.3 6.2 %collective-permute-start.9 = (bf16[768,1024]{1,0:T(8,128)(2,1)S(1)}, bf16[768,1024]{1,0:T(8,128)(2,1)S(1)}, u32[]{:S(2)}, u32[]{:S(2)}) collective-permute-start(bf16[768,1024]{1,0:T(8,128)(2,1)S(1)} %get-tuple-element.142.refs_3_.refs_2_), channel_id=1, source_target_pairs={{0,1},{1,0},{2,3},{3,2},{4,5},{5,4},{6,7},{7,6},{8,9},{9,8},{10,11... | collective-permute-start | bytes 4718600 | tf_op jit(solution)/shard_map/ppermute | solution.py:597
  39.3 11.3 %collective-permute-start.15 = (bf16[768,768]{1,0:T(8,128)(2,1)S(1)}, bf16[768,768]{1,0:T(8,128)(2,1)S(1)}, u32[]{:S(2)}, u32[]{:S(2)}) collective-permute-start(bf16[768,768]{1,0:T(8,128)(2,1)S(1)} %get-tuple-element.143.refs_4_.refs_2_.refs_3_), channel_id=1, source_target_pairs={{0,1},{1,0},{2,3},{3,2},{4,5},{5,4},{6,7},{7,6},{8,9},{9,8},{10,11... | collective-permute-start | bytes 3538952 | tf_op jit(solution)/shard_map/ppermute | solution.py:597
  46.1 14.9 %collective-permute-start.10 = (bf16[512,1024]{1,0:T(8,128)(2,1)S(1)}, bf16[512,1024]{1,0:T(8,128)(2,1)S(1)}, u32[]{:S(2)}, u32[]{:S(2)}) collective-permute-start(bf16[512,1024]{1,0:T(8,128)(2,1)S(1)} %get-tuple-element.154), channel_id=1, source_target_pairs={{0,2},{1,5},{2,0},{3,7},{4,6},{5,1},{6,4},{7,3},{8,10},{9,13},{10,... | collective-permute-start | bytes 3145736 | tf_op jit(solution)/shard_map/ppermute | solution.py:419
  46.8 7.5 %collective-permute-start.14 = (bf16[768,256]{1,0:T(8,128)(2,1)S(1)}, bf16[768,256]{1,0:T(8,128)(2,1)S(1)}, u32[]{:S(2)}, u32[]{:S(2)}) collective-permute-start(bf16[768,256]{1,0:T(8,128)(2,1)S(1)} %get-tuple-element.144.refs_5_.refs_2_.refs_4_), channel_id=1, source_target_pairs={{0,1},{1,0},{2,3},{3,2},{4,5},{5,4},{6,7},{7,6},{8,9},{9,8},{10,11... | collective-permute-start | bytes 1179656 | tf_op jit(solution)/shard_map/ppermute | solution.py:597
  46.8 9.3 %collective-permute-start.11 = (bf16[32,2176]{1,0:T(8,128)(2,1)S(1)}, bf16[32,2176]{1,0:T(8,128)(2,1)S(1)}, u32[]{:S(2)}, u32[]{:S(2)}) collective-permute-start(bf16[32,2176]{1,0:T(8,128)(2,1)S(1)} %get-tuple-element.156), channel_id=1, source_target_pairs={{0,8},{2,10},{4,12},{6,14},{8,0},{10,2},{12,4},{14,6},{16,24},{18,... | collective-permute-start | bytes 417800 | tf_op jit(solution)/shard_map/ppermute | solution.py:495
  49.5 7.1 %collective-permute-start.12 = (bf16[32,2176]{1,0:T(8,128)(2,1)S(1)}, bf16[32,2176]{1,0:T(8,128)(2,1)S(1)}, u32[]{:S(2)}, u32[]{:S(2)}) collective-permute-start(bf16[32,2176]{1,0:T(8,128)(2,1)S(1)} %get-tuple-element.157), channel_id=1, source_target_pairs={{0,16},{2,18},{4,20},{6,22},{8,24},{10,26},{12,28},{14,30},{16,0},... | collective-permute-start | bytes 417800 | tf_op jit(solution)/shard_map/ppermute | solution.py:495
  50.5 10.5 %collective-permute-start.13 = (bf16[32,2176]{1,0:T(8,128)(2,1)S(1)}, bf16[32,2176]{1,0:T(8,128)(2,1)S(1)}, u32[]{:S(2)}, u32[]{:S(2)}) collective-permute-start(bf16[32,2176]{1,0:T(8,128)(2,1)S(1)} %get-tuple-element.158), channel_id=1, source_target_pairs={{0,24},{2,26},{4,28},{6,30},{8,16},{10,18},{12,20},{14,22},{16,8},... | collective-permute-start | bytes 417800 | tf_op jit(solution)/shard_map/ppermute | solution.py:495
  54.4 16.2 %collective-permute-start.17 = (bf16[512,768]{1,0:T(8,128)(2,1)S(1)}, bf16[512,768]{1,0:T(8,128)(2,1)S(1)}, u32[]{:S(2)}, u32[]{:S(2)}) collective-permute-start(bf16[512,768]{1,0:T(8,128)(2,1)S(1)} %get-tuple-element.168), channel_id=1, source_target_pairs={{0,2},{1,5},{2,0},{3,7},{4,6},{5,1},{6,4},{7,3},{8,10},{9,13},{10,... | collective-permute-start | bytes 2359304 | tf_op jit(solution)/shard_map/ppermute | solution.py:419
  56.1 10.9 %collective-permute-start.18 = (bf16[512,256]{1,0:T(8,128)(2,1)S(1)}, bf16[512,256]{1,0:T(8,128)(2,1)S(1)}, u32[]{:S(2)}, u32[]{:S(2)}) collective-permute-start(bf16[512,256]{1,0:T(8,128)(2,1)S(1)} %get-tuple-element.170), channel_id=1, source_target_pairs={{0,8},{1,9},{2,10},{3,11},{4,12},{5,13},{6,14},{7,15},{8,0},{9,1},... | collective-permute-start | bytes 786440 | tf_op jit(solution)/shard_map/ppermute | solution.py:419
  61.3 13.3 %collective-permute-start.16 = (bf16[256,1024]{1,0:T(8,128)(2,1)S(1)}, bf16[256,1024]{1,0:T(8,128)(2,1)S(1)}, u32[]{:S(2)}, u32[]{:S(2)}) collective-permute-start(bf16[256,1024]{1,0:T(8,128)(2,1)S(1)} %get-tuple-element.166), channel_id=1, source_target_pairs={{0,4},{1,3},{2,6},{3,1},{4,0},{5,7},{6,2},{7,5},{8,12},{9,11},{10,... | collective-permute-start | bytes 1572872 | tf_op jit(solution)/shard_map/ppermute | solution.py:419
  67.1 14.8 %collective-permute-start.21 = (bf16[256,256]{1,0:T(8,128)(2,1)S(1)}, bf16[256,256]{1,0:T(8,128)(2,1)S(1)}, u32[]{:S(2)}, u32[]{:S(2)}) collective-permute-start(bf16[256,256]{1,0:T(8,128)(2,1)S(1)} %get-tuple-element.184), channel_id=1, source_target_pairs={{0,16},{1,17},{2,18},{3,19},{4,20},{5,21},{6,22},{7,23},{8,24},{9,... | collective-permute-start | bytes 393224 | tf_op jit(solution)/shard_map/ppermute | solution.py:419
  70.8 10.9 %collective-permute-start.19 = (bf16[256,768]{1,0:T(8,128)(2,1)S(1)}, bf16[256,768]{1,0:T(8,128)(2,1)S(1)}, u32[]{:S(2)}, u32[]{:S(2)}) collective-permute-start(bf16[256,768]{1,0:T(8,128)(2,1)S(1)} %get-tuple-element.179), channel_id=1, source_target_pairs={{0,4},{1,3},{2,6},{3,1},{4,0},{5,7},{6,2},{7,5},{8,12},{9,11},{10,... | collective-permute-start | bytes 1179656 | tf_op jit(solution)/shard_map/ppermute | solution.py:419
  74.7 9.3 %collective-permute-start.23 = (bf16[128,1024]{1,0:T(8,128)(2,1)S(1)}, bf16[128,1024]{1,0:T(8,128)(2,1)S(1)}, u32[]{:S(2)}, u32[]{:S(2)}) collective-permute-start(bf16[128,1024]{1,0:T(8,128)(2,1)S(1)} %get-tuple-element.189), channel_id=1, source_target_pairs={{0,8},{1,9},{2,10},{3,11},{4,12},{5,13},{6,14},{7,15},{8,0},{9,1},... | collective-permute-start | bytes 786440 | tf_op jit(solution)/shard_map/ppermute | solution.py:419
  81.8 6.3 %collective-permute-start.20 = (bf16[128,768]{1,0:T(8,128)(2,1)S(1)}, bf16[128,768]{1,0:T(8,128)(2,1)S(1)}, u32[]{:S(2)}, u32[]{:S(2)}) collective-permute-start(bf16[128,768]{1,0:T(8,128)(2,1)S(1)} %get-tuple-element.182), channel_id=1, source_target_pairs={{0,8},{1,9},{2,10},{3,11},{4,12},{5,13},{6,14},{7,15},{8,0},{9,1},... | collective-permute-start | bytes 589832 | tf_op jit(solution)/shard_map/ppermute | solution.py:419
  81.9 3.7 %collective-permute-start.22 = (bf16[128,256]{1,0:T(8,128)(2,1)S(1)}, bf16[128,256]{1,0:T(8,128)(2,1)S(1)}, u32[]{:S(2)}, u32[]{:S(2)}) collective-permute-start(bf16[128,256]{1,0:T(8,128)(2,1)S(1)} %get-tuple-element.187), channel_id=1, source_target_pairs={{0,2},{1,5},{2,0},{3,7},{4,6},{5,1},{6,4},{7,3},{8,10},{9,13},{10,... | collective-permute-start | bytes 196616 | tf_op jit(solution)/shard_map/ppermute | solution.py:419
  82.8 5.8 %collective-permute-start.24 = (bf16[32,2176]{1,0:T(8,128)(2,1)S(1)}, bf16[32,2176]{1,0:T(8,128)(2,1)S(1)}, u32[]{:S(2)}, u32[]{:S(2)}) collective-permute-start(bf16[32,2176]{1,0:T(8,128)(2,1)S(1)} %get-tuple-element.196), channel_id=1, source_target_pairs={{0,2},{2,0},{4,6},{6,4},{8,10},{10,8},{12,14},{14,12},{16,18},{18,... | collective-permute-start | bytes 417800 | tf_op jit(solution)/shard_map/ppermute | solution.py:495
  83.2 7.8 %collective-permute-start.25 = (bf16[32,2176]{1,0:T(8,128)(2,1)S(1)}, bf16[32,2176]{1,0:T(8,128)(2,1)S(1)}, u32[]{:S(2)}, u32[]{:S(2)}) collective-permute-start(bf16[32,2176]{1,0:T(8,128)(2,1)S(1)} %get-tuple-element.197), channel_id=1, source_target_pairs={{0,4},{2,6},{4,0},{6,2},{8,12},{10,14},{12,8},{14,10},{16,20},{18,... | collective-permute-start | bytes 417800 | tf_op jit(solution)/shard_map/ppermute | solution.py:495
  84.0 7.0 %collective-permute-start.26 = (bf16[32,2176]{1,0:T(8,128)(2,1)S(1)}, bf16[32,2176]{1,0:T(8,128)(2,1)S(1)}, u32[]{:S(2)}, u32[]{:S(2)}) collective-permute-start(bf16[32,2176]{1,0:T(8,128)(2,1)S(1)} %get-tuple-element.198), channel_id=1, source_target_pairs={{0,6},{2,4},{4,2},{6,0},{8,14},{10,12},{12,10},{14,8},{16,22},{18,... | collective-permute-start | bytes 417800 | tf_op jit(solution)/shard_map/ppermute | solution.py:495
  85.6 14.9 %collective-permute-start.28 = (bf16[64,1024]{1,0:T(8,128)(2,1)S(1)}, bf16[64,1024]{1,0:T(8,128)(2,1)S(1)}, u32[]{:S(2)}, u32[]{:S(2)}) collective-permute-start(bf16[64,1024]{1,0:T(8,128)(2,1)S(1)} %get-tuple-element.204), channel_id=1, source_target_pairs={{0,16},{1,17},{2,18},{3,19},{4,20},{5,21},{6,22},{7,23},{8,24},{9,... | collective-permute-start | bytes 393224 | tf_op jit(solution)/shard_map/ppermute | solution.py:419
  88.2 12.3 %collective-permute-start.29 = (bf16[64,768]{1,0:T(8,128)(2,1)S(1)}, bf16[64,768]{1,0:T(8,128)(2,1)S(1)}, u32[]{:S(2)}, u32[]{:S(2)}) collective-permute-start(bf16[64,768]{1,0:T(8,128)(2,1)S(1)} %get-tuple-element.206), channel_id=1, source_target_pairs={{0,16},{1,17},{2,18},{3,19},{4,20},{5,21},{6,22},{7,23},{8,24},{9,... | collective-permute-start | bytes 294920 | tf_op jit(solution)/shard_map/ppermute | solution.py:419
  88.7 11.8 %collective-permute-start.30 = (bf16[64,256]{1,0:T(8,128)(2,1)S(1)}, bf16[64,256]{1,0:T(8,128)(2,1)S(1)}, u32[]{:S(2)}, u32[]{:S(2)}) collective-permute-start(bf16[64,256]{1,0:T(8,128)(2,1)S(1)} %get-tuple-element.208), channel_id=1, source_target_pairs={{0,4},{1,3},{2,6},{3,1},{4,0},{5,7},{6,2},{7,5},{8,12},{9,11},{10,... | collective-permute-start | bytes 98312 | tf_op jit(solution)/shard_map/ppermute | solution.py:419
  91.0 9.5 %collective-permute-start.27 = (f32[1,128]{1,0:T(1,128)S(1)}, f32[1,128]{1,0:T(1,128)S(1)}, u32[]{:S(2)}, u32[]{:S(2)}) collective-permute-start(f32[1,128]{1,0:T(1,128)S(1)} %get-tuple-element.202.refs_1_), channel_id=1, source_target_pairs={{0,1},{1,0},{2,3},{3,2},{4,5},{5,4},{6,7},{7,6},{8,9},{9,8},{10,11... | collective-permute-start | bytes 1544 | tf_op jit(solution)/shard_map/ppermute | solution.py:669

commit v3 on v2

--- a/solution.py
+++ b/solution.py
@@ -182,13 +182,10 @@
     copies[3].wait()
 
 
-def pre_own_kernel(place, away, mixed, weight, pre, other, sem):
-    copy = pltpu.make_async_copy(away, other, sem)
-    copy.start()
+def pre_own_kernel(place, mixed, weight, pre):
     me = place[0]
     for at in tiles(pre.shape[1]):
         pre[:, at] = jnp.dot(mixed[me], weight[:, at], preferred_element_type=F32)
-    copy.wait()
 
 
 def pre_other_kernel(place, before, mixed, weight, pre):
@@ -523,6 +520,7 @@
         outgoing = move(outgoing, near)
 
     row = sds((1, slots), jnp.int32)
+    order.cost = 6 * 10**10
     mixed, mixed_t, ratio, ratio_row, adj_t, weight, send_row, recv_row, back_row = run(
         functools.partial(mix_kernel, orders),
         "mix",
@@ -542,15 +540,8 @@
         far=(weight, local_adj, *turned),
         scratch=[pltpu.VMEM(local_adj.shape, jnp.int32), *indices, pltpu.SemaphoreType.DMA((4,))],
     )
-    pre, other = run(
-        pre_own_kernel,
-        "pre_own",
-        (sds((rows, width), F32), sds(other.shape, BF16)),
-        (mixed, weight),
-        scalars=(place,),
-        far=(other,),
-        scratch=[pltpu.SemaphoreType.DMA(())],
-    )
+    order.cost = 1
+    (pre,) = run(pre_own_kernel, "pre_own", (sds((rows, width), F32),), (mixed, weight), scalars=(place,))
     if paired:
         arrived = run(
             functools.partial(
@@ -564,11 +555,7 @@
     else:
         arrived = [exchange(outgoing[0])]
     (pre,) = run(
-        pre_other_kernel,
-        "pre_other",
-        (sds((rows, width), F32),),
-        (pre, mixed, other),
-        scalars=(place,),
+        pre_other_kernel, "pre_other", (sds((rows, width), F32),), (pre, mixed, other), scalars=(place,)
     )
     remote, bias_full = run(
         remote_kernel,

time: 102 us -> 101 us (level)
    ppermute x12, waiting for transfers between devices: 5.53 us -> 4.12 us  [move(): moved[i] = lax.ppermute(pieces[i], 'parts', perm)]
    ppermute x12, starting transfers between devices: 15.3 us -> 14.1 us  [move(): moved[i] = lax.ppermute(pieces[i], 'parts', perm)]
    ppermute x1, starting transfers between devices: 0.12 us -> 1.23 us  [local(): other = lax.ppermute(weight, 'mp', SWAP)]
  transfers between devices with their start and end apart: 31 -> 31, of which waited for: 4 -> 4; matrix products, arithmetic and copies ran while one was open for 0% -> 0% of each run, Pallas kernels for 46% -> 43%
where the time goes in v3:
time: 101 us
  Pallas kernels  51.7 us (51%)
  starting transfers between devices  39 us (39%)
  waiting for transfers between devices  9.03 us (9%)
  between operations  1.03 us (1%)
    pallas_call x31, Pallas kernels, run(): pl.pallas_call(body, name=name, in_specs=specs, out_specs=(VMEM if keep i...  51.7 us
    ppermute x12, starting transfers between devices, send(): lax.ppermute(leave, AXES, partners(self.parts, self.axes.pop(0)))  14.4 us
    ppermute x12, starting transfers between devices, move(): moved[i] = lax.ppermute(pieces[i], 'parts', perm)  14.1 us
    ppermute x12, waiting for transfers between devices, send(): lax.ppermute(leave, AXES, partners(self.parts, self.axes.pop(0)))  4.89 us
    ppermute x12, waiting for transfers between devices, move(): moved[i] = lax.ppermute(pieces[i], 'parts', perm)  4.12 us
    ppermute x1, starting transfers between devices, local(): bias_theirs = lax.ppermute(bias_mine, 'mp', SWAP)  3.97 us
    ppermute x1, starting transfers between devices, local(): bias_other = lax.ppermute(bias_own, 'mp', SWAP)  3.2 us
  transfers between devices with their start and end apart: 31, of which 4 were waited for; matrix products, arithmetic and copies ran while one was open for 0% of the time, Pallas kernels for 43%

profile of v3, /device:TPU:1, one launch (start us, length us, event | category | flops | bytes accessed | tf_op | source)
XLA Modules:
  0.0 100.8 jit_solution(15537056176093843352)
XLA Ops:
  0.7 2.8 %outgoing.1 = (bf16[768,2048]{1,0:T(8,128)(2,1)S(1)}, bf16[32,2048]{1,0:T(8,128)(2,1)S(1)}, bf16[32,2048]{1,0:T(8,128)(2,1)S(1)}, bf16[32,2048]{1,0:T(8,128)(2,1...) custom-call(s32[2]{0:T(128)S(1)} %pad_add_fusion.refs_0_, bf16[768,2048]{1,0:T(8,128)(2,1)} %bitcast.12, ...), custom_call_target="tpu_custom_call" | custom-call | flops 1 | bytes 1 | tf_op jit(solution)/shard_map/outgoing/pallas_call | solution.py:59
  3.6 2.2 %collective-permute-start.2 = (bf16[32,2048]{1,0:T(8,128)(2,1)S(1)}, bf16[32,2048]{1,0:T(8,128)(2,1)S(1)}, u32[]{:S(2)}, u32[]{:S(2)}) collective-permute-start(bf16[32,2048]{1,0:T(8,128)(2,1)S(1)} %get-tuple-element.113), channel_id=1, source_target_pairs={{0,8},{2,10},{4,12},{6,14},{8,0},{10,2},{12,4},{14,6},{16,24},{18,... | collective-permute-start | bytes 393224 | tf_op jit(solution)/shard_map/ppermute | solution.py:492
  5.8 2.3 %collective-permute-start.3 = (bf16[32,2048]{1,0:T(8,128)(2,1)S(1)}, bf16[32,2048]{1,0:T(8,128)(2,1)S(1)}, u32[]{:S(2)}, u32[]{:S(2)}) collective-permute-start(bf16[32,2048]{1,0:T(8,128)(2,1)S(1)} %get-tuple-element.114), channel_id=1, source_target_pairs={{0,16},{2,18},{4,20},{6,22},{8,24},{10,26},{12,28},{14,30},{16,0},... | collective-permute-start | bytes 393224 | tf_op jit(solution)/shard_map/ppermute | solution.py:492
  8.1 1.2 %collective-permute-start = (bf16[1024,2048]{1,0:T(8,128)(2,1)}, bf16[1024,2048]{1,0:T(8,128)(2,1)S(1)}, u32[]{:S(2)}, u32[]{:S(2)}) collective-permute-start(bf16[1024,2048]{1,0:T(8,128)(2,1)} %refs_1_.1), channel_id=1, source_target_pairs={{0,1},{1,0},{2,3},{3,2},{4,5},{5,4},{6,7},{7,6},{8,9},{9,8},{10,11... | collective-permute-start | bytes 12582920 | tf_op jit(solution)/shard_map/ppermute | solution.py:501
  9.3 4.0 %mix.1 = (bf16[2,768,1024]{2,1,0:T(8,128)(2,1)S(1)}, bf16[2048,768]{1,0:T(8,128)(2,1)S(1)}, f32[768,1]{1,0:T(8,128)S(1)}, f32[8,768]{1,0:T(8,128)S(1)}, bf16[2,3...) custom-call(s32[2]{0:T(128)S(1)} %pad_add_fusion.refs_0_, ...), custom_call_target="tpu_custom_call" | custom-call | flops 60000002048 | bytes 1 | tf_op jit(solution)/shard_map/mix/pallas_call | solution.py:59
  13.3 4.0 %pre_own.1 = (f32[768,2048]{1,0:T(8,128)S(1)}, f32[8,128]{1,0:T(8,128)S(1)}) custom-call(s32[2]{0:T(128)S(1)} %pad_add_fusion.refs_0_, bf16[2,768,1024]{2,1,0:T(8,128)(2,1)S(1)} %get-tuple-element.116.refs_1_.refs_2_, bf16[1024,2048]{1,0:T(8,128)(2,1)S(1)} %get-tuple-element.111.refs_2_.refs_1_.refs_4_, f32[8,128]{1,0:T(8,128)S(1)} %get-tuple-element.117.refs_3_), custom_call_target="tpu_custom_call" | custom-call | flops 1 | bytes 1 | tf_op jit(solution)/shard_map/pre_own/pallas_call | solution.py:59
  17.4 1.5 %collective-permute-start.5 = (bf16[32,2048]{1,0:T(8,128)(2,1)S(1)}, bf16[32,2048]{1,0:T(8,128)(2,1)S(1)}, u32[]{:S(2)}, u32[]{:S(2)}) collective-permute-start(bf16[32,2048]{1,0:T(8,128)(2,1)S(1)} %get-tuple-element.120), channel_id=1, source_target_pairs={{0,2},{2,0},{4,6},{6,4},{8,10},{10,8},{12,14},{14,12},{16,18},{18,... | collective-permute-start | bytes 393224 | tf_op jit(solution)/shard_map/ppermute | solution.py:492
  18.8 1.2 %collective-permute-start.6 = (bf16[32,2048]{1,0:T(8,128)(2,1)S(1)}, bf16[32,2048]{1,0:T(8,128)(2,1)S(1)}, u32[]{:S(2)}, u32[]{:S(2)}) collective-permute-start(bf16[32,2048]{1,0:T(8,128)(2,1)S(1)} %get-tuple-element.121), channel_id=1, source_target_pairs={{0,4},{2,6},{4,0},{6,2},{8,12},{10,14},{12,8},{14,10},{16,20},{18,... | collective-permute-start | bytes 393224 | tf_op jit(solution)/shard_map/ppermute | solution.py:492
  20.1 3.2 %collective-permute-start.1 = (bf16[1,1024]{1,0:T(2,128)(2,1)S(1)}, bf16[1,1024]{1,0:T(2,128)(2,1)S(1)}, u32[]{:S(2)}, u32[]{:S(2)}) collective-permute-start(bf16[1,1024]{1,0:T(2,128)(2,1)S(1)} %reshape.27.refs_3_), channel_id=1, source_target_pairs={{0,1},{1,0},{2,3},{3,2},{4,5},{5,4},{6,7},{7,6},{8,9},{9,8},{10,11... | collective-permute-start | bytes 6152 | tf_op jit(solution)/shard_map/ppermute | solution.py:503
  23.3 4.0 %pre_other.1 = (f32[768,2048]{1,0:T(8,128)S(1)}, f32[8,128]{1,0:T(8,128)S(1)}) custom-call(s32[2]{0:T(128)S(1)} %pad_add_fusion.refs_0_, f32[768,2048]{1,0:T(8,128)S(1)} %get-tuple-element.123.refs_1_, bf16[2,768,1024]{2,1,0:T(8,128)(2,1)S(1)} %get-tuple-element.116.refs_1_.refs_2_, ...), custom_call_target="tpu_custom_call" | custom-call | flops 1 | bytes 1 | tf_op jit(solution)/shard_map/pre_other/pallas_call | solution.py:59
  27.3 1.9 %remote_product.1 = (bf16[256,2048]{1,0:T(8,128)(2,1)S(1)}, f32[1,2048]{1,0:T(1,128)S(1)}, f32[8,128]{1,0:T(8,128)S(1)}) custom-call(s32[2]{0:T(128)S(1)} %pad_add_fusion.refs_0_, bf16[1024,2048]{1,0:T(8,128)(2,1)S(1)} %get-tuple-element.111.refs_2_.refs_1_.refs_4_, bf16[1024,2048]{1,0:T(8,128)(2,1)S(1)} %collective-permute-done.refs_3_.refs_2_.refs_1_.refs_5_, ...), custom_call_target="tpu_custom_call" | custom-call | flops 1 | bytes 1 | tf_op jit(solution)/shard_map/remote_product/pallas_call | solution.py:59
  29.2 1.9 %finish_mixed.1 = (bf16[1024,768]{1,0:T(8,128)(2,1)S(1)}, bf16[1024,768]{1,0:T(8,128)(2,1)S(1)}, f32[8,128]{1,0:T(8,128)S(1)}) custom-call(s32[2]{0:T(128)S(1)} %pad_add_fusion.refs_0_, s32[1,128]{1,0:T(1,128)S(1)} %get-tuple-element.109.refs_1_.refs_0_, f32[8,768]{1,0:T(8,128)S(1)} %get-tuple-element.129.refs_2_, ...), custom_call_target="tpu_custom_call" | custom-call | flops 1 | bytes 1 | tf_op jit(solution)/shard_map/finish_mixed/pallas_call | solution.py:59
  31.2 1.4 %collective-permute-start.8 = (bf16[1024,768]{1,0:T(8,128)(2,1)S(1)}, bf16[1024,768]{1,0:T(8,128)(2,1)S(1)}, u32[]{:S(2)}, u32[]{:S(2)}) collective-permute-start(bf16[1024,768]{1,0:T(8,128)(2,1)S(1)} %get-tuple-element.144), channel_id=1, source_target_pairs={{0,1},{1,0},{2,3},{3,2},{4,5},{5,4},{6,7},{7,6},{8,9},{9,8},{10,11... | collective-permute-start | bytes 4718600 | tf_op jit(solution)/shard_map/ppermute | solution.py:623
  32.5 3.5 %gelu.3 = (bf16[768,2048]{1,0:T(8,128)(2,1)}, bf16[768,1024]{1,0:T(8,128)(2,1)S(1)}, f32[1,1024]{1,0:T(1,128)S(1)}, f32[8,128]{1,0:T(8,128)S(1)}) custom-call(s32[1,128]{1,0:T(1,128)S(1)} %get-tuple-element.109.refs_1_.refs_0_, f32[768,1]{1,0:T(8,128)S(1)} %get-tuple-element.110.refs_1_.refs_0_, bf16[256,2048]{1,0:T(8,128)(2,1)S(1)} %get-tuple-element.126.refs_2_, ...), custom_call_target="tpu_custom_call" | custom-call | flops 1000000000 | bytes 1 | tf_op jit(solution)/shard_map/gelu/pallas_call | solution.py:59
  36.1 2.9 %gelu.4 = (bf16[768,2048]{1,0:T(8,128)(2,1)}, bf16[768,768]{1,0:T(8,128)(2,1)S(1)}, f32[1,768]{1,0:T(1,128)S(1)}, f32[8,128]{1,0:T(8,128)S(1)}) custom-call(s32[1,128]{1,0:T(1,128)S(1)} %get-tuple-element.109.refs_1_.refs_0_, f32[768,1]{1,0:T(8,128)S(1)} %get-tuple-element.110.refs_1_.refs_0_, ...), custom_call_target="tpu_custom_call", output_to_operand_aliasing={{0}: (6, {})} | custom-call | flops 4000000000 | bytes 1 | tf_op jit(solution)/shard_map/gelu/pallas_call | solution.py:59
  39.0 0.6 collective-permute-start.15
  39.6 1.5 %gelu.5 = (bf16[768,2048]{1,0:T(8,128)(2,1)}, bf16[768,256]{1,0:T(8,128)(2,1)S(1)}, f32[1,256]{1,0:T(1,128)S(1)}, f32[8,128]{1,0:T(8,128)S(1)}) custom-call(s32[1,128]{1,0:T(1,128)S(1)} %get-tuple-element.109.refs_1_.refs_0_, f32[768,1]{1,0:T(8,128)S(1)} %get-tuple-element.110.refs_1_.refs_0_, ...), custom_call_target="tpu_custom_call", output_to_operand_aliasing={{0}: (6, {})} | custom-call | flops 1 | bytes 1 | tf_op jit(solution)/shard_map/gelu/pallas_call | solution.py:59
  41.1 1.2 %sent_grads.1 = (bf16[32,2176]{1,0:T(8,128)(2,1)S(1)}, bf16[32,2176]{1,0:T(8,128)(2,1)S(1)}, bf16[32,2176]{1,0:T(8,128)(2,1)S(1)}, bf16[32,2176]{1,0:T(8,128)(2,1)S(1)}, f32[8,128]{1,0:T(8,128)S(1)}) custom-call(s32[2]{0:T(128)S(1)} %pad_add_fusion.refs_0_, s32[1,128]{1,0:T(1,128)S(1)} %get-tuple-element.145.refs_1_, ...), custom_call_target="tpu_custom_call" | custom-call | flops 8000000000 | bytes 1 | tf_op jit(solution)/shard_map/sent_grads/pallas_call | solution.py:59
  42.3 3.4 %grad.3 = (bf16[512,1024]{1,0:T(8,128)(2,1)S(1)}, bf16[512,1024]{1,0:T(8,128)(2,1)S(1)}, f32[8,128]{1,0:T(8,128)S(1)}) custom-call(bf16[1024,768]{1,0:T(8,128)(2,1)S(1)} %get-tuple-element.143.refs_0_, bf16[1024,768]{1,0:T(8,128)(2,1)S(1)} %collective-permute-done.8.refs_1_, bf16[768,1024]{1,0:T(8,128)(2,1)S(1)} %get-tuple-element.140.refs_3_.refs_2_, ...), custom_call_target="tpu_custom_call" | custom-call | flops 16000000000 | bytes 1 | tf_op jit(solution)/shard_map/grad/pallas_call | solution.py:59
  45.7 0.7 collective-permute-start.10
  46.5 1.7 %collective-permute-start.11 = (bf16[32,2176]{1,0:T(8,128)(2,1)S(1)}, bf16[32,2176]{1,0:T(8,128)(2,1)S(1)}, u32[]{:S(2)}, u32[]{:S(2)}) collective-permute-start(bf16[32,2176]{1,0:T(8,128)(2,1)S(1)} %get-tuple-element.154), channel_id=1, source_target_pairs={{0,8},{2,10},{4,12},{6,14},{8,0},{10,2},{12,4},{14,6},{16,24},{18,... | collective-permute-start | bytes 417800 | tf_op jit(solution)/shard_map/ppermute | solution.py:492
  48.2 1.4 %collective-permute-start.12 = (bf16[32,2176]{1,0:T(8,128)(2,1)S(1)}, bf16[32,2176]{1,0:T(8,128)(2,1)S(1)}, u32[]{:S(2)}, u32[]{:S(2)}) collective-permute-start(bf16[32,2176]{1,0:T(8,128)(2,1)S(1)} %get-tuple-element.155), channel_id=1, source_target_pairs={{0,16},{2,18},{4,20},{6,22},{8,24},{10,26},{12,28},{14,30},{16,0},... | collective-permute-start | bytes 417800 | tf_op jit(solution)/shard_map/ppermute | solution.py:492
  49.6 1.1 %collective-permute-start.13 = (bf16[32,2176]{1,0:T(8,128)(2,1)S(1)}, bf16[32,2176]{1,0:T(8,128)(2,1)S(1)}, u32[]{:S(2)}, u32[]{:S(2)}) collective-permute-start(bf16[32,2176]{1,0:T(8,128)(2,1)S(1)} %get-tuple-element.156), channel_id=1, source_target_pairs={{0,24},{2,26},{4,28},{6,30},{8,16},{10,18},{12,20},{14,22},{16,8},... | collective-permute-start | bytes 417800 | tf_op jit(solution)/shard_map/ppermute | solution.py:492
  50.7 2.7 %grad.4 = (bf16[512,768]{1,0:T(8,128)(2,1)S(1)}, bf16[512,768]{1,0:T(8,128)(2,1)S(1)}, f32[8,128]{1,0:T(8,128)S(1)}) custom-call(bf16[1024,768]{1,0:T(8,128)(2,1)S(1)} %get-tuple-element.143.refs_0_, bf16[1024,768]{1,0:T(8,128)(2,1)S(1)} %collective-permute-done.8.refs_1_, bf16[768,768]{1,0:T(8,128)(2,1)S(1)} %get-tuple-element.141.refs_4_.refs_2_.refs_3_, ...), custom_call_target="tpu_custom_call" | custom-call | flops 1 | bytes 1 | tf_op jit(solution)/shard_map/grad/pallas_call | solution.py:59
  53.4 1.0 collective-permute-start.17
  54.4 1.0 grad.5
  55.4 0.5 collective-permute-start.18
  55.9 4.1 %collective-permute-done.13.refs_3_ = bf16[32,2176]{1,0:T(8,128)(2,1)S(1)} collective-permute-done((bf16[32,2176]{1,0:T(8,128)(2,1)S(1)}, bf16[32,2176]{1,0:T(8,128)(2,1)S(1)}, u32[]{:S(2)}, u32[]{:S(2)}) %collective-permute-start.13) | collective-permute-done | bytes 139296 | tf_op jit(solution)/shard_map/ppermute | solution.py:492
  60.0 0.2 halve.9
  60.3 1.7 %collective-permute-start.16 = (bf16[256,1024]{1,0:T(8,128)(2,1)S(1)}, bf16[256,1024]{1,0:T(8,128)(2,1)S(1)}, u32[]{:S(2)}, u32[]{:S(2)}) collective-permute-start(bf16[256,1024]{1,0:T(8,128)(2,1)S(1)} %get-tuple-element.164), channel_id=1, source_target_pairs={{0,4},{1,3},{2,6},{3,1},{4,0},{5,7},{6,2},{7,5},{8,12},{9,11},{10,... | collective-permute-start | bytes 1572872 | tf_op jit(solution)/shard_map/ppermute | solution.py:416
  62.0 3.5 %back.2 = (bf16[768,1024]{1,0:T(8,128)(2,1)S(1)}, f32[8,128]{1,0:T(8,128)S(1)}) custom-call(f32[768,1]{1,0:T(8,128)S(1)} %get-tuple-element.110.refs_1_.refs_0_, bf16[1024,2048]{1,0:T(8,128)(2,1)S(1)} %get-tuple-element.111.refs_2_.refs_1_.refs_4_, bf16[768,1024]{1,0:T(8,128)(2,1)S(1)} %get-tuple-element.140.refs_3_.refs_2_, ...), custom_call_target="tpu_custom_call" | custom-call | flops 1 | bytes 1 | tf_op jit(solution)/shard_map/back/pallas_call | solution.py:59
  65.5 0.6 collective-permute-done.18.refs_1_
  66.2 3.6 %collective-permute-start.21 = (bf16[256,256]{1,0:T(8,128)(2,1)S(1)}, bf16[256,256]{1,0:T(8,128)(2,1)S(1)}, u32[]{:S(2)}, u32[]{:S(2)}) collective-permute-start(bf16[256,256]{1,0:T(8,128)(2,1)S(1)} %get-tuple-element.182), channel_id=1, source_target_pairs={{0,16},{1,17},{2,18},{3,19},{4,20},{5,21},{6,22},{7,23},{8,24},{9,... | collective-permute-start | bytes 393224 | tf_op jit(solution)/shard_map/ppermute | solution.py:416
  69.8 0.5 collective-permute-done.17.refs_1_
  70.5 3.7 %collective-permute-done.16.refs_1_ = bf16[256,1024]{1,0:T(8,128)(2,1)S(1)} collective-permute-done((bf16[256,1024]{1,0:T(8,128)(2,1)S(1)}, bf16[256,1024]{1,0:T(8,128)(2,1)S(1)}, u32[]{:S(2)}, u32[]{:S(2)}) %collective-permute-start.16) | collective-permute-done | bytes 524320 | tf_op jit(solution)/shard_map/ppermute | solution.py:416
  74.4 1.5 %collective-permute-start.23 = (bf16[128,1024]{1,0:T(8,128)(2,1)S(1)}, bf16[128,1024]{1,0:T(8,128)(2,1)S(1)}, u32[]{:S(2)}, u32[]{:S(2)}) collective-permute-start(bf16[128,1024]{1,0:T(8,128)(2,1)S(1)} %get-tuple-element.187), channel_id=1, source_target_pairs={{0,8},{1,9},{2,10},{3,11},{4,12},{5,13},{6,14},{7,15},{8,0},{9,1},... | collective-permute-start | bytes 786440 | tf_op jit(solution)/shard_map/ppermute | solution.py:416
  75.8 3.7 %back.3 = (bf16[768,1024]{1,0:T(8,128)(2,1)S(1)}, f32[8,128]{1,0:T(8,128)S(1)}) custom-call(f32[768,1]{1,0:T(8,128)S(1)} %get-tuple-element.110.refs_1_.refs_0_, bf16[1024,2048]{1,0:T(8,128)(2,1)S(1)} %collective-permute-done.refs_3_.refs_2_.refs_1_.refs_5_, bf16[768,1024]{1,0:T(8,128)(2,1)S(1)} %get-tuple-element.140.refs_3_.refs_2_, ...), custom_call_target="tpu_custom_call" | custom-call | flops 1000000000 | bytes 1 | tf_op jit(solution)/shard_map/back/pallas_call | solution.py:59
  79.5 1.0 input_local.2
  80.8 0.7 collective-permute-start.22
  81.6 0.9 collective-permute-start.24
  82.7 1.5 %collective-permute-start.26 = (bf16[32,2176]{1,0:T(8,128)(2,1)S(1)}, bf16[32,2176]{1,0:T(8,128)(2,1)S(1)}, u32[]{:S(2)}, u32[]{:S(2)}) collective-permute-start(bf16[32,2176]{1,0:T(8,128)(2,1)S(1)} %get-tuple-element.196), channel_id=1, source_target_pairs={{0,6},{2,4},{4,2},{6,0},{8,14},{10,12},{12,10},{14,8},{16,22},{18,... | collective-permute-start | bytes 417800 | tf_op jit(solution)/shard_map/ppermute | solution.py:492
  84.3 2.8 %collective-permute-start.28 = (bf16[64,1024]{1,0:T(8,128)(2,1)S(1)}, bf16[64,1024]{1,0:T(8,128)(2,1)S(1)}, u32[]{:S(2)}, u32[]{:S(2)}) collective-permute-start(bf16[64,1024]{1,0:T(8,128)(2,1)S(1)} %get-tuple-element.202), channel_id=1, source_target_pairs={{0,16},{1,17},{2,18},{3,19},{4,20},{5,21},{6,22},{7,23},{8,24},{9,... | collective-permute-start | bytes 393224 | tf_op jit(solution)/shard_map/ppermute | solution.py:416
  87.2 0.2 collective-permute-start.29
  87.4 1.4 %collective-permute-start.30 = (bf16[64,256]{1,0:T(8,128)(2,1)S(1)}, bf16[64,256]{1,0:T(8,128)(2,1)S(1)}, u32[]{:S(2)}, u32[]{:S(2)}) collective-permute-start(bf16[64,256]{1,0:T(8,128)(2,1)S(1)} %get-tuple-element.206), channel_id=1, source_target_pairs={{0,4},{1,3},{2,6},{3,1},{4,0},{5,7},{6,2},{7,5},{8,12},{9,11},{10,... | collective-permute-start | bytes 98312 | tf_op jit(solution)/shard_map/ppermute | solution.py:416
  88.8 1.0 input_local.3
  89.9 4.0 %collective-permute-start.27 = (f32[1,128]{1,0:T(1,128)S(1)}, f32[1,128]{1,0:T(1,128)S(1)}, u32[]{:S(2)}, u32[]{:S(2)}) collective-permute-start(f32[1,128]{1,0:T(1,128)S(1)} %get-tuple-element.200.refs_1_), channel_id=1, source_target_pairs={{0,1},{1,0},{2,3},{3,2},{4,5},{5,4},{6,7},{7,6},{8,9},{9,8},{10,11... | collective-permute-start | bytes 1544 | tf_op jit(solution)/shard_map/ppermute | solution.py:656
  93.8 5.6 %input_gradient.1 = (bf16[768,2048]{1,0:T(8,128)(2,1)}, f32[8,128]{1,0:T(8,128)S(1)}) custom-call(s32[2]{0:T(128)S(1)} %pad_add_fusion.refs_0_, s32[1,128]{1,0:T(1,128)S(1)} %get-tuple-element.138.refs_1_, f32[768,1024]{1,0:T(8,128)S(1)} %get-tuple-element.174.refs_2_, f32[768,1024]{1,0:T(8,128)S(1)} %get-tuple-element.192.refs_3_, ...), custom_call_target="tpu_custom_call" | custom-call | flops 1 | bytes 1 | tf_op jit(solution)/shard_map/input_gradient/pallas_call | solution.py:59
  99.4 1.4 %last_sum.1 = (f32[64,2048]{1,0:T(8,128)}, f32[1,64]{1,0:T(1,128)}, f32[8,128]{1,0:T(8,128)}) custom-call(s32[2]{0:T(128)S(1)} %pad_add_fusion.refs_0_, f32[1,128]{1,0:T(1,128)S(1)} %get-tuple-element.200.refs_1_, f32[1,128]{1,0:T(1,128)S(1)} %collective-permute-done.27.refs_2_, bf16[64,1024]{1,0:T(8,128)(2,1)S(1)} %get-tuple-element.201.refs_3_, ...), custom_call_target="tpu_custom_call" | custom-call | flops 1 | bytes 1 | tf_op jit(solution)/shard_map/last_sum/pallas_call | solution.py:59
  (51 shorter events, 1.4 us)
Async XLA Ops:
  3.6 13.7 %collective-permute-start.2 = (bf16[32,2048]{1,0:T(8,128)(2,1)S(1)}, bf16[32,2048]{1,0:T(8,128)(2,1)S(1)}, u32[]{:S(2)}, u32[]{:S(2)}) collective-permute-start(bf16[32,2048]{1,0:T(8,128)(2,1)S(1)} %get-tuple-element.113), channel_id=1, source_target_pairs={{0,8},{2,10},{4,12},{6,14},{8,0},{10,2},{12,4},{14,6},{16,24},{18,... | collective-permute-start | bytes 393224 | tf_op jit(solution)/shard_map/ppermute | solution.py:492
  5.8 11.5 %collective-permute-start.3 = (bf16[32,2048]{1,0:T(8,128)(2,1)S(1)}, bf16[32,2048]{1,0:T(8,128)(2,1)S(1)}, u32[]{:S(2)}, u32[]{:S(2)}) collective-permute-start(bf16[32,2048]{1,0:T(8,128)(2,1)S(1)} %get-tuple-element.114), channel_id=1, source_target_pairs={{0,16},{2,18},{4,20},{6,22},{8,24},{10,26},{12,28},{14,30},{16,0},... | collective-permute-start | bytes 393224 | tf_op jit(solution)/shard_map/ppermute | solution.py:492
  8.1 9.2 %collective-permute-start.4 = (bf16[32,2048]{1,0:T(8,128)(2,1)S(1)}, bf16[32,2048]{1,0:T(8,128)(2,1)S(1)}, u32[]{:S(2)}, u32[]{:S(2)}) collective-permute-start(bf16[32,2048]{1,0:T(8,128)(2,1)S(1)} %get-tuple-element.115), channel_id=1, source_target_pairs={{0,24},{2,26},{4,28},{6,30},{8,16},{10,18},{12,20},{14,22},{16,8},... | collective-permute-start | bytes 393224 | tf_op jit(solution)/shard_map/ppermute | solution.py:492
  8.1 15.2 %collective-permute-start = (bf16[1024,2048]{1,0:T(8,128)(2,1)}, bf16[1024,2048]{1,0:T(8,128)(2,1)S(1)}, u32[]{:S(2)}, u32[]{:S(2)}) collective-permute-start(bf16[1024,2048]{1,0:T(8,128)(2,1)} %refs_1_.1), channel_id=1, source_target_pairs={{0,1},{1,0},{2,3},{3,2},{4,5},{5,4},{6,7},{7,6},{8,9},{9,8},{10,11... | collective-permute-start | bytes 12582920 | tf_op jit(solution)/shard_map/ppermute | solution.py:501
  13.3 6.8 %copy-start.1 = (bf16[1024]{0:T(1024)(128)(2,1)S(1)}, bf16[1024]{0:T(1024)(128)(2,1)}, u32[]{:S(2)}) copy-start(bf16[1024]{0:T(1024)(128)(2,1)} %param.9) | copy-start | bytes 6148
  17.4 9.9 %collective-permute-start.5 = (bf16[32,2048]{1,0:T(8,128)(2,1)S(1)}, bf16[32,2048]{1,0:T(8,128)(2,1)S(1)}, u32[]{:S(2)}, u32[]{:S(2)}) collective-permute-start(bf16[32,2048]{1,0:T(8,128)(2,1)S(1)} %get-tuple-element.120), channel_id=1, source_target_pairs={{0,2},{2,0},{4,6},{6,4},{8,10},{10,8},{12,14},{14,12},{16,18},{18,... | collective-permute-start | bytes 393224 | tf_op jit(solution)/shard_map/ppermute | solution.py:492
  18.8 8.5 %collective-permute-start.6 = (bf16[32,2048]{1,0:T(8,128)(2,1)S(1)}, bf16[32,2048]{1,0:T(8,128)(2,1)S(1)}, u32[]{:S(2)}, u32[]{:S(2)}) collective-permute-start(bf16[32,2048]{1,0:T(8,128)(2,1)S(1)} %get-tuple-element.121), channel_id=1, source_target_pairs={{0,4},{2,6},{4,0},{6,2},{8,12},{10,14},{12,8},{14,10},{16,20},{18,... | collective-permute-start | bytes 393224 | tf_op jit(solution)/shard_map/ppermute | solution.py:492
  20.1 7.2 %collective-permute-start.7 = (bf16[32,2048]{1,0:T(8,128)(2,1)S(1)}, bf16[32,2048]{1,0:T(8,128)(2,1)S(1)}, u32[]{:S(2)}, u32[]{:S(2)}) collective-permute-start(bf16[32,2048]{1,0:T(8,128)(2,1)S(1)} %get-tuple-element.122), channel_id=1, source_target_pairs={{0,6},{2,4},{4,2},{6,0},{8,14},{10,12},{12,10},{14,8},{16,22},{18,... | collective-permute-start | bytes 393224 | tf_op jit(solution)/shard_map/ppermute | solution.py:492
  20.1 7.2 %collective-permute-start.1 = (bf16[1,1024]{1,0:T(2,128)(2,1)S(1)}, bf16[1,1024]{1,0:T(2,128)(2,1)S(1)}, u32[]{:S(2)}, u32[]{:S(2)}) collective-permute-start(bf16[1,1024]{1,0:T(2,128)(2,1)S(1)} %reshape.27.refs_3_), channel_id=1, source_target_pairs={{0,1},{1,0},{2,3},{3,2},{4,5},{5,4},{6,7},{7,6},{8,9},{9,8},{10,11... | collective-permute-start | bytes 6152 | tf_op jit(solution)/shard_map/ppermute | solution.py:503
  29.2 3.3 %copy-start = (bf16[2,384,2048]{2,1,0:T(8,128)(2,1)S(1)}, bf16[2,384,2048]{2,1,0:T(8,128)(2,1)}, u32[]{:S(2)}) copy-start(bf16[2,384,2048]{2,1,0:T(8,128)(2,1)} %param.13) | copy-start | bytes 9437188
  31.2 11.1 %collective-permute-start.8 = (bf16[1024,768]{1,0:T(8,128)(2,1)S(1)}, bf16[1024,768]{1,0:T(8,128)(2,1)S(1)}, u32[]{:S(2)}, u32[]{:S(2)}) collective-permute-start(bf16[1024,768]{1,0:T(8,128)(2,1)S(1)} %get-tuple-element.144), channel_id=1, source_target_pairs={{0,1},{1,0},{2,3},{3,2},{4,5},{5,4},{6,7},{7,6},{8,9},{9,8},{10,11... | collective-permute-start | bytes 4718600 | tf_op jit(solution)/shard_map/ppermute | solution.py:623
  36.1 6.2 %collective-permute-start.9 = (bf16[768,1024]{1,0:T(8,128)(2,1)S(1)}, bf16[768,1024]{1,0:T(8,128)(2,1)S(1)}, u32[]{:S(2)}, u32[]{:S(2)}) collective-permute-start(bf16[768,1024]{1,0:T(8,128)(2,1)S(1)} %get-tuple-element.140.refs_3_.refs_2_), channel_id=1, source_target_pairs={{0,1},{1,0},{2,3},{3,2},{4,5},{5,4},{6,7},{7,6},{8,9},{9,8},{10,11... | collective-permute-start | bytes 4718600 | tf_op jit(solution)/shard_map/ppermute | solution.py:584
  39.0 10.6 %collective-permute-start.15 = (bf16[768,768]{1,0:T(8,128)(2,1)S(1)}, bf16[768,768]{1,0:T(8,128)(2,1)S(1)}, u32[]{:S(2)}, u32[]{:S(2)}) collective-permute-start(bf16[768,768]{1,0:T(8,128)(2,1)S(1)} %get-tuple-element.141.refs_4_.refs_2_.refs_3_), channel_id=1, source_target_pairs={{0,1},{1,0},{2,3},{3,2},{4,5},{5,4},{6,7},{7,6},{8,9},{9,8},{10,11... | collective-permute-start | bytes 3538952 | tf_op jit(solution)/shard_map/ppermute | solution.py:584
  45.7 14.3 %collective-permute-start.10 = (bf16[512,1024]{1,0:T(8,128)(2,1)S(1)}, bf16[512,1024]{1,0:T(8,128)(2,1)S(1)}, u32[]{:S(2)}, u32[]{:S(2)}) collective-permute-start(bf16[512,1024]{1,0:T(8,128)(2,1)S(1)} %get-tuple-element.152), channel_id=1, source_target_pairs={{0,2},{1,5},{2,0},{3,7},{4,6},{5,1},{6,4},{7,3},{8,10},{9,13},{10,... | collective-permute-start | bytes 3145736 | tf_op jit(solution)/shard_map/ppermute | solution.py:416
  46.5 6.9 %collective-permute-start.14 = (bf16[768,256]{1,0:T(8,128)(2,1)S(1)}, bf16[768,256]{1,0:T(8,128)(2,1)S(1)}, u32[]{:S(2)}, u32[]{:S(2)}) collective-permute-start(bf16[768,256]{1,0:T(8,128)(2,1)S(1)} %get-tuple-element.142.refs_5_.refs_2_.refs_4_), channel_id=1, source_target_pairs={{0,1},{1,0},{2,3},{3,2},{4,5},{5,4},{6,7},{7,6},{8,9},{9,8},{10,11... | collective-permute-start | bytes 1179656 | tf_op jit(solution)/shard_map/ppermute | solution.py:584
  46.5 8.9 %collective-permute-start.11 = (bf16[32,2176]{1,0:T(8,128)(2,1)S(1)}, bf16[32,2176]{1,0:T(8,128)(2,1)S(1)}, u32[]{:S(2)}, u32[]{:S(2)}) collective-permute-start(bf16[32,2176]{1,0:T(8,128)(2,1)S(1)} %get-tuple-element.154), channel_id=1, source_target_pairs={{0,8},{2,10},{4,12},{6,14},{8,0},{10,2},{12,4},{14,6},{16,24},{18,... | collective-permute-start | bytes 417800 | tf_op jit(solution)/shard_map/ppermute | solution.py:492
  48.2 7.7 %collective-permute-start.12 = (bf16[32,2176]{1,0:T(8,128)(2,1)S(1)}, bf16[32,2176]{1,0:T(8,128)(2,1)S(1)}, u32[]{:S(2)}, u32[]{:S(2)}) collective-permute-start(bf16[32,2176]{1,0:T(8,128)(2,1)S(1)} %get-tuple-element.155), channel_id=1, source_target_pairs={{0,16},{2,18},{4,20},{6,22},{8,24},{10,26},{12,28},{14,30},{16,0},... | collective-permute-start | bytes 417800 | tf_op jit(solution)/shard_map/ppermute | solution.py:492
  49.6 10.4 %collective-permute-start.13 = (bf16[32,2176]{1,0:T(8,128)(2,1)S(1)}, bf16[32,2176]{1,0:T(8,128)(2,1)S(1)}, u32[]{:S(2)}, u32[]{:S(2)}) collective-permute-start(bf16[32,2176]{1,0:T(8,128)(2,1)S(1)} %get-tuple-element.156), channel_id=1, source_target_pairs={{0,24},{2,26},{4,28},{6,30},{8,16},{10,18},{12,20},{14,22},{16,8},... | collective-permute-start | bytes 417800 | tf_op jit(solution)/shard_map/ppermute | solution.py:492
  53.4 16.9 %collective-permute-start.17 = (bf16[512,768]{1,0:T(8,128)(2,1)S(1)}, bf16[512,768]{1,0:T(8,128)(2,1)S(1)}, u32[]{:S(2)}, u32[]{:S(2)}) collective-permute-start(bf16[512,768]{1,0:T(8,128)(2,1)S(1)} %get-tuple-element.166), channel_id=1, source_target_pairs={{0,2},{1,5},{2,0},{3,7},{4,6},{5,1},{6,4},{7,3},{8,10},{9,13},{10,... | collective-permute-start | bytes 2359304 | tf_op jit(solution)/shard_map/ppermute | solution.py:416
  55.4 10.8 %collective-permute-start.18 = (bf16[512,256]{1,0:T(8,128)(2,1)S(1)}, bf16[512,256]{1,0:T(8,128)(2,1)S(1)}, u32[]{:S(2)}, u32[]{:S(2)}) collective-permute-start(bf16[512,256]{1,0:T(8,128)(2,1)S(1)} %get-tuple-element.168), channel_id=1, source_target_pairs={{0,8},{1,9},{2,10},{3,11},{4,12},{5,13},{6,14},{7,15},{8,0},{9,1},... | collective-permute-start | bytes 786440 | tf_op jit(solution)/shard_map/ppermute | solution.py:416
  60.3 14.0 %collective-permute-start.16 = (bf16[256,1024]{1,0:T(8,128)(2,1)S(1)}, bf16[256,1024]{1,0:T(8,128)(2,1)S(1)}, u32[]{:S(2)}, u32[]{:S(2)}) collective-permute-start(bf16[256,1024]{1,0:T(8,128)(2,1)S(1)} %get-tuple-element.164), channel_id=1, source_target_pairs={{0,4},{1,3},{2,6},{3,1},{4,0},{5,7},{6,2},{7,5},{8,12},{9,11},{10,... | collective-permute-start | bytes 1572872 | tf_op jit(solution)/shard_map/ppermute | solution.py:416
  66.2 14.6 %collective-permute-start.21 = (bf16[256,256]{1,0:T(8,128)(2,1)S(1)}, bf16[256,256]{1,0:T(8,128)(2,1)S(1)}, u32[]{:S(2)}, u32[]{:S(2)}) collective-permute-start(bf16[256,256]{1,0:T(8,128)(2,1)S(1)} %get-tuple-element.182), channel_id=1, source_target_pairs={{0,16},{1,17},{2,18},{3,19},{4,20},{5,21},{6,22},{7,23},{8,24},{9,... | collective-permute-start | bytes 393224 | tf_op jit(solution)/shard_map/ppermute | solution.py:416
  70.5 10.1 %collective-permute-start.19 = (bf16[256,768]{1,0:T(8,128)(2,1)S(1)}, bf16[256,768]{1,0:T(8,128)(2,1)S(1)}, u32[]{:S(2)}, u32[]{:S(2)}) collective-permute-start(bf16[256,768]{1,0:T(8,128)(2,1)S(1)} %get-tuple-element.177), channel_id=1, source_target_pairs={{0,4},{1,3},{2,6},{3,1},{4,0},{5,7},{6,2},{7,5},{8,12},{9,11},{10,... | collective-permute-start | bytes 1179656 | tf_op jit(solution)/shard_map/ppermute | solution.py:416
  74.4 8.3 %collective-permute-start.23 = (bf16[128,1024]{1,0:T(8,128)(2,1)S(1)}, bf16[128,1024]{1,0:T(8,128)(2,1)S(1)}, u32[]{:S(2)}, u32[]{:S(2)}) collective-permute-start(bf16[128,1024]{1,0:T(8,128)(2,1)S(1)} %get-tuple-element.187), channel_id=1, source_target_pairs={{0,8},{1,9},{2,10},{3,11},{4,12},{5,13},{6,14},{7,15},{8,0},{9,1},... | collective-permute-start | bytes 786440 | tf_op jit(solution)/shard_map/ppermute | solution.py:416
  80.6 6.5 %collective-permute-start.20 = (bf16[128,768]{1,0:T(8,128)(2,1)S(1)}, bf16[128,768]{1,0:T(8,128)(2,1)S(1)}, u32[]{:S(2)}, u32[]{:S(2)}) collective-permute-start(bf16[128,768]{1,0:T(8,128)(2,1)S(1)} %get-tuple-element.180), channel_id=1, source_target_pairs={{0,8},{1,9},{2,10},{3,11},{4,12},{5,13},{6,14},{7,15},{8,0},{9,1},... | collective-permute-start | bytes 589832 | tf_op jit(solution)/shard_map/ppermute | solution.py:416
  80.8 3.5 %collective-permute-start.22 = (bf16[128,256]{1,0:T(8,128)(2,1)S(1)}, bf16[128,256]{1,0:T(8,128)(2,1)S(1)}, u32[]{:S(2)}, u32[]{:S(2)}) collective-permute-start(bf16[128,256]{1,0:T(8,128)(2,1)S(1)} %get-tuple-element.185), channel_id=1, source_target_pairs={{0,2},{1,5},{2,0},{3,7},{4,6},{5,1},{6,4},{7,3},{8,10},{9,13},{10,... | collective-permute-start | bytes 196616 | tf_op jit(solution)/shard_map/ppermute | solution.py:416
  81.6 5.9 %collective-permute-start.24 = (bf16[32,2176]{1,0:T(8,128)(2,1)S(1)}, bf16[32,2176]{1,0:T(8,128)(2,1)S(1)}, u32[]{:S(2)}, u32[]{:S(2)}) collective-permute-start(bf16[32,2176]{1,0:T(8,128)(2,1)S(1)} %get-tuple-element.194), channel_id=1, source_target_pairs={{0,2},{2,0},{4,6},{6,4},{8,10},{10,8},{12,14},{14,12},{16,18},{18,... | collective-permute-start | bytes 417800 | tf_op jit(solution)/shard_map/ppermute | solution.py:492
  82.5 7.3 %collective-permute-start.25 = (bf16[32,2176]{1,0:T(8,128)(2,1)S(1)}, bf16[32,2176]{1,0:T(8,128)(2,1)S(1)}, u32[]{:S(2)}, u32[]{:S(2)}) collective-permute-start(bf16[32,2176]{1,0:T(8,128)(2,1)S(1)} %get-tuple-element.195), channel_id=1, source_target_pairs={{0,4},{2,6},{4,0},{6,2},{8,12},{10,14},{12,8},{14,10},{16,20},{18,... | collective-permute-start | bytes 417800 | tf_op jit(solution)/shard_map/ppermute | solution.py:492
  82.7 7.1 %collective-permute-start.26 = (bf16[32,2176]{1,0:T(8,128)(2,1)S(1)}, bf16[32,2176]{1,0:T(8,128)(2,1)S(1)}, u32[]{:S(2)}, u32[]{:S(2)}) collective-permute-start(bf16[32,2176]{1,0:T(8,128)(2,1)S(1)} %get-tuple-element.196), channel_id=1, source_target_pairs={{0,6},{2,4},{4,2},{6,0},{8,14},{10,12},{12,10},{14,8},{16,22},{18,... | collective-permute-start | bytes 417800 | tf_op jit(solution)/shard_map/ppermute | solution.py:492
  84.3 15.1 %collective-permute-start.28 = (bf16[64,1024]{1,0:T(8,128)(2,1)S(1)}, bf16[64,1024]{1,0:T(8,128)(2,1)S(1)}, u32[]{:S(2)}, u32[]{:S(2)}) collective-permute-start(bf16[64,1024]{1,0:T(8,128)(2,1)S(1)} %get-tuple-element.202), channel_id=1, source_target_pairs={{0,16},{1,17},{2,18},{3,19},{4,20},{5,21},{6,22},{7,23},{8,24},{9,... | collective-permute-start | bytes 393224 | tf_op jit(solution)/shard_map/ppermute | solution.py:416
  87.2 12.2 %collective-permute-start.29 = (bf16[64,768]{1,0:T(8,128)(2,1)S(1)}, bf16[64,768]{1,0:T(8,128)(2,1)S(1)}, u32[]{:S(2)}, u32[]{:S(2)}) collective-permute-start(bf16[64,768]{1,0:T(8,128)(2,1)S(1)} %get-tuple-element.204), channel_id=1, source_target_pairs={{0,16},{1,17},{2,18},{3,19},{4,20},{5,21},{6,22},{7,23},{8,24},{9,... | collective-permute-start | bytes 294920 | tf_op jit(solution)/shard_map/ppermute | solution.py:416
  87.4 12.0 %collective-permute-start.30 = (bf16[64,256]{1,0:T(8,128)(2,1)S(1)}, bf16[64,256]{1,0:T(8,128)(2,1)S(1)}, u32[]{:S(2)}, u32[]{:S(2)}) collective-permute-start(bf16[64,256]{1,0:T(8,128)(2,1)S(1)} %get-tuple-element.206), channel_id=1, source_target_pairs={{0,4},{1,3},{2,6},{3,1},{4,0},{5,7},{6,2},{7,5},{8,12},{9,11},{10,... | collective-permute-start | bytes 98312 | tf_op jit(solution)/shard_map/ppermute | solution.py:416
  89.9 9.6 %collective-permute-start.27 = (f32[1,128]{1,0:T(1,128)S(1)}, f32[1,128]{1,0:T(1,128)S(1)}, u32[]{:S(2)}, u32[]{:S(2)}) collective-permute-start(f32[1,128]{1,0:T(1,128)S(1)} %get-tuple-element.200.refs_1_), channel_id=1, source_target_pairs={{0,1},{1,0},{2,3},{3,2},{4,5},{5,4},{6,7},{7,6},{8,9},{9,8},{10,11... | collective-permute-start | bytes 1544 | tf_op jit(solution)/shard_map/ppermute | solution.py:656

commit v4 on v3

--- a/solution.py
+++ b/solution.py
@@ -487,7 +487,7 @@
 
     def move(pieces, stride):
         moved = list(pieces)
-        for i in reversed(range(1, len(pieces))):
+        for i in range(1, len(pieces)) if stride > 1 else reversed(range(1, len(pieces))):
             perm = [(p, p ^ (i * stride)) for p in range(parts)]
             moved[i] = lax.ppermute(pieces[i], "parts", perm)
         return moved

time: 101 us -> 101 us (level)
  no operation moved by 1% of the time
where the time goes in v4:
time: 101 us
  Pallas kernels  51.7 us (51%)
  starting transfers between devices  39 us (39%)
  waiting for transfers between devices  9.03 us (9%)
  between operations  1.03 us (1%)
    pallas_call x31, Pallas kernels, run(): pl.pallas_call(body, name=name, in_specs=specs, out_specs=(VMEM if keep i...  51.7 us
    ppermute x12, starting transfers between devices, send(): lax.ppermute(leave, AXES, partners(self.parts, self.axes.pop(0)))  14.4 us
    ppermute x12, starting transfers between devices, move(): moved[i] = lax.ppermute(pieces[i], 'parts', perm)  14.1 us
    ppermute x12, waiting for transfers between devices, send(): lax.ppermute(leave, AXES, partners(self.parts, self.axes.pop(0)))  4.89 us
    ppermute x12, waiting for transfers between devices, move(): moved[i] = lax.ppermute(pieces[i], 'parts', perm)  4.12 us
    ppermute x1, starting transfers between devices, local(): bias_theirs = lax.ppermute(bias_mine, 'mp', SWAP)  3.97 us
    ppermute x1, starting transfers between devices, local(): bias_other = lax.ppermute(bias_own, 'mp', SWAP)  3.2 us
  transfers between devices with their start and end apart: 31, of which 4 were waited for; matrix products, arithmetic and copies ran while one was open for 0% of the time, Pallas kernels for 43%

profile of v4, /device:TPU:1, one launch (start us, length us, event | category | flops | bytes accessed | tf_op | source)
XLA Modules:
  0.0 100.8 jit_solution(15537056176093843352)
XLA Ops:
  0.7 2.8 %outgoing.1 = (bf16[768,2048]{1,0:T(8,128)(2,1)S(1)}, bf16[32,2048]{1,0:T(8,128)(2,1)S(1)}, bf16[32,2048]{1,0:T(8,128)(2,1)S(1)}, bf16[32,2048]{1,0:T(8,128)(2,1...) custom-call(s32[2]{0:T(128)S(1)} %pad_add_fusion.refs_0_, bf16[768,2048]{1,0:T(8,128)(2,1)} %bitcast.12, ...), custom_call_target="tpu_custom_call" | custom-call | flops 1 | bytes 1 | tf_op jit(solution)/shard_map/outgoing/pallas_call | solution.py:59
  3.6 2.2 %collective-permute-start.2 = (bf16[32,2048]{1,0:T(8,128)(2,1)S(1)}, bf16[32,2048]{1,0:T(8,128)(2,1)S(1)}, u32[]{:S(2)}, u32[]{:S(2)}) collective-permute-start(bf16[32,2048]{1,0:T(8,128)(2,1)S(1)} %get-tuple-element.113), channel_id=1, source_target_pairs={{0,8},{2,10},{4,12},{6,14},{8,0},{10,2},{12,4},{14,6},{16,24},{18,... | collective-permute-start | bytes 393224 | tf_op jit(solution)/shard_map/ppermute | solution.py:492
  5.8 2.3 %collective-permute-start.3 = (bf16[32,2048]{1,0:T(8,128)(2,1)S(1)}, bf16[32,2048]{1,0:T(8,128)(2,1)S(1)}, u32[]{:S(2)}, u32[]{:S(2)}) collective-permute-start(bf16[32,2048]{1,0:T(8,128)(2,1)S(1)} %get-tuple-element.114), channel_id=1, source_target_pairs={{0,16},{2,18},{4,20},{6,22},{8,24},{10,26},{12,28},{14,30},{16,0},... | collective-permute-start | bytes 393224 | tf_op jit(solution)/shard_map/ppermute | solution.py:492
  8.1 1.2 %collective-permute-start = (bf16[1024,2048]{1,0:T(8,128)(2,1)}, bf16[1024,2048]{1,0:T(8,128)(2,1)S(1)}, u32[]{:S(2)}, u32[]{:S(2)}) collective-permute-start(bf16[1024,2048]{1,0:T(8,128)(2,1)} %refs_1_.1), channel_id=1, source_target_pairs={{0,1},{1,0},{2,3},{3,2},{4,5},{5,4},{6,7},{7,6},{8,9},{9,8},{10,11... | collective-permute-start | bytes 12582920 | tf_op jit(solution)/shard_map/ppermute | solution.py:501
  9.3 4.0 %mix.1 = (bf16[2,768,1024]{2,1,0:T(8,128)(2,1)S(1)}, bf16[2048,768]{1,0:T(8,128)(2,1)S(1)}, f32[768,1]{1,0:T(8,128)S(1)}, f32[8,768]{1,0:T(8,128)S(1)}, bf16[2,3...) custom-call(s32[2]{0:T(128)S(1)} %pad_add_fusion.refs_0_, ...), custom_call_target="tpu_custom_call" | custom-call | flops 60000002048 | bytes 1 | tf_op jit(solution)/shard_map/mix/pallas_call | solution.py:59
  13.3 4.0 %pre_own.1 = (f32[768,2048]{1,0:T(8,128)S(1)}, f32[8,128]{1,0:T(8,128)S(1)}) custom-call(s32[2]{0:T(128)S(1)} %pad_add_fusion.refs_0_, bf16[2,768,1024]{2,1,0:T(8,128)(2,1)S(1)} %get-tuple-element.116.refs_1_.refs_2_, bf16[1024,2048]{1,0:T(8,128)(2,1)S(1)} %get-tuple-element.111.refs_2_.refs_1_.refs_4_, f32[8,128]{1,0:T(8,128)S(1)} %get-tuple-element.117.refs_3_), custom_call_target="tpu_custom_call" | custom-call | flops 1 | bytes 1 | tf_op jit(solution)/shard_map/pre_own/pallas_call | solution.py:59
  17.4 1.5 %collective-permute-start.5 = (bf16[32,2048]{1,0:T(8,128)(2,1)S(1)}, bf16[32,2048]{1,0:T(8,128)(2,1)S(1)}, u32[]{:S(2)}, u32[]{:S(2)}) collective-permute-start(bf16[32,2048]{1,0:T(8,128)(2,1)S(1)} %get-tuple-element.120), channel_id=1, source_target_pairs={{0,2},{2,0},{4,6},{6,4},{8,10},{10,8},{12,14},{14,12},{16,18},{18,... | collective-permute-start | bytes 393224 | tf_op jit(solution)/shard_map/ppermute | solution.py:492
  18.8 1.2 %collective-permute-start.6 = (bf16[32,2048]{1,0:T(8,128)(2,1)S(1)}, bf16[32,2048]{1,0:T(8,128)(2,1)S(1)}, u32[]{:S(2)}, u32[]{:S(2)}) collective-permute-start(bf16[32,2048]{1,0:T(8,128)(2,1)S(1)} %get-tuple-element.121), channel_id=1, source_target_pairs={{0,4},{2,6},{4,0},{6,2},{8,12},{10,14},{12,8},{14,10},{16,20},{18,... | collective-permute-start | bytes 393224 | tf_op jit(solution)/shard_map/ppermute | solution.py:492
  20.1 3.2 %collective-permute-start.1 = (bf16[1,1024]{1,0:T(2,128)(2,1)S(1)}, bf16[1,1024]{1,0:T(2,128)(2,1)S(1)}, u32[]{:S(2)}, u32[]{:S(2)}) collective-permute-start(bf16[1,1024]{1,0:T(2,128)(2,1)S(1)} %reshape.27.refs_3_), channel_id=1, source_target_pairs={{0,1},{1,0},{2,3},{3,2},{4,5},{5,4},{6,7},{7,6},{8,9},{9,8},{10,11... | collective-permute-start | bytes 6152 | tf_op jit(solution)/shard_map/ppermute | solution.py:503
  23.3 4.0 %pre_other.1 = (f32[768,2048]{1,0:T(8,128)S(1)}, f32[8,128]{1,0:T(8,128)S(1)}) custom-call(s32[2]{0:T(128)S(1)} %pad_add_fusion.refs_0_, f32[768,2048]{1,0:T(8,128)S(1)} %get-tuple-element.123.refs_1_, bf16[2,768,1024]{2,1,0:T(8,128)(2,1)S(1)} %get-tuple-element.116.refs_1_.refs_2_, ...), custom_call_target="tpu_custom_call" | custom-call | flops 1 | bytes 1 | tf_op jit(solution)/shard_map/pre_other/pallas_call | solution.py:59
  27.3 1.9 %remote_product.1 = (bf16[256,2048]{1,0:T(8,128)(2,1)S(1)}, f32[1,2048]{1,0:T(1,128)S(1)}, f32[8,128]{1,0:T(8,128)S(1)}) custom-call(s32[2]{0:T(128)S(1)} %pad_add_fusion.refs_0_, bf16[1024,2048]{1,0:T(8,128)(2,1)S(1)} %get-tuple-element.111.refs_2_.refs_1_.refs_4_, bf16[1024,2048]{1,0:T(8,128)(2,1)S(1)} %collective-permute-done.refs_3_.refs_2_.refs_1_.refs_5_, ...), custom_call_target="tpu_custom_call" | custom-call | flops 1 | bytes 1 | tf_op jit(solution)/shard_map/remote_product/pallas_call | solution.py:59
  29.2 1.9 %finish_mixed.1 = (bf16[1024,768]{1,0:T(8,128)(2,1)S(1)}, bf16[1024,768]{1,0:T(8,128)(2,1)S(1)}, f32[8,128]{1,0:T(8,128)S(1)}) custom-call(s32[2]{0:T(128)S(1)} %pad_add_fusion.refs_0_, s32[1,128]{1,0:T(1,128)S(1)} %get-tuple-element.109.refs_1_.refs_0_, f32[8,768]{1,0:T(8,128)S(1)} %get-tuple-element.129.refs_2_, ...), custom_call_target="tpu_custom_call" | custom-call | flops 1 | bytes 1 | tf_op jit(solution)/shard_map/finish_mixed/pallas_call | solution.py:59
  31.2 1.4 %collective-permute-start.8 = (bf16[1024,768]{1,0:T(8,128)(2,1)S(1)}, bf16[1024,768]{1,0:T(8,128)(2,1)S(1)}, u32[]{:S(2)}, u32[]{:S(2)}) collective-permute-start(bf16[1024,768]{1,0:T(8,128)(2,1)S(1)} %get-tuple-element.144), channel_id=1, source_target_pairs={{0,1},{1,0},{2,3},{3,2},{4,5},{5,4},{6,7},{7,6},{8,9},{9,8},{10,11... | collective-permute-start | bytes 4718600 | tf_op jit(solution)/shard_map/ppermute | solution.py:623
  32.5 3.5 %gelu.3 = (bf16[768,2048]{1,0:T(8,128)(2,1)}, bf16[768,1024]{1,0:T(8,128)(2,1)S(1)}, f32[1,1024]{1,0:T(1,128)S(1)}, f32[8,128]{1,0:T(8,128)S(1)}) custom-call(s32[1,128]{1,0:T(1,128)S(1)} %get-tuple-element.109.refs_1_.refs_0_, f32[768,1]{1,0:T(8,128)S(1)} %get-tuple-element.110.refs_1_.refs_0_, bf16[256,2048]{1,0:T(8,128)(2,1)S(1)} %get-tuple-element.126.refs_2_, ...), custom_call_target="tpu_custom_call" | custom-call | flops 1000000000 | bytes 1 | tf_op jit(solution)/shard_map/gelu/pallas_call | solution.py:59
  36.1 2.9 %gelu.4 = (bf16[768,2048]{1,0:T(8,128)(2,1)}, bf16[768,768]{1,0:T(8,128)(2,1)S(1)}, f32[1,768]{1,0:T(1,128)S(1)}, f32[8,128]{1,0:T(8,128)S(1)}) custom-call(s32[1,128]{1,0:T(1,128)S(1)} %get-tuple-element.109.refs_1_.refs_0_, f32[768,1]{1,0:T(8,128)S(1)} %get-tuple-element.110.refs_1_.refs_0_, ...), custom_call_target="tpu_custom_call", output_to_operand_aliasing={{0}: (6, {})} | custom-call | flops 4000000000 | bytes 1 | tf_op jit(solution)/shard_map/gelu/pallas_call | solution.py:59
  39.0 0.6 collective-permute-start.15
  39.6 1.5 %gelu.5 = (bf16[768,2048]{1,0:T(8,128)(2,1)}, bf16[768,256]{1,0:T(8,128)(2,1)S(1)}, f32[1,256]{1,0:T(1,128)S(1)}, f32[8,128]{1,0:T(8,128)S(1)}) custom-call(s32[1,128]{1,0:T(1,128)S(1)} %get-tuple-element.109.refs_1_.refs_0_, f32[768,1]{1,0:T(8,128)S(1)} %get-tuple-element.110.refs_1_.refs_0_, ...), custom_call_target="tpu_custom_call", output_to_operand_aliasing={{0}: (6, {})} | custom-call | flops 1 | bytes 1 | tf_op jit(solution)/shard_map/gelu/pallas_call | solution.py:59
  41.1 1.2 %sent_grads.1 = (bf16[32,2176]{1,0:T(8,128)(2,1)S(1)}, bf16[32,2176]{1,0:T(8,128)(2,1)S(1)}, bf16[32,2176]{1,0:T(8,128)(2,1)S(1)}, bf16[32,2176]{1,0:T(8,128)(2,1)S(1)}, f32[8,128]{1,0:T(8,128)S(1)}) custom-call(s32[2]{0:T(128)S(1)} %pad_add_fusion.refs_0_, s32[1,128]{1,0:T(1,128)S(1)} %get-tuple-element.145.refs_1_, ...), custom_call_target="tpu_custom_call" | custom-call | flops 8000000000 | bytes 1 | tf_op jit(solution)/shard_map/sent_grads/pallas_call | solution.py:59
  42.3 3.4 %grad.3 = (bf16[512,1024]{1,0:T(8,128)(2,1)S(1)}, bf16[512,1024]{1,0:T(8,128)(2,1)S(1)}, f32[8,128]{1,0:T(8,128)S(1)}) custom-call(bf16[1024,768]{1,0:T(8,128)(2,1)S(1)} %get-tuple-element.143.refs_0_, bf16[1024,768]{1,0:T(8,128)(2,1)S(1)} %collective-permute-done.8.refs_1_, bf16[768,1024]{1,0:T(8,128)(2,1)S(1)} %get-tuple-element.140.refs_3_.refs_2_, ...), custom_call_target="tpu_custom_call" | custom-call | flops 16000000000 | bytes 1 | tf_op jit(solution)/shard_map/grad/pallas_call | solution.py:59
  45.7 0.7 collective-permute-start.10
  46.5 1.7 %collective-permute-start.11 = (bf16[32,2176]{1,0:T(8,128)(2,1)S(1)}, bf16[32,2176]{1,0:T(8,128)(2,1)S(1)}, u32[]{:S(2)}, u32[]{:S(2)}) collective-permute-start(bf16[32,2176]{1,0:T(8,128)(2,1)S(1)} %get-tuple-element.154), channel_id=1, source_target_pairs={{0,8},{2,10},{4,12},{6,14},{8,0},{10,2},{12,4},{14,6},{16,24},{18,... | collective-permute-start | bytes 417800 | tf_op jit(solution)/shard_map/ppermute | solution.py:492
  48.2 1.4 %collective-permute-start.12 = (bf16[32,2176]{1,0:T(8,128)(2,1)S(1)}, bf16[32,2176]{1,0:T(8,128)(2,1)S(1)}, u32[]{:S(2)}, u32[]{:S(2)}) collective-permute-start(bf16[32,2176]{1,0:T(8,128)(2,1)S(1)} %get-tuple-element.155), channel_id=1, source_target_pairs={{0,16},{2,18},{4,20},{6,22},{8,24},{10,26},{12,28},{14,30},{16,0},... | collective-permute-start | bytes 417800 | tf_op jit(solution)/shard_map/ppermute | solution.py:492
  49.6 1.1 %collective-permute-start.13 = (bf16[32,2176]{1,0:T(8,128)(2,1)S(1)}, bf16[32,2176]{1,0:T(8,128)(2,1)S(1)}, u32[]{:S(2)}, u32[]{:S(2)}) collective-permute-start(bf16[32,2176]{1,0:T(8,128)(2,1)S(1)} %get-tuple-element.156), channel_id=1, source_target_pairs={{0,24},{2,26},{4,28},{6,30},{8,16},{10,18},{12,20},{14,22},{16,8},... | collective-permute-start | bytes 417800 | tf_op jit(solution)/shard_map/ppermute | solution.py:492
  50.7 2.7 %grad.4 = (bf16[512,768]{1,0:T(8,128)(2,1)S(1)}, bf16[512,768]{1,0:T(8,128)(2,1)S(1)}, f32[8,128]{1,0:T(8,128)S(1)}) custom-call(bf16[1024,768]{1,0:T(8,128)(2,1)S(1)} %get-tuple-element.143.refs_0_, bf16[1024,768]{1,0:T(8,128)(2,1)S(1)} %collective-permute-done.8.refs_1_, bf16[768,768]{1,0:T(8,128)(2,1)S(1)} %get-tuple-element.141.refs_4_.refs_2_.refs_3_, ...), custom_call_target="tpu_custom_call" | custom-call | flops 1 | bytes 1 | tf_op jit(solution)/shard_map/grad/pallas_call | solution.py:59
  53.4 1.0 collective-permute-start.17
  54.4 1.0 grad.5
  55.4 0.5 collective-permute-start.18
  55.9 4.1 %collective-permute-done.13.refs_3_ = bf16[32,2176]{1,0:T(8,128)(2,1)S(1)} collective-permute-done((bf16[32,2176]{1,0:T(8,128)(2,1)S(1)}, bf16[32,2176]{1,0:T(8,128)(2,1)S(1)}, u32[]{:S(2)}, u32[]{:S(2)}) %collective-permute-start.13) | collective-permute-done | bytes 139296 | tf_op jit(solution)/shard_map/ppermute | solution.py:492
  60.0 0.2 halve.9
  60.3 1.7 %collective-permute-start.16 = (bf16[256,1024]{1,0:T(8,128)(2,1)S(1)}, bf16[256,1024]{1,0:T(8,128)(2,1)S(1)}, u32[]{:S(2)}, u32[]{:S(2)}) collective-permute-start(bf16[256,1024]{1,0:T(8,128)(2,1)S(1)} %get-tuple-element.164), channel_id=1, source_target_pairs={{0,4},{1,3},{2,6},{3,1},{4,0},{5,7},{6,2},{7,5},{8,12},{9,11},{10,... | collective-permute-start | bytes 1572872 | tf_op jit(solution)/shard_map/ppermute | solution.py:416
  62.0 3.5 %back.2 = (bf16[768,1024]{1,0:T(8,128)(2,1)S(1)}, f32[8,128]{1,0:T(8,128)S(1)}) custom-call(f32[768,1]{1,0:T(8,128)S(1)} %get-tuple-element.110.refs_1_.refs_0_, bf16[1024,2048]{1,0:T(8,128)(2,1)S(1)} %get-tuple-element.111.refs_2_.refs_1_.refs_4_, bf16[768,1024]{1,0:T(8,128)(2,1)S(1)} %get-tuple-element.140.refs_3_.refs_2_, ...), custom_call_target="tpu_custom_call" | custom-call | flops 1 | bytes 1 | tf_op jit(solution)/shard_map/back/pallas_call | solution.py:59
  65.5 0.6 collective-permute-done.18.refs_1_
  66.2 3.6 %collective-permute-start.21 = (bf16[256,256]{1,0:T(8,128)(2,1)S(1)}, bf16[256,256]{1,0:T(8,128)(2,1)S(1)}, u32[]{:S(2)}, u32[]{:S(2)}) collective-permute-start(bf16[256,256]{1,0:T(8,128)(2,1)S(1)} %get-tuple-element.182), channel_id=1, source_target_pairs={{0,16},{1,17},{2,18},{3,19},{4,20},{5,21},{6,22},{7,23},{8,24},{9,... | collective-permute-start | bytes 393224 | tf_op jit(solution)/shard_map/ppermute | solution.py:416
  69.8 0.5 collective-permute-done.17.refs_1_
  70.5 3.7 %collective-permute-done.16.refs_1_ = bf16[256,1024]{1,0:T(8,128)(2,1)S(1)} collective-permute-done((bf16[256,1024]{1,0:T(8,128)(2,1)S(1)}, bf16[256,1024]{1,0:T(8,128)(2,1)S(1)}, u32[]{:S(2)}, u32[]{:S(2)}) %collective-permute-start.16) | collective-permute-done | bytes 524320 | tf_op jit(solution)/shard_map/ppermute | solution.py:416
  74.4 1.5 %collective-permute-start.23 = (bf16[128,1024]{1,0:T(8,128)(2,1)S(1)}, bf16[128,1024]{1,0:T(8,128)(2,1)S(1)}, u32[]{:S(2)}, u32[]{:S(2)}) collective-permute-start(bf16[128,1024]{1,0:T(8,128)(2,1)S(1)} %get-tuple-element.187), channel_id=1, source_target_pairs={{0,8},{1,9},{2,10},{3,11},{4,12},{5,13},{6,14},{7,15},{8,0},{9,1},... | collective-permute-start | bytes 786440 | tf_op jit(solution)/shard_map/ppermute | solution.py:416
  75.8 3.7 %back.3 = (bf16[768,1024]{1,0:T(8,128)(2,1)S(1)}, f32[8,128]{1,0:T(8,128)S(1)}) custom-call(f32[768,1]{1,0:T(8,128)S(1)} %get-tuple-element.110.refs_1_.refs_0_, bf16[1024,2048]{1,0:T(8,128)(2,1)S(1)} %collective-permute-done.refs_3_.refs_2_.refs_1_.refs_5_, bf16[768,1024]{1,0:T(8,128)(2,1)S(1)} %get-tuple-element.140.refs_3_.refs_2_, ...), custom_call_target="tpu_custom_call" | custom-call | flops 1000000000 | bytes 1 | tf_op jit(solution)/shard_map/back/pallas_call | solution.py:59
  79.5 1.0 input_local.2
  80.8 0.7 collective-permute-start.22
  81.6 0.9 collective-permute-start.24
  82.7 1.5 %collective-permute-start.26 = (bf16[32,2176]{1,0:T(8,128)(2,1)S(1)}, bf16[32,2176]{1,0:T(8,128)(2,1)S(1)}, u32[]{:S(2)}, u32[]{:S(2)}) collective-permute-start(bf16[32,2176]{1,0:T(8,128)(2,1)S(1)} %get-tuple-element.196), channel_id=1, source_target_pairs={{0,6},{2,4},{4,2},{6,0},{8,14},{10,12},{12,10},{14,8},{16,22},{18,... | collective-permute-start | bytes 417800 | tf_op jit(solution)/shard_map/ppermute | solution.py:492
  84.3 2.8 %collective-permute-start.28 = (bf16[64,1024]{1,0:T(8,128)(2,1)S(1)}, bf16[64,1024]{1,0:T(8,128)(2,1)S(1)}, u32[]{:S(2)}, u32[]{:S(2)}) collective-permute-start(bf16[64,1024]{1,0:T(8,128)(2,1)S(1)} %get-tuple-element.202), channel_id=1, source_target_pairs={{0,16},{1,17},{2,18},{3,19},{4,20},{5,21},{6,22},{7,23},{8,24},{9,... | collective-permute-start | bytes 393224 | tf_op jit(solution)/shard_map/ppermute | solution.py:416
  87.2 0.2 collective-permute-start.29
  87.4 1.4 %collective-permute-start.30 = (bf16[64,256]{1,0:T(8,128)(2,1)S(1)}, bf16[64,256]{1,0:T(8,128)(2,1)S(1)}, u32[]{:S(2)}, u32[]{:S(2)}) collective-permute-start(bf16[64,256]{1,0:T(8,128)(2,1)S(1)} %get-tuple-element.206), channel_id=1, source_target_pairs={{0,4},{1,3},{2,6},{3,1},{4,0},{5,7},{6,2},{7,5},{8,12},{9,11},{10,... | collective-permute-start | bytes 98312 | tf_op jit(solution)/shard_map/ppermute | solution.py:416
  88.8 1.0 input_local.3
  89.9 4.0 %collective-permute-start.27 = (f32[1,128]{1,0:T(1,128)S(1)}, f32[1,128]{1,0:T(1,128)S(1)}, u32[]{:S(2)}, u32[]{:S(2)}) collective-permute-start(f32[1,128]{1,0:T(1,128)S(1)} %get-tuple-element.200.refs_1_), channel_id=1, source_target_pairs={{0,1},{1,0},{2,3},{3,2},{4,5},{5,4},{6,7},{7,6},{8,9},{9,8},{10,11... | collective-permute-start | bytes 1544 | tf_op jit(solution)/shard_map/ppermute | solution.py:656
  93.8 5.6 %input_gradient.1 = (bf16[768,2048]{1,0:T(8,128)(2,1)}, f32[8,128]{1,0:T(8,128)S(1)}) custom-call(s32[2]{0:T(128)S(1)} %pad_add_fusion.refs_0_, s32[1,128]{1,0:T(1,128)S(1)} %get-tuple-element.138.refs_1_, f32[768,1024]{1,0:T(8,128)S(1)} %get-tuple-element.174.refs_2_, f32[768,1024]{1,0:T(8,128)S(1)} %get-tuple-element.192.refs_3_, ...), custom_call_target="tpu_custom_call" | custom-call | flops 1 | bytes 1 | tf_op jit(solution)/shard_map/input_gradient/pallas_call | solution.py:59
  99.4 1.4 %last_sum.1 = (f32[64,2048]{1,0:T(8,128)}, f32[1,64]{1,0:T(1,128)}, f32[8,128]{1,0:T(8,128)}) custom-call(s32[2]{0:T(128)S(1)} %pad_add_fusion.refs_0_, f32[1,128]{1,0:T(1,128)S(1)} %get-tuple-element.200.refs_1_, f32[1,128]{1,0:T(1,128)S(1)} %collective-permute-done.27.refs_2_, bf16[64,1024]{1,0:T(8,128)(2,1)S(1)} %get-tuple-element.201.refs_3_, ...), custom_call_target="tpu_custom_call" | custom-call | flops 1 | bytes 1 | tf_op jit(solution)/shard_map/last_sum/pallas_call | solution.py:59
  (51 shorter events, 1.4 us)
Async XLA Ops:
  3.6 13.7 %collective-permute-start.2 = (bf16[32,2048]{1,0:T(8,128)(2,1)S(1)}, bf16[32,2048]{1,0:T(8,128)(2,1)S(1)}, u32[]{:S(2)}, u32[]{:S(2)}) collective-permute-start(bf16[32,2048]{1,0:T(8,128)(2,1)S(1)} %get-tuple-element.113), channel_id=1, source_target_pairs={{0,8},{2,10},{4,12},{6,14},{8,0},{10,2},{12,4},{14,6},{16,24},{18,... | collective-permute-start | bytes 393224 | tf_op jit(solution)/shard_map/ppermute | solution.py:492
  5.8 11.5 %collective-permute-start.3 = (bf16[32,2048]{1,0:T(8,128)(2,1)S(1)}, bf16[32,2048]{1,0:T(8,128)(2,1)S(1)}, u32[]{:S(2)}, u32[]{:S(2)}) collective-permute-start(bf16[32,2048]{1,0:T(8,128)(2,1)S(1)} %get-tuple-element.114), channel_id=1, source_target_pairs={{0,16},{2,18},{4,20},{6,22},{8,24},{10,26},{12,28},{14,30},{16,0},... | collective-permute-start | bytes 393224 | tf_op jit(solution)/shard_map/ppermute | solution.py:492
  8.1 9.2 %collective-permute-start.4 = (bf16[32,2048]{1,0:T(8,128)(2,1)S(1)}, bf16[32,2048]{1,0:T(8,128)(2,1)S(1)}, u32[]{:S(2)}, u32[]{:S(2)}) collective-permute-start(bf16[32,2048]{1,0:T(8,128)(2,1)S(1)} %get-tuple-element.115), channel_id=1, source_target_pairs={{0,24},{2,26},{4,28},{6,30},{8,16},{10,18},{12,20},{14,22},{16,8},... | collective-permute-start | bytes 393224 | tf_op jit(solution)/shard_map/ppermute | solution.py:492
  8.1 15.2 %collective-permute-start = (bf16[1024,2048]{1,0:T(8,128)(2,1)}, bf16[1024,2048]{1,0:T(8,128)(2,1)S(1)}, u32[]{:S(2)}, u32[]{:S(2)}) collective-permute-start(bf16[1024,2048]{1,0:T(8,128)(2,1)} %refs_1_.1), channel_id=1, source_target_pairs={{0,1},{1,0},{2,3},{3,2},{4,5},{5,4},{6,7},{7,6},{8,9},{9,8},{10,11... | collective-permute-start | bytes 12582920 | tf_op jit(solution)/shard_map/ppermute | solution.py:501
  13.3 6.8 %copy-start.1 = (bf16[1024]{0:T(1024)(128)(2,1)S(1)}, bf16[1024]{0:T(1024)(128)(2,1)}, u32[]{:S(2)}) copy-start(bf16[1024]{0:T(1024)(128)(2,1)} %param.9) | copy-start | bytes 6148
  17.4 9.9 %collective-permute-start.5 = (bf16[32,2048]{1,0:T(8,128)(2,1)S(1)}, bf16[32,2048]{1,0:T(8,128)(2,1)S(1)}, u32[]{:S(2)}, u32[]{:S(2)}) collective-permute-start(bf16[32,2048]{1,0:T(8,128)(2,1)S(1)} %get-tuple-element.120), channel_id=1, source_target_pairs={{0,2},{2,0},{4,6},{6,4},{8,10},{10,8},{12,14},{14,12},{16,18},{18,... | collective-permute-start | bytes 393224 | tf_op jit(solution)/shard_map/ppermute | solution.py:492
  18.8 8.5 %collective-permute-start.6 = (bf16[32,2048]{1,0:T(8,128)(2,1)S(1)}, bf16[32,2048]{1,0:T(8,128)(2,1)S(1)}, u32[]{:S(2)}, u32[]{:S(2)}) collective-permute-start(bf16[32,2048]{1,0:T(8,128)(2,1)S(1)} %get-tuple-element.121), channel_id=1, source_target_pairs={{0,4},{2,6},{4,0},{6,2},{8,12},{10,14},{12,8},{14,10},{16,20},{18,... | collective-permute-start | bytes 393224 | tf_op jit(solution)/shard_map/ppermute | solution.py:492
  20.1 7.2 %collective-permute-start.7 = (bf16[32,2048]{1,0:T(8,128)(2,1)S(1)}, bf16[32,2048]{1,0:T(8,128)(2,1)S(1)}, u32[]{:S(2)}, u32[]{:S(2)}) collective-permute-start(bf16[32,2048]{1,0:T(8,128)(2,1)S(1)} %get-tuple-element.122), channel_id=1, source_target_pairs={{0,6},{2,4},{4,2},{6,0},{8,14},{10,12},{12,10},{14,8},{16,22},{18,... | collective-permute-start | bytes 393224 | tf_op jit(solution)/shard_map/ppermute | solution.py:492
  20.1 7.2 %collective-permute-start.1 = (bf16[1,1024]{1,0:T(2,128)(2,1)S(1)}, bf16[1,1024]{1,0:T(2,128)(2,1)S(1)}, u32[]{:S(2)}, u32[]{:S(2)}) collective-permute-start(bf16[1,1024]{1,0:T(2,128)(2,1)S(1)} %reshape.27.refs_3_), channel_id=1, source_target_pairs={{0,1},{1,0},{2,3},{3,2},{4,5},{5,4},{6,7},{7,6},{8,9},{9,8},{10,11... | collective-permute-start | bytes 6152 | tf_op jit(solution)/shard_map/ppermute | solution.py:503
  29.2 3.3 %copy-start = (bf16[2,384,2048]{2,1,0:T(8,128)(2,1)S(1)}, bf16[2,384,2048]{2,1,0:T(8,128)(2,1)}, u32[]{:S(2)}) copy-start(bf16[2,384,2048]{2,1,0:T(8,128)(2,1)} %param.13) | copy-start | bytes 9437188
  31.2 11.1 %collective-permute-start.8 = (bf16[1024,768]{1,0:T(8,128)(2,1)S(1)}, bf16[1024,768]{1,0:T(8,128)(2,1)S(1)}, u32[]{:S(2)}, u32[]{:S(2)}) collective-permute-start(bf16[1024,768]{1,0:T(8,128)(2,1)S(1)} %get-tuple-element.144), channel_id=1, source_target_pairs={{0,1},{1,0},{2,3},{3,2},{4,5},{5,4},{6,7},{7,6},{8,9},{9,8},{10,11... | collective-permute-start | bytes 4718600 | tf_op jit(solution)/shard_map/ppermute | solution.py:623
  36.1 6.2 %collective-permute-start.9 = (bf16[768,1024]{1,0:T(8,128)(2,1)S(1)}, bf16[768,1024]{1,0:T(8,128)(2,1)S(1)}, u32[]{:S(2)}, u32[]{:S(2)}) collective-permute-start(bf16[768,1024]{1,0:T(8,128)(2,1)S(1)} %get-tuple-element.140.refs_3_.refs_2_), channel_id=1, source_target_pairs={{0,1},{1,0},{2,3},{3,2},{4,5},{5,4},{6,7},{7,6},{8,9},{9,8},{10,11... | collective-permute-start | bytes 4718600 | tf_op jit(solution)/shard_map/ppermute | solution.py:584
  39.0 10.6 %collective-permute-start.15 = (bf16[768,768]{1,0:T(8,128)(2,1)S(1)}, bf16[768,768]{1,0:T(8,128)(2,1)S(1)}, u32[]{:S(2)}, u32[]{:S(2)}) collective-permute-start(bf16[768,768]{1,0:T(8,128)(2,1)S(1)} %get-tuple-element.141.refs_4_.refs_2_.refs_3_), channel_id=1, source_target_pairs={{0,1},{1,0},{2,3},{3,2},{4,5},{5,4},{6,7},{7,6},{8,9},{9,8},{10,11... | collective-permute-start | bytes 3538952 | tf_op jit(solution)/shard_map/ppermute | solution.py:584
  45.7 14.3 %collective-permute-start.10 = (bf16[512,1024]{1,0:T(8,128)(2,1)S(1)}, bf16[512,1024]{1,0:T(8,128)(2,1)S(1)}, u32[]{:S(2)}, u32[]{:S(2)}) collective-permute-start(bf16[512,1024]{1,0:T(8,128)(2,1)S(1)} %get-tuple-element.152), channel_id=1, source_target_pairs={{0,2},{1,5},{2,0},{3,7},{4,6},{5,1},{6,4},{7,3},{8,10},{9,13},{10,... | collective-permute-start | bytes 3145736 | tf_op jit(solution)/shard_map/ppermute | solution.py:416
  46.5 6.9 %collective-permute-start.14 = (bf16[768,256]{1,0:T(8,128)(2,1)S(1)}, bf16[768,256]{1,0:T(8,128)(2,1)S(1)}, u32[]{:S(2)}, u32[]{:S(2)}) collective-permute-start(bf16[768,256]{1,0:T(8,128)(2,1)S(1)} %get-tuple-element.142.refs_5_.refs_2_.refs_4_), channel_id=1, source_target_pairs={{0,1},{1,0},{2,3},{3,2},{4,5},{5,4},{6,7},{7,6},{8,9},{9,8},{10,11... | collective-permute-start | bytes 1179656 | tf_op jit(solution)/shard_map/ppermute | solution.py:584
  46.5 8.9 %collective-permute-start.11 = (bf16[32,2176]{1,0:T(8,128)(2,1)S(1)}, bf16[32,2176]{1,0:T(8,128)(2,1)S(1)}, u32[]{:S(2)}, u32[]{:S(2)}) collective-permute-start(bf16[32,2176]{1,0:T(8,128)(2,1)S(1)} %get-tuple-element.154), channel_id=1, source_target_pairs={{0,8},{2,10},{4,12},{6,14},{8,0},{10,2},{12,4},{14,6},{16,24},{18,... | collective-permute-start | bytes 417800 | tf_op jit(solution)/shard_map/ppermute | solution.py:492
  48.2 7.7 %collective-permute-start.12 = (bf16[32,2176]{1,0:T(8,128)(2,1)S(1)}, bf16[32,2176]{1,0:T(8,128)(2,1)S(1)}, u32[]{:S(2)}, u32[]{:S(2)}) collective-permute-start(bf16[32,2176]{1,0:T(8,128)(2,1)S(1)} %get-tuple-element.155), channel_id=1, source_target_pairs={{0,16},{2,18},{4,20},{6,22},{8,24},{10,26},{12,28},{14,30},{16,0},... | collective-permute-start | bytes 417800 | tf_op jit(solution)/shard_map/ppermute | solution.py:492
  49.6 10.4 %collective-permute-start.13 = (bf16[32,2176]{1,0:T(8,128)(2,1)S(1)}, bf16[32,2176]{1,0:T(8,128)(2,1)S(1)}, u32[]{:S(2)}, u32[]{:S(2)}) collective-permute-start(bf16[32,2176]{1,0:T(8,128)(2,1)S(1)} %get-tuple-element.156), channel_id=1, source_target_pairs={{0,24},{2,26},{4,28},{6,30},{8,16},{10,18},{12,20},{14,22},{16,8},... | collective-permute-start | bytes 417800 | tf_op jit(solution)/shard_map/ppermute | solution.py:492
  53.4 16.9 %collective-permute-start.17 = (bf16[512,768]{1,0:T(8,128)(2,1)S(1)}, bf16[512,768]{1,0:T(8,128)(2,1)S(1)}, u32[]{:S(2)}, u32[]{:S(2)}) collective-permute-start(bf16[512,768]{1,0:T(8,128)(2,1)S(1)} %get-tuple-element.166), channel_id=1, source_target_pairs={{0,2},{1,5},{2,0},{3,7},{4,6},{5,1},{6,4},{7,3},{8,10},{9,13},{10,... | collective-permute-start | bytes 2359304 | tf_op jit(solution)/shard_map/ppermute | solution.py:416
  55.4 10.8 %collective-permute-start.18 = (bf16[512,256]{1,0:T(8,128)(2,1)S(1)}, bf16[512,256]{1,0:T(8,128)(2,1)S(1)}, u32[]{:S(2)}, u32[]{:S(2)}) collective-permute-start(bf16[512,256]{1,0:T(8,128)(2,1)S(1)} %get-tuple-element.168), channel_id=1, source_target_pairs={{0,8},{1,9},{2,10},{3,11},{4,12},{5,13},{6,14},{7,15},{8,0},{9,1},... | collective-permute-start | bytes 786440 | tf_op jit(solution)/shard_map/ppermute | solution.py:416
  60.3 14.0 %collective-permute-start.16 = (bf16[256,1024]{1,0:T(8,128)(2,1)S(1)}, bf16[256,1024]{1,0:T(8,128)(2,1)S(1)}, u32[]{:S(2)}, u32[]{:S(2)}) collective-permute-start(bf16[256,1024]{1,0:T(8,128)(2,1)S(1)} %get-tuple-element.164), channel_id=1, source_target_pairs={{0,4},{1,3},{2,6},{3,1},{4,0},{5,7},{6,2},{7,5},{8,12},{9,11},{10,... | collective-permute-start | bytes 1572872 | tf_op jit(solution)/shard_map/ppermute | solution.py:416
  66.2 14.6 %collective-permute-start.21 = (bf16[256,256]{1,0:T(8,128)(2,1)S(1)}, bf16[256,256]{1,0:T(8,128)(2,1)S(1)}, u32[]{:S(2)}, u32[]{:S(2)}) collective-permute-start(bf16[256,256]{1,0:T(8,128)(2,1)S(1)} %get-tuple-element.182), channel_id=1, source_target_pairs={{0,16},{1,17},{2,18},{3,19},{4,20},{5,21},{6,22},{7,23},{8,24},{9,... | collective-permute-start | bytes 393224 | tf_op jit(solution)/shard_map/ppermute | solution.py:416
  70.5 10.1 %collective-permute-start.19 = (bf16[256,768]{1,0:T(8,128)(2,1)S(1)}, bf16[256,768]{1,0:T(8,128)(2,1)S(1)}, u32[]{:S(2)}, u32[]{:S(2)}) collective-permute-start(bf16[256,768]{1,0:T(8,128)(2,1)S(1)} %get-tuple-element.177), channel_id=1, source_target_pairs={{0,4},{1,3},{2,6},{3,1},{4,0},{5,7},{6,2},{7,5},{8,12},{9,11},{10,... | collective-permute-start | bytes 1179656 | tf_op jit(solution)/shard_map/ppermute | solution.py:416
  74.4 8.3 %collective-permute-start.23 = (bf16[128,1024]{1,0:T(8,128)(2,1)S(1)}, bf16[128,1024]{1,0:T(8,128)(2,1)S(1)}, u32[]{:S(2)}, u32[]{:S(2)}) collective-permute-start(bf16[128,1024]{1,0:T(8,128)(2,1)S(1)} %get-tuple-element.187), channel_id=1, source_target_pairs={{0,8},{1,9},{2,10},{3,11},{4,12},{5,13},{6,14},{7,15},{8,0},{9,1},... | collective-permute-start | bytes 786440 | tf_op jit(solution)/shard_map/ppermute | solution.py:416
  80.6 6.5 %collective-permute-start.20 = (bf16[128,768]{1,0:T(8,128)(2,1)S(1)}, bf16[128,768]{1,0:T(8,128)(2,1)S(1)}, u32[]{:S(2)}, u32[]{:S(2)}) collective-permute-start(bf16[128,768]{1,0:T(8,128)(2,1)S(1)} %get-tuple-element.180), channel_id=1, source_target_pairs={{0,8},{1,9},{2,10},{3,11},{4,12},{5,13},{6,14},{7,15},{8,0},{9,1},... | collective-permute-start | bytes 589832 | tf_op jit(solution)/shard_map/ppermute | solution.py:416
  80.8 3.5 %collective-permute-start.22 = (bf16[128,256]{1,0:T(8,128)(2,1)S(1)}, bf16[128,256]{1,0:T(8,128)(2,1)S(1)}, u32[]{:S(2)}, u32[]{:S(2)}) collective-permute-start(bf16[128,256]{1,0:T(8,128)(2,1)S(1)} %get-tuple-element.185), channel_id=1, source_target_pairs={{0,2},{1,5},{2,0},{3,7},{4,6},{5,1},{6,4},{7,3},{8,10},{9,13},{10,... | collective-permute-start | bytes 196616 | tf_op jit(solution)/shard_map/ppermute | solution.py:416
  81.6 5.9 %collective-permute-start.24 = (bf16[32,2176]{1,0:T(8,128)(2,1)S(1)}, bf16[32,2176]{1,0:T(8,128)(2,1)S(1)}, u32[]{:S(2)}, u32[]{:S(2)}) collective-permute-start(bf16[32,2176]{1,0:T(8,128)(2,1)S(1)} %get-tuple-element.194), channel_id=1, source_target_pairs={{0,2},{2,0},{4,6},{6,4},{8,10},{10,8},{12,14},{14,12},{16,18},{18,... | collective-permute-start | bytes 417800 | tf_op jit(solution)/shard_map/ppermute | solution.py:492
  82.5 7.3 %collective-permute-start.25 = (bf16[32,2176]{1,0:T(8,128)(2,1)S(1)}, bf16[32,2176]{1,0:T(8,128)(2,1)S(1)}, u32[]{:S(2)}, u32[]{:S(2)}) collective-permute-start(bf16[32,2176]{1,0:T(8,128)(2,1)S(1)} %get-tuple-element.195), channel_id=1, source_target_pairs={{0,4},{2,6},{4,0},{6,2},{8,12},{10,14},{12,8},{14,10},{16,20},{18,... | collective-permute-start | bytes 417800 | tf_op jit(solution)/shard_map/ppermute | solution.py:492
  82.7 7.1 %collective-permute-start.26 = (bf16[32,2176]{1,0:T(8,128)(2,1)S(1)}, bf16[32,2176]{1,0:T(8,128)(2,1)S(1)}, u32[]{:S(2)}, u32[]{:S(2)}) collective-permute-start(bf16[32,2176]{1,0:T(8,128)(2,1)S(1)} %get-tuple-element.196), channel_id=1, source_target_pairs={{0,6},{2,4},{4,2},{6,0},{8,14},{10,12},{12,10},{14,8},{16,22},{18,... | collective-permute-start | bytes 417800 | tf_op jit(solution)/shard_map/ppermute | solution.py:492
  84.3 15.1 %collective-permute-start.28 = (bf16[64,1024]{1,0:T(8,128)(2,1)S(1)}, bf16[64,1024]{1,0:T(8,128)(2,1)S(1)}, u32[]{:S(2)}, u32[]{:S(2)}) collective-permute-start(bf16[64,1024]{1,0:T(8,128)(2,1)S(1)} %get-tuple-element.202), channel_id=1, source_target_pairs={{0,16},{1,17},{2,18},{3,19},{4,20},{5,21},{6,22},{7,23},{8,24},{9,... | collective-permute-start | bytes 393224 | tf_op jit(solution)/shard_map/ppermute | solution.py:416
  87.2 12.2 %collective-permute-start.29 = (bf16[64,768]{1,0:T(8,128)(2,1)S(1)}, bf16[64,768]{1,0:T(8,128)(2,1)S(1)}, u32[]{:S(2)}, u32[]{:S(2)}) collective-permute-start(bf16[64,768]{1,0:T(8,128)(2,1)S(1)} %get-tuple-element.204), channel_id=1, source_target_pairs={{0,16},{1,17},{2,18},{3,19},{4,20},{5,21},{6,22},{7,23},{8,24},{9,... | collective-permute-start | bytes 294920 | tf_op jit(solution)/shard_map/ppermute | solution.py:416
  87.4 12.0 %collective-permute-start.30 = (bf16[64,256]{1,0:T(8,128)(2,1)S(1)}, bf16[64,256]{1,0:T(8,128)(2,1)S(1)}, u32[]{:S(2)}, u32[]{:S(2)}) collective-permute-start(bf16[64,256]{1,0:T(8,128)(2,1)S(1)} %get-tuple-element.206), channel_id=1, source_target_pairs={{0,4},{1,3},{2,6},{3,1},{4,0},{5,7},{6,2},{7,5},{8,12},{9,11},{10,... | collective-permute-start | bytes 98312 | tf_op jit(solution)/shard_map/ppermute | solution.py:416
  89.9 9.6 %collective-permute-start.27 = (f32[1,128]{1,0:T(1,128)S(1)}, f32[1,128]{1,0:T(1,128)S(1)}, u32[]{:S(2)}, u32[]{:S(2)}) collective-permute-start(f32[1,128]{1,0:T(1,128)S(1)} %get-tuple-element.200.refs_1_), channel_id=1, source_target_pairs={{0,1},{1,0},{2,3},{3,2},{4,5},{5,4},{6,7},{7,6},{8,9},{9,8},{10,11... | collective-permute-start | bytes 1544 | tf_op jit(solution)/shard_map/ppermute | solution.py:656

commit v5 on v3

--- a/solution.py
+++ b/solution.py
@@ -19,8 +19,8 @@
 BACK = (3, 2, 0, 1)
 DIRECT = True
 JOIN = False
-PLAN = ('f', 'g0', 'g1', 'g2', 's', 'd0', 'd1', 'd2', 'e', 'r0', 'b0', 'r2', 'r1', 'r0', 'b1', 'l0', 'r1', 'r2', 'r0', 'r2', 'r1', 'l1', 'i')
-COSTS = (1, 1000000000, 4000000000, 1, 8000000000, 16000000000, 1, 1, 4000000000, 1, 1, 4000000000, 2000000000, 4000000000, 1000000000, 1, 1, 1000000000, 1, 1, 1, 1, 1)
+PLAN = ('f', 'g0', 'g1', 'g2', 's', 'd0', 'd1', 'd2', 'b0', 'b1', 'e', 'r0', 'r2', 'l0', 'r1', 'r0', 'r2', 'r1', 'r2', 'r0', 'l1', 'r1', 'i')
+COSTS = (16000000000, 8500000000, 2000000000, 1500000000, 1, 10500000000, 1, 1, 1, 1, 1000000000, 1000000000, 4000000000, 1, 1, 1, 4000000000, 1, 1, 1000000000, 1000000000, 1, 1000000000)
 VMEM = pl.BlockSpec(memory_space=pltpu.VMEM)
 SMEM = pl.BlockSpec(memory_space=pltpu.SMEM)
 ANY = pl.BlockSpec(memory_space=pl.ANY)

time: 101 us -> 101 us (level); the launches traced: 101 us -> 99.2 us
  starting transfers between devices: 39 us -> 36.2 us
    ppermute x12, waiting for transfers between devices: 4.89 us -> 9.3 us  [send(): lax.ppermute(leave, AXES, partners(self.parts, self.axes.pop(0)))]
    ppermute x12, waiting for transfers between devices: 4.12 us -> 0.72 us  [move(): moved[i] = lax.ppermute(pieces[i], 'parts', perm)]
    ppermute x12, starting transfers between devices: 14.4 us -> 12.1 us  [send(): lax.ppermute(leave, AXES, partners(self.parts, self.axes.pop(0)))]
  transfers between devices with their start and end apart: 31 -> 31, of which waited for: 4 -> 6; matrix products, arithmetic and copies ran while one was open for 0% -> 0% of each run, Pallas kernels for 43% -> 44%
where the time goes in v5:
time: 101 us; the launch traced here: 99.2 us
  Pallas kernels  51.9 us (51%)
  starting transfers between devices  36.2 us (36%)
  waiting for transfers between devices  10 us (10%)
    pallas_call x31, Pallas kernels, run(): pl.pallas_call(body, name=name, in_specs=specs, out_specs=(VMEM if keep i...  51.9 us
    ppermute x12, starting transfers between devices, move(): moved[i] = lax.ppermute(pieces[i], 'parts', perm)  14.1 us
    ppermute x12, starting transfers between devices, send(): lax.ppermute(leave, AXES, partners(self.parts, self.axes.pop(0)))  12.1 us
    ppermute x12, waiting for transfers between devices, send(): lax.ppermute(leave, AXES, partners(self.parts, self.axes.pop(0)))  9.3 us
    ppermute x1, starting transfers between devices, local(): bias_theirs = lax.ppermute(bias_mine, 'mp', SWAP)  3.53 us
    ppermute x1, starting transfers between devices, local(): bias_other = lax.ppermute(bias_own, 'mp', SWAP)  3.2 us
  transfers between devices with their start and end apart: 31, of which 6 were waited for; matrix products, arithmetic and copies ran while one was open for 0% of the time, Pallas kernels for 44%

profile of v5, /device:TPU:1, one launch (start us, length us, event | category | flops | bytes accessed | tf_op | source)
XLA Modules:
  0.0 99.2 jit_solution(9941076593577934381)
XLA Ops:
  0.7 2.8 %outgoing.1 = (bf16[768,2048]{1,0:T(8,128)(2,1)S(1)}, bf16[32,2048]{1,0:T(8,128)(2,1)S(1)}, bf16[32,2048]{1,0:T(8,128)(2,1)S(1)}, bf16[32,2048]{1,0:T(8,128)(2,1...) custom-call(s32[2]{0:T(128)S(1)} %pad_add_fusion.refs_0_, bf16[768,2048]{1,0:T(8,128)(2,1)} %bitcast.13, ...), custom_call_target="tpu_custom_call" | custom-call | flops 1 | bytes 1 | tf_op jit(solution)/shard_map/outgoing/pallas_call | solution.py:59
  3.6 2.2 %collective-permute-start.2 = (bf16[32,2048]{1,0:T(8,128)(2,1)S(1)}, bf16[32,2048]{1,0:T(8,128)(2,1)S(1)}, u32[]{:S(2)}, u32[]{:S(2)}) collective-permute-start(bf16[32,2048]{1,0:T(8,128)(2,1)S(1)} %get-tuple-element.113), channel_id=1, source_target_pairs={{0,8},{2,10},{4,12},{6,14},{8,0},{10,2},{12,4},{14,6},{16,24},{18,... | collective-permute-start | bytes 393224 | tf_op jit(solution)/shard_map/ppermute | solution.py:492
  5.8 2.3 %collective-permute-start.3 = (bf16[32,2048]{1,0:T(8,128)(2,1)S(1)}, bf16[32,2048]{1,0:T(8,128)(2,1)S(1)}, u32[]{:S(2)}, u32[]{:S(2)}) collective-permute-start(bf16[32,2048]{1,0:T(8,128)(2,1)S(1)} %get-tuple-element.114), channel_id=1, source_target_pairs={{0,16},{2,18},{4,20},{6,22},{8,24},{10,26},{12,28},{14,30},{16,0},... | collective-permute-start | bytes 393224 | tf_op jit(solution)/shard_map/ppermute | solution.py:492
  8.1 1.2 %collective-permute-start = (bf16[1024,2048]{1,0:T(8,128)(2,1)}, bf16[1024,2048]{1,0:T(8,128)(2,1)S(1)}, u32[]{:S(2)}, u32[]{:S(2)}) collective-permute-start(bf16[1024,2048]{1,0:T(8,128)(2,1)} %refs_1_.1), channel_id=1, source_target_pairs={{0,1},{1,0},{2,3},{3,2},{4,5},{5,4},{6,7},{7,6},{8,9},{9,8},{10,11... | collective-permute-start | bytes 12582920 | tf_op jit(solution)/shard_map/ppermute | solution.py:501
  9.3 4.0 %mix.1 = (bf16[2,768,1024]{2,1,0:T(8,128)(2,1)S(1)}, bf16[2048,768]{1,0:T(8,128)(2,1)S(1)}, f32[768,1]{1,0:T(8,128)S(1)}, f32[8,768]{1,0:T(8,128)S(1)}, bf16[2,3...) custom-call(s32[2]{0:T(128)S(1)} %pad_add_fusion.refs_0_, ...), custom_call_target="tpu_custom_call" | custom-call | flops 60000002048 | bytes 1 | tf_op jit(solution)/shard_map/mix/pallas_call | solution.py:59
  13.3 4.0 %pre_own.1 = (f32[768,2048]{1,0:T(8,128)S(1)}, f32[8,128]{1,0:T(8,128)S(1)}) custom-call(s32[2]{0:T(128)S(1)} %pad_add_fusion.refs_0_, bf16[2,768,1024]{2,1,0:T(8,128)(2,1)S(1)} %get-tuple-element.116.refs_1_.refs_2_, bf16[1024,2048]{1,0:T(8,128)(2,1)S(1)} %get-tuple-element.111.refs_2_.refs_1_.refs_4_, f32[8,128]{1,0:T(8,128)S(1)} %get-tuple-element.117.refs_3_), custom_call_target="tpu_custom_call" | custom-call | flops 1 | bytes 1 | tf_op jit(solution)/shard_map/pre_own/pallas_call | solution.py:59
  17.4 1.5 %collective-permute-start.5 = (bf16[32,2048]{1,0:T(8,128)(2,1)S(1)}, bf16[32,2048]{1,0:T(8,128)(2,1)S(1)}, u32[]{:S(2)}, u32[]{:S(2)}) collective-permute-start(bf16[32,2048]{1,0:T(8,128)(2,1)S(1)} %get-tuple-element.120), channel_id=1, source_target_pairs={{0,2},{2,0},{4,6},{6,4},{8,10},{10,8},{12,14},{14,12},{16,18},{18,... | collective-permute-start | bytes 393224 | tf_op jit(solution)/shard_map/ppermute | solution.py:492
  18.8 1.2 %collective-permute-start.6 = (bf16[32,2048]{1,0:T(8,128)(2,1)S(1)}, bf16[32,2048]{1,0:T(8,128)(2,1)S(1)}, u32[]{:S(2)}, u32[]{:S(2)}) collective-permute-start(bf16[32,2048]{1,0:T(8,128)(2,1)S(1)} %get-tuple-element.121), channel_id=1, source_target_pairs={{0,4},{2,6},{4,0},{6,2},{8,12},{10,14},{12,8},{14,10},{16,20},{18,... | collective-permute-start | bytes 393224 | tf_op jit(solution)/shard_map/ppermute | solution.py:492
  20.1 3.2 %collective-permute-start.1 = (bf16[1,1024]{1,0:T(2,128)(2,1)S(1)}, bf16[1,1024]{1,0:T(2,128)(2,1)S(1)}, u32[]{:S(2)}, u32[]{:S(2)}) collective-permute-start(bf16[1,1024]{1,0:T(2,128)(2,1)S(1)} %reshape.27.refs_3_), channel_id=1, source_target_pairs={{0,1},{1,0},{2,3},{3,2},{4,5},{5,4},{6,7},{7,6},{8,9},{9,8},{10,11... | collective-permute-start | bytes 6152 | tf_op jit(solution)/shard_map/ppermute | solution.py:503
  23.3 4.0 %pre_other.1 = (f32[768,2048]{1,0:T(8,128)S(1)}, f32[8,128]{1,0:T(8,128)S(1)}) custom-call(s32[2]{0:T(128)S(1)} %pad_add_fusion.refs_0_, f32[768,2048]{1,0:T(8,128)S(1)} %get-tuple-element.123.refs_1_, bf16[2,768,1024]{2,1,0:T(8,128)(2,1)S(1)} %get-tuple-element.116.refs_1_.refs_2_, ...), custom_call_target="tpu_custom_call" | custom-call | flops 1 | bytes 1 | tf_op jit(solution)/shard_map/pre_other/pallas_call | solution.py:59
  27.3 1.9 %remote_product.1 = (bf16[256,2048]{1,0:T(8,128)(2,1)S(1)}, f32[1,2048]{1,0:T(1,128)S(1)}, f32[8,128]{1,0:T(8,128)S(1)}) custom-call(s32[2]{0:T(128)S(1)} %pad_add_fusion.refs_0_, bf16[1024,2048]{1,0:T(8,128)(2,1)S(1)} %get-tuple-element.111.refs_2_.refs_1_.refs_4_, bf16[1024,2048]{1,0:T(8,128)(2,1)S(1)} %collective-permute-done.refs_3_.refs_2_.refs_1_.refs_5_, ...), custom_call_target="tpu_custom_call" | custom-call | flops 1 | bytes 1 | tf_op jit(solution)/shard_map/remote_product/pallas_call | solution.py:59
  29.2 2.0 %finish_mixed.1 = (bf16[1024,768]{1,0:T(8,128)(2,1)S(1)}, bf16[1024,768]{1,0:T(8,128)(2,1)S(1)}, f32[8,128]{1,0:T(8,128)S(1)}) custom-call(s32[2]{0:T(128)S(1)} %pad_add_fusion.refs_0_, s32[1,128]{1,0:T(1,128)S(1)} %get-tuple-element.109.refs_1_.refs_0_, f32[8,768]{1,0:T(8,128)S(1)} %get-tuple-element.129.refs_2_, ...), custom_call_target="tpu_custom_call" | custom-call | flops 16000000000 | bytes 1 | tf_op jit(solution)/shard_map/finish_mixed/pallas_call | solution.py:59
  31.2 1.4 %collective-permute-start.8 = (bf16[1024,768]{1,0:T(8,128)(2,1)S(1)}, bf16[1024,768]{1,0:T(8,128)(2,1)S(1)}, u32[]{:S(2)}, u32[]{:S(2)}) collective-permute-start(bf16[1024,768]{1,0:T(8,128)(2,1)S(1)} %get-tuple-element.144), channel_id=1, source_target_pairs={{0,1},{1,0},{2,3},{3,2},{4,5},{5,4},{6,7},{7,6},{8,9},{9,8},{10,11... | collective-permute-start | bytes 4718600 | tf_op jit(solution)/shard_map/ppermute | solution.py:623
  32.5 3.5 %gelu.3 = (bf16[768,2048]{1,0:T(8,128)(2,1)}, bf16[768,1024]{1,0:T(8,128)(2,1)S(1)}, f32[1,1024]{1,0:T(1,128)S(1)}, f32[8,128]{1,0:T(8,128)S(1)}) custom-call(s32[1,128]{1,0:T(1,128)S(1)} %get-tuple-element.109.refs_1_.refs_0_, f32[768,1]{1,0:T(8,128)S(1)} %get-tuple-element.110.refs_1_.refs_0_, bf16[256,2048]{1,0:T(8,128)(2,1)S(1)} %get-tuple-element.126.refs_2_, ...), custom_call_target="tpu_custom_call" | custom-call | flops 8499999744 | bytes 1 | tf_op jit(solution)/shard_map/gelu/pallas_call | solution.py:59
  36.1 2.9 %gelu.4 = (bf16[768,2048]{1,0:T(8,128)(2,1)}, bf16[768,768]{1,0:T(8,128)(2,1)S(1)}, f32[1,768]{1,0:T(1,128)S(1)}, f32[8,128]{1,0:T(8,128)S(1)}) custom-call(s32[1,128]{1,0:T(1,128)S(1)} %get-tuple-element.109.refs_1_.refs_0_, f32[768,1]{1,0:T(8,128)S(1)} %get-tuple-element.110.refs_1_.refs_0_, ...), custom_call_target="tpu_custom_call", output_to_operand_aliasing={{0}: (6, {})} | custom-call | flops 2000000000 | bytes 1 | tf_op jit(solution)/shard_map/gelu/pallas_call | solution.py:59
  39.0 0.5 collective-permute-start.10
  39.6 1.5 %gelu.5 = (bf16[768,2048]{1,0:T(8,128)(2,1)}, bf16[768,256]{1,0:T(8,128)(2,1)S(1)}, f32[1,256]{1,0:T(1,128)S(1)}, f32[8,128]{1,0:T(8,128)S(1)}) custom-call(s32[1,128]{1,0:T(1,128)S(1)} %get-tuple-element.109.refs_1_.refs_0_, f32[768,1]{1,0:T(8,128)S(1)} %get-tuple-element.110.refs_1_.refs_0_, ...), custom_call_target="tpu_custom_call", output_to_operand_aliasing={{0}: (6, {})} | custom-call | flops 1500000000 | bytes 1 | tf_op jit(solution)/shard_map/gelu/pallas_call | solution.py:59
  41.1 1.2 %sent_grads.1 = (bf16[32,2176]{1,0:T(8,128)(2,1)S(1)}, bf16[32,2176]{1,0:T(8,128)(2,1)S(1)}, bf16[32,2176]{1,0:T(8,128)(2,1)S(1)}, bf16[32,2176]{1,0:T(8,128)(2,1)S(1)}, f32[8,128]{1,0:T(8,128)S(1)}) custom-call(s32[2]{0:T(128)S(1)} %pad_add_fusion.refs_0_, s32[1,128]{1,0:T(1,128)S(1)} %get-tuple-element.145.refs_1_, ...), custom_call_target="tpu_custom_call" | custom-call | flops 1 | bytes 1 | tf_op jit(solution)/shard_map/sent_grads/pallas_call | solution.py:59
  42.3 3.5 %grad.3 = (bf16[512,1024]{1,0:T(8,128)(2,1)S(1)}, bf16[512,1024]{1,0:T(8,128)(2,1)S(1)}, f32[8,128]{1,0:T(8,128)S(1)}) custom-call(bf16[1024,768]{1,0:T(8,128)(2,1)S(1)} %get-tuple-element.143.refs_0_, bf16[1024,768]{1,0:T(8,128)(2,1)S(1)} %collective-permute-done.8.refs_1_, bf16[768,1024]{1,0:T(8,128)(2,1)S(1)} %get-tuple-element.140.refs_3_.refs_2_, ...), custom_call_target="tpu_custom_call" | custom-call | flops 10499999744 | bytes 1 | tf_op jit(solution)/shard_map/grad/pallas_call | solution.py:59
  45.8 0.7 collective-permute-start.13
  46.6 1.7 %collective-permute-start.14 = (bf16[32,2176]{1,0:T(8,128)(2,1)S(1)}, bf16[32,2176]{1,0:T(8,128)(2,1)S(1)}, u32[]{:S(2)}, u32[]{:S(2)}) collective-permute-start(bf16[32,2176]{1,0:T(8,128)(2,1)S(1)} %get-tuple-element.160), channel_id=1, source_target_pairs={{0,8},{2,10},{4,12},{6,14},{8,0},{10,2},{12,4},{14,6},{16,24},{18,... | collective-permute-start | bytes 417800 | tf_op jit(solution)/shard_map/ppermute | solution.py:492
  48.3 1.4 %collective-permute-start.15 = (bf16[32,2176]{1,0:T(8,128)(2,1)S(1)}, bf16[32,2176]{1,0:T(8,128)(2,1)S(1)}, u32[]{:S(2)}, u32[]{:S(2)}) collective-permute-start(bf16[32,2176]{1,0:T(8,128)(2,1)S(1)} %get-tuple-element.161), channel_id=1, source_target_pairs={{0,16},{2,18},{4,20},{6,22},{8,24},{10,26},{12,28},{14,30},{16,0},... | collective-permute-start | bytes 417800 | tf_op jit(solution)/shard_map/ppermute | solution.py:492
  49.7 1.1 %collective-permute-start.16 = (bf16[32,2176]{1,0:T(8,128)(2,1)S(1)}, bf16[32,2176]{1,0:T(8,128)(2,1)S(1)}, u32[]{:S(2)}, u32[]{:S(2)}) collective-permute-start(bf16[32,2176]{1,0:T(8,128)(2,1)S(1)} %get-tuple-element.162), channel_id=1, source_target_pairs={{0,24},{2,26},{4,28},{6,30},{8,16},{10,18},{12,20},{14,22},{16,8},... | collective-permute-start | bytes 417800 | tf_op jit(solution)/shard_map/ppermute | solution.py:492
  50.8 2.7 %grad.4 = (bf16[512,768]{1,0:T(8,128)(2,1)S(1)}, bf16[512,768]{1,0:T(8,128)(2,1)S(1)}, f32[8,128]{1,0:T(8,128)S(1)}) custom-call(bf16[1024,768]{1,0:T(8,128)(2,1)S(1)} %get-tuple-element.143.refs_0_, bf16[1024,768]{1,0:T(8,128)(2,1)S(1)} %collective-permute-done.8.refs_1_, bf16[768,768]{1,0:T(8,128)(2,1)S(1)} %get-tuple-element.141.refs_4_.refs_2_.refs_3_, ...), custom_call_target="tpu_custom_call" | custom-call | flops 1 | bytes 1 | tf_op jit(solution)/shard_map/grad/pallas_call | solution.py:59
  53.5 1.0 collective-permute-start.18
  54.5 1.0 grad.5
  55.5 0.5 collective-permute-start.12
  56.0 3.5 %back.2 = (bf16[768,1024]{1,0:T(8,128)(2,1)S(1)}, f32[8,128]{1,0:T(8,128)S(1)}) custom-call(f32[768,1]{1,0:T(8,128)S(1)} %get-tuple-element.110.refs_1_.refs_0_, bf16[1024,2048]{1,0:T(8,128)(2,1)S(1)} %get-tuple-element.111.refs_2_.refs_1_.refs_4_, bf16[768,1024]{1,0:T(8,128)(2,1)S(1)} %get-tuple-element.140.refs_3_.refs_2_, ...), custom_call_target="tpu_custom_call" | custom-call | flops 1 | bytes 1 | tf_op jit(solution)/shard_map/back/pallas_call | solution.py:59
  59.5 3.5 %back.3 = (bf16[768,1024]{1,0:T(8,128)(2,1)S(1)}, f32[8,128]{1,0:T(8,128)S(1)}) custom-call(f32[768,1]{1,0:T(8,128)S(1)} %get-tuple-element.110.refs_1_.refs_0_, bf16[1024,2048]{1,0:T(8,128)(2,1)S(1)} %collective-permute-done.refs_3_.refs_2_.refs_1_.refs_5_, bf16[768,1024]{1,0:T(8,128)(2,1)S(1)} %get-tuple-element.140.refs_3_.refs_2_, ...), custom_call_target="tpu_custom_call" | custom-call | flops 1 | bytes 1 | tf_op jit(solution)/shard_map/back/pallas_call | solution.py:59
  63.2 0.8 collective-permute-start.17
  64.0 2.2 %collective-permute-done.12.refs_1_ = bf16[512,256]{1,0:T(8,128)(2,1)S(1)} collective-permute-done((bf16[512,256]{1,0:T(8,128)(2,1)S(1)}, bf16[512,256]{1,0:T(8,128)(2,1)S(1)}, u32[]{:S(2)}, u32[]{:S(2)}) %collective-permute-start.12) | collective-permute-done | bytes 262176 | tf_op jit(solution)/shard_map/ppermute | solution.py:416
  66.3 0.8 collective-permute-start.20
  67.1 1.2 %input_local.2 = (f32[768,1024]{1,0:T(8,128)S(1)}, f32[8,128]{1,0:T(8,128)S(1)}) custom-call(bf16[2,384,384]{2,1,0:T(8,128)(2,1)S(1)} %get-tuple-element.139.refs_0_, bf16[768,1024]{1,0:T(8,128)(2,1)S(1)} %get-tuple-element.154.refs_1_, f32[8,128]{1,0:T(8,128)S(1)} %get-tuple-element.167.refs_2_), custom_call_target="tpu_custom_call" | custom-call | flops 1 | bytes 1 | tf_op jit(solution)/shard_map/input_local/pallas_call | solution.py:59
  68.9 0.7 collective-permute-start.22
  69.7 4.7 %collective-permute-done.17.refs_1_ = bf16[256,1024]{1,0:T(8,128)(2,1)S(1)} collective-permute-done((bf16[256,1024]{1,0:T(8,128)(2,1)S(1)}, bf16[256,1024]{1,0:T(8,128)(2,1)S(1)}, u32[]{:S(2)}, u32[]{:S(2)}) %collective-permute-start.17) | collective-permute-done | bytes 524320 | tf_op jit(solution)/shard_map/ppermute | solution.py:416
  74.5 1.5 %collective-permute-start.19 = (bf16[128,1024]{1,0:T(8,128)(2,1)S(1)}, bf16[128,1024]{1,0:T(8,128)(2,1)S(1)}, u32[]{:S(2)}, u32[]{:S(2)}) collective-permute-start(bf16[128,1024]{1,0:T(8,128)(2,1)S(1)} %get-tuple-element.177), channel_id=1, source_target_pairs={{0,8},{1,9},{2,10},{3,11},{4,12},{5,13},{6,14},{7,15},{8,0},{9,1},... | collective-permute-start | bytes 786440 | tf_op jit(solution)/shard_map/ppermute | solution.py:416
  76.0 0.8 collective-permute-start.21
  76.8 1.8 %collective-permute-done.22.refs_1_ = bf16[256,768]{1,0:T(8,128)(2,1)S(1)} collective-permute-done((bf16[256,768]{1,0:T(8,128)(2,1)S(1)}, bf16[256,768]{1,0:T(8,128)(2,1)S(1)}, u32[]{:S(2)}, u32[]{:S(2)}) %collective-permute-start.22) | collective-permute-done | bytes 393248 | tf_op jit(solution)/shard_map/ppermute | solution.py:416
  78.7 2.5 %collective-permute-start.26 = (bf16[128,768]{1,0:T(8,128)(2,1)S(1)}, bf16[128,768]{1,0:T(8,128)(2,1)S(1)}, u32[]{:S(2)}, u32[]{:S(2)}) collective-permute-start(bf16[128,768]{1,0:T(8,128)(2,1)S(1)} %get-tuple-element.195), channel_id=1, source_target_pairs={{0,8},{1,9},{2,10},{3,11},{4,12},{5,13},{6,14},{7,15},{8,0},{9,1},... | collective-permute-start | bytes 589832 | tf_op jit(solution)/shard_map/ppermute | solution.py:416
  81.5 1.2 %collective-permute-start.24 = (bf16[32,2176]{1,0:T(8,128)(2,1)S(1)}, bf16[32,2176]{1,0:T(8,128)(2,1)S(1)}, u32[]{:S(2)}, u32[]{:S(2)}) collective-permute-start(bf16[32,2176]{1,0:T(8,128)(2,1)S(1)} %get-tuple-element.192), channel_id=1, source_target_pairs={{0,4},{2,6},{4,0},{6,2},{8,12},{10,14},{12,8},{14,10},{16,20},{18,... | collective-permute-start | bytes 417800 | tf_op jit(solution)/shard_map/ppermute | solution.py:492
  82.8 1.0 %collective-permute-start.25 = (bf16[32,2176]{1,0:T(8,128)(2,1)S(1)}, bf16[32,2176]{1,0:T(8,128)(2,1)S(1)}, u32[]{:S(2)}, u32[]{:S(2)}) collective-permute-start(bf16[32,2176]{1,0:T(8,128)(2,1)S(1)} %get-tuple-element.193), channel_id=1, source_target_pairs={{0,6},{2,4},{4,2},{6,0},{8,14},{10,12},{12,10},{14,8},{16,22},{18,... | collective-permute-start | bytes 417800 | tf_op jit(solution)/shard_map/ppermute | solution.py:492
  84.3 1.0 input_local.3
  85.4 2.0 %collective-permute-start.28 = (bf16[64,1024]{1,0:T(8,128)(2,1)S(1)}, bf16[64,1024]{1,0:T(8,128)(2,1)S(1)}, u32[]{:S(2)}, u32[]{:S(2)}) collective-permute-start(bf16[64,1024]{1,0:T(8,128)(2,1)S(1)} %get-tuple-element.202), channel_id=1, source_target_pairs={{0,16},{1,17},{2,18},{3,19},{4,20},{5,21},{6,22},{7,23},{8,24},{9,... | collective-permute-start | bytes 393224 | tf_op jit(solution)/shard_map/ppermute | solution.py:416
  87.5 0.5 collective-permute-start.29
  87.9 0.7 collective-permute-done.25.refs_3_.refs_9_
  88.6 3.5 %collective-permute-start.27 = (f32[1,128]{1,0:T(1,128)S(1)}, f32[1,128]{1,0:T(1,128)S(1)}, u32[]{:S(2)}, u32[]{:S(2)}) collective-permute-start(f32[1,128]{1,0:T(1,128)S(1)} %get-tuple-element.200.refs_1_), channel_id=1, source_target_pairs={{0,1},{1,0},{2,3},{3,2},{4,5},{5,4},{6,7},{7,6},{8,9},{9,8},{10,11... | collective-permute-start | bytes 1544 | tf_op jit(solution)/shard_map/ppermute | solution.py:656
  92.2 5.6 %input_gradient.1 = (bf16[768,2048]{1,0:T(8,128)(2,1)}, f32[8,128]{1,0:T(8,128)S(1)}) custom-call(s32[2]{0:T(128)S(1)} %pad_add_fusion.refs_0_, s32[1,128]{1,0:T(1,128)S(1)} %get-tuple-element.138.refs_1_, f32[768,1024]{1,0:T(8,128)S(1)} %get-tuple-element.168.refs_2_, f32[768,1024]{1,0:T(8,128)S(1)} %get-tuple-element.189.refs_3_, ...), custom_call_target="tpu_custom_call" | custom-call | flops 1000000000 | bytes 1 | tf_op jit(solution)/shard_map/input_gradient/pallas_call | solution.py:59
  97.8 1.4 %last_sum.1 = (f32[64,2048]{1,0:T(8,128)}, f32[1,64]{1,0:T(1,128)}, f32[8,128]{1,0:T(8,128)}) custom-call(s32[2]{0:T(128)S(1)} %pad_add_fusion.refs_0_, f32[1,128]{1,0:T(1,128)S(1)} %get-tuple-element.200.refs_1_, f32[1,128]{1,0:T(1,128)S(1)} %collective-permute-done.27.refs_2_, bf16[64,1024]{1,0:T(8,128)(2,1)S(1)} %get-tuple-element.201.refs_3_, ...), custom_call_target="tpu_custom_call" | custom-call | flops 1000000000 | bytes 1 | tf_op jit(solution)/shard_map/last_sum/pallas_call | solution.py:59
  (51 shorter events, 2.6 us)
Async XLA Ops:
  3.6 13.7 %collective-permute-start.2 = (bf16[32,2048]{1,0:T(8,128)(2,1)S(1)}, bf16[32,2048]{1,0:T(8,128)(2,1)S(1)}, u32[]{:S(2)}, u32[]{:S(2)}) collective-permute-start(bf16[32,2048]{1,0:T(8,128)(2,1)S(1)} %get-tuple-element.113), channel_id=1, source_target_pairs={{0,8},{2,10},{4,12},{6,14},{8,0},{10,2},{12,4},{14,6},{16,24},{18,... | collective-permute-start | bytes 393224 | tf_op jit(solution)/shard_map/ppermute | solution.py:492
  5.8 11.5 %collective-permute-start.3 = (bf16[32,2048]{1,0:T(8,128)(2,1)S(1)}, bf16[32,2048]{1,0:T(8,128)(2,1)S(1)}, u32[]{:S(2)}, u32[]{:S(2)}) collective-permute-start(bf16[32,2048]{1,0:T(8,128)(2,1)S(1)} %get-tuple-element.114), channel_id=1, source_target_pairs={{0,16},{2,18},{4,20},{6,22},{8,24},{10,26},{12,28},{14,30},{16,0},... | collective-permute-start | bytes 393224 | tf_op jit(solution)/shard_map/ppermute | solution.py:492
  8.1 9.2 %collective-permute-start.4 = (bf16[32,2048]{1,0:T(8,128)(2,1)S(1)}, bf16[32,2048]{1,0:T(8,128)(2,1)S(1)}, u32[]{:S(2)}, u32[]{:S(2)}) collective-permute-start(bf16[32,2048]{1,0:T(8,128)(2,1)S(1)} %get-tuple-element.115), channel_id=1, source_target_pairs={{0,24},{2,26},{4,28},{6,30},{8,16},{10,18},{12,20},{14,22},{16,8},... | collective-permute-start | bytes 393224 | tf_op jit(solution)/shard_map/ppermute | solution.py:492
  8.1 15.2 %collective-permute-start = (bf16[1024,2048]{1,0:T(8,128)(2,1)}, bf16[1024,2048]{1,0:T(8,128)(2,1)S(1)}, u32[]{:S(2)}, u32[]{:S(2)}) collective-permute-start(bf16[1024,2048]{1,0:T(8,128)(2,1)} %refs_1_.1), channel_id=1, source_target_pairs={{0,1},{1,0},{2,3},{3,2},{4,5},{5,4},{6,7},{7,6},{8,9},{9,8},{10,11... | collective-permute-start | bytes 12582920 | tf_op jit(solution)/shard_map/ppermute | solution.py:501
  13.3 6.8 %copy-start.1 = (bf16[1024]{0:T(1024)(128)(2,1)S(1)}, bf16[1024]{0:T(1024)(128)(2,1)}, u32[]{:S(2)}) copy-start(bf16[1024]{0:T(1024)(128)(2,1)} %param.9) | copy-start | bytes 6148
  17.4 9.9 %collective-permute-start.5 = (bf16[32,2048]{1,0:T(8,128)(2,1)S(1)}, bf16[32,2048]{1,0:T(8,128)(2,1)S(1)}, u32[]{:S(2)}, u32[]{:S(2)}) collective-permute-start(bf16[32,2048]{1,0:T(8,128)(2,1)S(1)} %get-tuple-element.120), channel_id=1, source_target_pairs={{0,2},{2,0},{4,6},{6,4},{8,10},{10,8},{12,14},{14,12},{16,18},{18,... | collective-permute-start | bytes 393224 | tf_op jit(solution)/shard_map/ppermute | solution.py:492
  18.8 8.5 %collective-permute-start.6 = (bf16[32,2048]{1,0:T(8,128)(2,1)S(1)}, bf16[32,2048]{1,0:T(8,128)(2,1)S(1)}, u32[]{:S(2)}, u32[]{:S(2)}) collective-permute-start(bf16[32,2048]{1,0:T(8,128)(2,1)S(1)} %get-tuple-element.121), channel_id=1, source_target_pairs={{0,4},{2,6},{4,0},{6,2},{8,12},{10,14},{12,8},{14,10},{16,20},{18,... | collective-permute-start | bytes 393224 | tf_op jit(solution)/shard_map/ppermute | solution.py:492
  20.1 7.2 %collective-permute-start.7 = (bf16[32,2048]{1,0:T(8,128)(2,1)S(1)}, bf16[32,2048]{1,0:T(8,128)(2,1)S(1)}, u32[]{:S(2)}, u32[]{:S(2)}) collective-permute-start(bf16[32,2048]{1,0:T(8,128)(2,1)S(1)} %get-tuple-element.122), channel_id=1, source_target_pairs={{0,6},{2,4},{4,2},{6,0},{8,14},{10,12},{12,10},{14,8},{16,22},{18,... | collective-permute-start | bytes 393224 | tf_op jit(solution)/shard_map/ppermute | solution.py:492
  20.1 7.2 %collective-permute-start.1 = (bf16[1,1024]{1,0:T(2,128)(2,1)S(1)}, bf16[1,1024]{1,0:T(2,128)(2,1)S(1)}, u32[]{:S(2)}, u32[]{:S(2)}) collective-permute-start(bf16[1,1024]{1,0:T(2,128)(2,1)S(1)} %reshape.27.refs_3_), channel_id=1, source_target_pairs={{0,1},{1,0},{2,3},{3,2},{4,5},{5,4},{6,7},{7,6},{8,9},{9,8},{10,11... | collective-permute-start | bytes 6152 | tf_op jit(solution)/shard_map/ppermute | solution.py:503
  29.2 3.3 %copy-start = (bf16[2,384,2048]{2,1,0:T(8,128)(2,1)S(1)}, bf16[2,384,2048]{2,1,0:T(8,128)(2,1)}, u32[]{:S(2)}) copy-start(bf16[2,384,2048]{2,1,0:T(8,128)(2,1)} %param.13) | copy-start | bytes 9437188
  31.2 11.1 %collective-permute-start.8 = (bf16[1024,768]{1,0:T(8,128)(2,1)S(1)}, bf16[1024,768]{1,0:T(8,128)(2,1)S(1)}, u32[]{:S(2)}, u32[]{:S(2)}) collective-permute-start(bf16[1024,768]{1,0:T(8,128)(2,1)S(1)} %get-tuple-element.144), channel_id=1, source_target_pairs={{0,1},{1,0},{2,3},{3,2},{4,5},{5,4},{6,7},{7,6},{8,9},{9,8},{10,11... | collective-permute-start | bytes 4718600 | tf_op jit(solution)/shard_map/ppermute | solution.py:623
  36.1 6.2 %collective-permute-start.11 = (bf16[768,1024]{1,0:T(8,128)(2,1)S(1)}, bf16[768,1024]{1,0:T(8,128)(2,1)S(1)}, u32[]{:S(2)}, u32[]{:S(2)}) collective-permute-start(bf16[768,1024]{1,0:T(8,128)(2,1)S(1)} %get-tuple-element.140.refs_3_.refs_2_), channel_id=1, source_target_pairs={{0,1},{1,0},{2,3},{3,2},{4,5},{5,4},{6,7},{7,6},{8,9},{9,8},{10,11... | collective-permute-start | bytes 4718600 | tf_op jit(solution)/shard_map/ppermute | solution.py:584
  39.0 10.7 %collective-permute-start.10 = (bf16[768,768]{1,0:T(8,128)(2,1)S(1)}, bf16[768,768]{1,0:T(8,128)(2,1)S(1)}, u32[]{:S(2)}, u32[]{:S(2)}) collective-permute-start(bf16[768,768]{1,0:T(8,128)(2,1)S(1)} %get-tuple-element.141.refs_4_.refs_2_.refs_3_), channel_id=1, source_target_pairs={{0,1},{1,0},{2,3},{3,2},{4,5},{5,4},{6,7},{7,6},{8,9},{9,8},{10,11... | collective-permute-start | bytes 3538952 | tf_op jit(solution)/shard_map/ppermute | solution.py:584
  45.8 17.2 %collective-permute-start.13 = (bf16[512,1024]{1,0:T(8,128)(2,1)S(1)}, bf16[512,1024]{1,0:T(8,128)(2,1)S(1)}, u32[]{:S(2)}, u32[]{:S(2)}) collective-permute-start(bf16[512,1024]{1,0:T(8,128)(2,1)S(1)} %get-tuple-element.158), channel_id=1, source_target_pairs={{0,2},{1,5},{2,0},{3,7},{4,6},{5,1},{6,4},{7,3},{8,10},{9,13},{10,... | collective-permute-start | bytes 3145736 | tf_op jit(solution)/shard_map/ppermute | solution.py:416
  46.6 6.9 %collective-permute-start.9 = (bf16[768,256]{1,0:T(8,128)(2,1)S(1)}, bf16[768,256]{1,0:T(8,128)(2,1)S(1)}, u32[]{:S(2)}, u32[]{:S(2)}) collective-permute-start(bf16[768,256]{1,0:T(8,128)(2,1)S(1)} %get-tuple-element.142.refs_5_.refs_2_.refs_4_), channel_id=1, source_target_pairs={{0,1},{1,0},{2,3},{3,2},{4,5},{5,4},{6,7},{7,6},{8,9},{9,8},{10,11... | collective-permute-start | bytes 1179656 | tf_op jit(solution)/shard_map/ppermute | solution.py:584
  46.6 8.9 %collective-permute-start.14 = (bf16[32,2176]{1,0:T(8,128)(2,1)S(1)}, bf16[32,2176]{1,0:T(8,128)(2,1)S(1)}, u32[]{:S(2)}, u32[]{:S(2)}) collective-permute-start(bf16[32,2176]{1,0:T(8,128)(2,1)S(1)} %get-tuple-element.160), channel_id=1, source_target_pairs={{0,8},{2,10},{4,12},{6,14},{8,0},{10,2},{12,4},{14,6},{16,24},{18,... | collective-permute-start | bytes 417800 | tf_op jit(solution)/shard_map/ppermute | solution.py:492
  48.3 14.6 %collective-permute-start.15 = (bf16[32,2176]{1,0:T(8,128)(2,1)S(1)}, bf16[32,2176]{1,0:T(8,128)(2,1)S(1)}, u32[]{:S(2)}, u32[]{:S(2)}) collective-permute-start(bf16[32,2176]{1,0:T(8,128)(2,1)S(1)} %get-tuple-element.161), channel_id=1, source_target_pairs={{0,16},{2,18},{4,20},{6,22},{8,24},{10,26},{12,28},{14,30},{16,0},... | collective-permute-start | bytes 417800 | tf_op jit(solution)/shard_map/ppermute | solution.py:492
  49.7 13.2 %collective-permute-start.16 = (bf16[32,2176]{1,0:T(8,128)(2,1)S(1)}, bf16[32,2176]{1,0:T(8,128)(2,1)S(1)}, u32[]{:S(2)}, u32[]{:S(2)}) collective-permute-start(bf16[32,2176]{1,0:T(8,128)(2,1)S(1)} %get-tuple-element.162), channel_id=1, source_target_pairs={{0,24},{2,26},{4,28},{6,30},{8,16},{10,18},{12,20},{14,22},{16,8},... | collective-permute-start | bytes 417800 | tf_op jit(solution)/shard_map/ppermute | solution.py:492
  53.5 15.2 %collective-permute-start.18 = (bf16[512,768]{1,0:T(8,128)(2,1)S(1)}, bf16[512,768]{1,0:T(8,128)(2,1)S(1)}, u32[]{:S(2)}, u32[]{:S(2)}) collective-permute-start(bf16[512,768]{1,0:T(8,128)(2,1)S(1)} %get-tuple-element.173), channel_id=1, source_target_pairs={{0,2},{1,5},{2,0},{3,7},{4,6},{5,1},{6,4},{7,3},{8,10},{9,13},{10,... | collective-permute-start | bytes 2359304 | tf_op jit(solution)/shard_map/ppermute | solution.py:416
  55.5 10.8 %collective-permute-start.12 = (bf16[512,256]{1,0:T(8,128)(2,1)S(1)}, bf16[512,256]{1,0:T(8,128)(2,1)S(1)}, u32[]{:S(2)}, u32[]{:S(2)}) collective-permute-start(bf16[512,256]{1,0:T(8,128)(2,1)S(1)} %get-tuple-element.156), channel_id=1, source_target_pairs={{0,8},{1,9},{2,10},{3,11},{4,12},{5,13},{6,14},{7,15},{8,0},{9,1},... | collective-permute-start | bytes 786440 | tf_op jit(solution)/shard_map/ppermute | solution.py:416
  63.2 11.1 %collective-permute-start.17 = (bf16[256,1024]{1,0:T(8,128)(2,1)S(1)}, bf16[256,1024]{1,0:T(8,128)(2,1)S(1)}, u32[]{:S(2)}, u32[]{:S(2)}) collective-permute-start(bf16[256,1024]{1,0:T(8,128)(2,1)S(1)} %get-tuple-element.171), channel_id=1, source_target_pairs={{0,4},{1,3},{2,6},{3,1},{4,0},{5,7},{6,2},{7,5},{8,12},{9,11},{10,... | collective-permute-start | bytes 1572872 | tf_op jit(solution)/shard_map/ppermute | solution.py:416
  66.3 9.7 %collective-permute-start.20 = (bf16[256,256]{1,0:T(8,128)(2,1)S(1)}, bf16[256,256]{1,0:T(8,128)(2,1)S(1)}, u32[]{:S(2)}, u32[]{:S(2)}) collective-permute-start(bf16[256,256]{1,0:T(8,128)(2,1)S(1)} %get-tuple-element.179), channel_id=1, source_target_pairs={{0,16},{1,17},{2,18},{3,19},{4,20},{5,21},{6,22},{7,23},{8,24},{9,... | collective-permute-start | bytes 393224 | tf_op jit(solution)/shard_map/ppermute | solution.py:416
  68.9 9.7 %collective-permute-start.22 = (bf16[256,768]{1,0:T(8,128)(2,1)S(1)}, bf16[256,768]{1,0:T(8,128)(2,1)S(1)}, u32[]{:S(2)}, u32[]{:S(2)}) collective-permute-start(bf16[256,768]{1,0:T(8,128)(2,1)S(1)} %get-tuple-element.184), channel_id=1, source_target_pairs={{0,4},{1,3},{2,6},{3,1},{4,0},{5,7},{6,2},{7,5},{8,12},{9,11},{10,... | collective-permute-start | bytes 1179656 | tf_op jit(solution)/shard_map/ppermute | solution.py:416
  74.5 9.3 %collective-permute-start.19 = (bf16[128,1024]{1,0:T(8,128)(2,1)S(1)}, bf16[128,1024]{1,0:T(8,128)(2,1)S(1)}, u32[]{:S(2)}, u32[]{:S(2)}) collective-permute-start(bf16[128,1024]{1,0:T(8,128)(2,1)S(1)} %get-tuple-element.177), channel_id=1, source_target_pairs={{0,8},{1,9},{2,10},{3,11},{4,12},{5,13},{6,14},{7,15},{8,0},{9,1},... | collective-permute-start | bytes 786440 | tf_op jit(solution)/shard_map/ppermute | solution.py:416
  76.0 6.8 %collective-permute-start.21 = (bf16[128,256]{1,0:T(8,128)(2,1)S(1)}, bf16[128,256]{1,0:T(8,128)(2,1)S(1)}, u32[]{:S(2)}, u32[]{:S(2)}) collective-permute-start(bf16[128,256]{1,0:T(8,128)(2,1)S(1)} %get-tuple-element.182), channel_id=1, source_target_pairs={{0,2},{1,5},{2,0},{3,7},{4,6},{5,1},{6,4},{7,3},{8,10},{9,13},{10,... | collective-permute-start | bytes 196616 | tf_op jit(solution)/shard_map/ppermute | solution.py:416
  78.7 6.7 %collective-permute-start.26 = (bf16[128,768]{1,0:T(8,128)(2,1)S(1)}, bf16[128,768]{1,0:T(8,128)(2,1)S(1)}, u32[]{:S(2)}, u32[]{:S(2)}) collective-permute-start(bf16[128,768]{1,0:T(8,128)(2,1)S(1)} %get-tuple-element.195), channel_id=1, source_target_pairs={{0,8},{1,9},{2,10},{3,11},{4,12},{5,13},{6,14},{7,15},{8,0},{9,1},... | collective-permute-start | bytes 589832 | tf_op jit(solution)/shard_map/ppermute | solution.py:416
  81.1 6.3 %collective-permute-start.23 = (bf16[32,2176]{1,0:T(8,128)(2,1)S(1)}, bf16[32,2176]{1,0:T(8,128)(2,1)S(1)}, u32[]{:S(2)}, u32[]{:S(2)}) collective-permute-start(bf16[32,2176]{1,0:T(8,128)(2,1)S(1)} %get-tuple-element.191), channel_id=1, source_target_pairs={{0,2},{2,0},{4,6},{6,4},{8,10},{10,8},{12,14},{14,12},{16,18},{18,... | collective-permute-start | bytes 417800 | tf_op jit(solution)/shard_map/ppermute | solution.py:492
  81.5 6.4 %collective-permute-start.24 = (bf16[32,2176]{1,0:T(8,128)(2,1)S(1)}, bf16[32,2176]{1,0:T(8,128)(2,1)S(1)}, u32[]{:S(2)}, u32[]{:S(2)}) collective-permute-start(bf16[32,2176]{1,0:T(8,128)(2,1)S(1)} %get-tuple-element.192), channel_id=1, source_target_pairs={{0,4},{2,6},{4,0},{6,2},{8,12},{10,14},{12,8},{14,10},{16,20},{18,... | collective-permute-start | bytes 417800 | tf_op jit(solution)/shard_map/ppermute | solution.py:492
  82.8 5.8 %collective-permute-start.25 = (bf16[32,2176]{1,0:T(8,128)(2,1)S(1)}, bf16[32,2176]{1,0:T(8,128)(2,1)S(1)}, u32[]{:S(2)}, u32[]{:S(2)}) collective-permute-start(bf16[32,2176]{1,0:T(8,128)(2,1)S(1)} %get-tuple-element.193), channel_id=1, source_target_pairs={{0,6},{2,4},{4,2},{6,0},{8,14},{10,12},{12,10},{14,8},{16,22},{18,... | collective-permute-start | bytes 417800 | tf_op jit(solution)/shard_map/ppermute | solution.py:492
  83.8 13.9 %collective-permute-start.30 = (bf16[64,256]{1,0:T(8,128)(2,1)S(1)}, bf16[64,256]{1,0:T(8,128)(2,1)S(1)}, u32[]{:S(2)}, u32[]{:S(2)}) collective-permute-start(bf16[64,256]{1,0:T(8,128)(2,1)S(1)} %get-tuple-element.206), channel_id=1, source_target_pairs={{0,4},{1,3},{2,6},{3,1},{4,0},{5,7},{6,2},{7,5},{8,12},{9,11},{10,... | collective-permute-start | bytes 98312 | tf_op jit(solution)/shard_map/ppermute | solution.py:416
  85.4 12.3 %collective-permute-start.28 = (bf16[64,1024]{1,0:T(8,128)(2,1)S(1)}, bf16[64,1024]{1,0:T(8,128)(2,1)S(1)}, u32[]{:S(2)}, u32[]{:S(2)}) collective-permute-start(bf16[64,1024]{1,0:T(8,128)(2,1)S(1)} %get-tuple-element.202), channel_id=1, source_target_pairs={{0,16},{1,17},{2,18},{3,19},{4,20},{5,21},{6,22},{7,23},{8,24},{9,... | collective-permute-start | bytes 393224 | tf_op jit(solution)/shard_map/ppermute | solution.py:416
  87.5 10.3 %collective-permute-start.29 = (bf16[64,768]{1,0:T(8,128)(2,1)S(1)}, bf16[64,768]{1,0:T(8,128)(2,1)S(1)}, u32[]{:S(2)}, u32[]{:S(2)}) collective-permute-start(bf16[64,768]{1,0:T(8,128)(2,1)S(1)} %get-tuple-element.204), channel_id=1, source_target_pairs={{0,16},{1,17},{2,18},{3,19},{4,20},{5,21},{6,22},{7,23},{8,24},{9,... | collective-permute-start | bytes 294920 | tf_op jit(solution)/shard_map/ppermute | solution.py:416
  88.6 9.1 %collective-permute-start.27 = (f32[1,128]{1,0:T(1,128)S(1)}, f32[1,128]{1,0:T(1,128)S(1)}, u32[]{:S(2)}, u32[]{:S(2)}) collective-permute-start(f32[1,128]{1,0:T(1,128)S(1)} %get-tuple-element.200.refs_1_), channel_id=1, source_target_pairs={{0,1},{1,0},{2,3},{3,2},{4,5},{5,4},{6,7},{7,6},{8,9},{9,8},{10,11... | collective-permute-start | bytes 1544 | tf_op jit(solution)/shard_map/ppermute | solution.py:656
